TPU v7x, 512 devices: a whole 4x4x16 slice. The times are simulated.
512 devices in a mesh: section: 16 (over y, z_hi), tp: 32 (over z_lo, x, core).
Axes of the slice: x: 4, y: 4, z: 16 (z_hi: 4, z_lo: 4; z = z_hi * 4 + z_lo), core: 2. Of those that a mesh axis runs over, the one named last changes fastest.
Arguments:
- grad_in: bfloat16 [16, 128, 4096], P('section', None, 'tp'), may hold values from -6 to 6
- fresh_grads: bfloat16 [1, 128, 4096], P(None, None, 'tp'), may hold values from -6 to 6
- acc_in: float32 [16, 128, 4096], P('section', None, 'tp'), may hold values from -3 to 3
- queries: bfloat16 [16, 2, 128, 4096], P('section', None, None, 'tp'), may hold values from -4.625 to 4.625
- keys: bfloat16 [16, 2, 128, 4096], P('section', None, None, 'tp'), may hold values from -4.625 to 4.625
- values: bfloat16 [16, 2, 128, 4096], P('section', None, None, 'tp'), may hold values from -12 to 12
- query_weight: bfloat16 [16, 4096, 4096], P('section', 'tp'), may hold values from -0.09375 to 0.09375
- key_weight: bfloat16 [16, 4096, 4096], P('section', None, 'tp'), may hold values from -0.1875 to 0.1875
- value_weight: bfloat16 [16, 4096, 4096], P('section', None, 'tp'), may hold values from -0.1875 to 0.1875
- out_weight: bfloat16 [16, 4096, 4096], P('section', 'tp'), may hold values from -0.09375 to 0.09375
Outputs:
- grad_out: bfloat16 [16, 128, 4096], P('section', None, 'tp')
- acc_out: float32 [16, 128, 4096], P('section', None, 'tp')
All inputs are finite; a program needn't handle non-finite values.
Results may differ from a plain program's by a relative error of at most 0.025.
Values may be sent and summed in bfloat16 or wider, within the bound.
No kernel may reach another device: no remote copies, remote signals or barrier semaphores. Data moves between devices by JAX's collectives and lax.ppermute only.
A program may use at most 64 MiB of HBM per device.

v0:
```python
import jax
import jax.numpy as jnp
from jax import lax
from jax.sharding import PartitionSpec as P

HEAD_DIM = 64
SEQS = 1


def passed_along(value, axis, steps):
    count = lax.axis_size(axis)
    leading, last = (max(0, -steps), min(count, count - steps))
    return lax.ppermute(value, axis, [(source, source + steps) for source in range(leading, last)])


def cut_along(x, dim, length):
    lengths = x.shape
    parts = x.reshape(*lengths[:dim], length, lengths[dim] // length, *lengths[dim + 1 :])
    return jnp.moveaxis(parts, dim, 0)


def sum_at_owner(x, axis, dim):
    parts = cut_along(x, dim, lax.axis_size(axis))
    arrived = lax.all_to_all(parts, axis, split_axis=0, concat_axis=0, tiled=True)
    return arrived.astype(jnp.float32).sum(axis=0)


def from_everyone(x, axis):
    copies = jnp.broadcast_to(x, (lax.axis_size(axis), *x.shape))
    return lax.all_to_all(copies, axis, split_axis=0, concat_axis=0, tiled=True)


def in_order(parts, dim):
    parts = jnp.moveaxis(parts, 0, dim)
    lengths = parts.shape
    return parts.reshape(*lengths[:dim], lengths[dim] * lengths[dim + 1], *lengths[dim + 2 :])


def gather_directly(x, axis, dim):
    parts = from_everyone(x, axis)
    return in_order(parts, dim)


def transpose_product(left, right):
    return lax.dot_general(
        left, right, (((1,), (1,)), ((), ())), preferred_element_type=jnp.float32
    )


def attention_grads(upstream, queries, keys, values):
    token_rows, columns = queries.shape
    enc_rows = keys.shape[0]
    heads = columns // HEAD_DIM
    query_heads = queries.reshape(SEQS, token_rows // SEQS, heads, HEAD_DIM)
    key_heads = keys.reshape(SEQS, enc_rows // SEQS, heads, HEAD_DIM)
    value_heads = values.reshape(SEQS, enc_rows // SEQS, heads, HEAD_DIM)
    upstream_heads = upstream.reshape(SEQS, token_rows // SEQS, heads, HEAD_DIM)
    scores = jnp.einsum(
        "bqhd,bkhd->bhqk", query_heads, key_heads, preferred_element_type=jnp.float32
    )
    attention = jax.nn.softmax(scores, axis=-1)
    weights = attention.astype(jnp.bfloat16)
    output = jnp.einsum("bhqk,bkhd->bqhd", weights, value_heads, preferred_element_type=jnp.float32)
    delta = jnp.sum(upstream_heads.astype(jnp.float32) * output, axis=-1)
    prob_grad = jnp.einsum(
        "bqhd,bkhd->bhqk", upstream_heads, value_heads, preferred_element_type=jnp.float32
    )
    score_grad = (attention * (prob_grad - jnp.transpose(delta, (0, 2, 1))[..., None])).astype(
        jnp.bfloat16
    )
    query_grad = jnp.einsum(
        "bhqk,bkhd->bqhd", score_grad, key_heads, preferred_element_type=jnp.float32
    )
    key_grad = jnp.einsum(
        "bhqk,bqhd->bkhd", score_grad, query_heads, preferred_element_type=jnp.float32
    )
    value_grad = jnp.einsum(
        "bhqk,bqhd->bkhd", weights, upstream_heads, preferred_element_type=jnp.float32
    )
    return (
        query_grad.reshape(token_rows, columns).astype(jnp.bfloat16),
        key_grad.reshape(enc_rows, columns).astype(jnp.bfloat16),
        value_grad.reshape(enc_rows, columns).astype(jnp.bfloat16),
    )


def body(
    grad_in,
    fresh_grads,
    acc_in,
    queries,
    keys,
    values,
    query_weight,
    key_weight,
    value_weight,
    out_weight,
):
    grad_slice = grad_in[0]
    carried = acc_in[0]
    w_query = query_weight[0]
    w_key = key_weight[0]
    w_value = value_weight[0]
    w_out = out_weight[0]
    slot_count = queries.shape[1]
    is_top = lax.axis_index("section") == lax.axis_size("section") - 1
    passed = grad_slice
    for slot in range(slot_count):
        upstream = transpose_product(gather_directly(grad_slice, "tp", 1), w_out)
        query_grad, key_grad, value_grad = attention_grads(
            upstream.astype(jnp.bfloat16), queries[0, slot], keys[0, slot], values[0, slot]
        )
        branch = transpose_product(gather_directly(query_grad, "tp", 1), w_query)
        passed = (grad_slice.astype(jnp.float32) + branch).astype(jnp.bfloat16)
        passes_on = slot + 1 < slot_count
        summed = carried
        term = transpose_product(key_grad, w_key) + transpose_product(value_grad, w_value)
        summed = summed + sum_at_owner(term.astype(jnp.bfloat16), "tp", 1)
        if passes_on:
            summed = passed_along(summed.astype(jnp.bfloat16), "section", -1).astype(summed.dtype)
        carried = summed
        if passes_on:
            received = passed_along(passed, "section", -1)
            new_slice = jnp.where(is_top, fresh_grads[slot], received)
            grad_slice = new_slice
            pass
    return (passed[None], carried[None])


def solution(mesh):
    in_specs = (
        P("section", None, "tp"),
        P(None, None, "tp"),
        P("section", None, "tp"),
        P("section", None, None, "tp"),
        P("section", None, None, "tp"),
        P("section", None, None, "tp"),
        P("section", "tp", None),
        P("section", None, "tp"),
        P("section", None, "tp"),
        P("section", "tp", None),
    )
    out_specs = (P("section", None, "tp"), P("section", None, "tp"))
    return jax.shard_map(body, mesh=mesh, in_specs=in_specs, out_specs=out_specs, check_vma=False)
```

profile of v0, /device:TPU:25, one launch (start us, length us, event | category | flops | bytes accessed | tf_op | source)
XLA Modules:
  0.0 220.9 jit_solution(6960012011799568031)
XLA Ops:
  0.6 0.0 copy-start
  0.7 1.0 copy.50
  1.7 1.2 broadcast_in_dim.24
  2.9 9.2 %all-to-all-start = ((bf16[32,128,128]{1,2,0:T(8,128)(2,1)}), bf16[32,128,128]{1,2,0:T(8,128)(2,1)S(1)}, u32[]{:S(2)}, u32[]{:S(2)}) async-start(bf16[32,128,128]{1,2,0:T(8,128)(2,1)} %broadcast_in_dim.24), calls=%async_computation | async-start | bytes 2097152 | tf_op jit(solution)/shard_map/all_to_all | solution.py:30
  12.1 0.1 copy.48
  12.3 0.1 copy.49
  12.4 0.1 copy.51
  12.5 0.0 copy-start.13
  12.6 0.3 fusion.45
  12.8 25.9 %all-to-all-done = bf16[32,128,128]{1,2,0:T(8,128)(2,1)S(1)} async-done(((bf16[32,128,128]{1,2,0:T(8,128)(2,1)}), bf16[32,128,128]{1,2,0:T(8,128)(2,1)S(1)}, u32[]{:S(2)}, u32[]{:S(2)}) %all-to-all-start) | async-done | bytes 1048608 | tf_op jit(solution)/shard_map/all_to_all | solution.py:30
  38.7 0.4 convolution_convert_fusion.3
  39.1 0.0 copy-start.10
  39.1 0.0 copy-start.2
  39.2 0.0 copy-start.5
  39.2 0.2 fusion.17
  39.3 0.4 copy-done.10
  39.8 1.0 fusion.12
  40.7 0.1 convolution_convert_fusion.2
  40.9 0.2 broadcast_in_dim.25
  41.1 0.0 copy-start.12
  41.1 31.6 %all_to_all.30 = bf16[32,128,128]{1,2,0:T(8,128)(2,1)S(1)} all-to-all(bf16[32,128,128]{1,2,0:T(8,128)(2,1)S(1)} %broadcast_in_dim.25), channel_id=1, replica_groups=mesh['section'=16,'tp'=32] {'tp'}, dimensions={0} | all-to-all | bytes 2097152 | tf_op jit(solution)/shard_map/all_to_all | solution.py:30
  72.7 0.5 fusion.16
  73.2 9.9 %collective-permute-start = (bf16[128,128]{1,0:T(8,128)(2,1)S(1)}, bf16[128,128]{1,0:T(8,128)(2,1)}, u32[]{:S(2)}, u32[]{:S(2)}) collective-permute-start(bf16[128,128]{1,0:T(8,128)(2,1)S(1)} %fusion.16), channel_id=1, source_target_pairs={{32,0},{64,32},{96,64},{128,96},{160,128},{192,160},{224,192},{256... | collective-permute-start | bytes 98312 | tf_op jit(solution)/shard_map/ppermute | solution.py:13
  83.2 1.0 collective-permute-done
  84.2 0.8 bitcast_select_fusion
  84.9 0.1 copy.57
  85.0 1.2 broadcast_in_dim.26
  86.3 6.9 %all-to-all-start.2 = ((bf16[32,128,128]{1,2,0:T(8,128)(2,1)}), bf16[32,128,128]{1,2,0:T(8,128)(2,1)}, u32[]{:S(2)}, u32[]{:S(2)}) async-start(bf16[32,128,128]{1,2,0:T(8,128)(2,1)} %broadcast_in_dim.26), calls=%async_computation.2 | async-start | bytes 2097152 | tf_op jit(solution)/shard_map/all_to_all | solution.py:30
  93.2 0.1 convolution_convert_fusion.7
  93.3 0.0 copy-done.11
  93.4 0.1 convolution_convert_fusion.6
  93.5 0.0 copy-done
  93.5 0.5 fusion.23
  94.0 0.4 copy-done.3
  94.4 0.5 fusion.5
  94.9 1.3 copy.83
  96.2 23.8 %all-to-all-done.2 = bf16[32,128,128]{1,2,0:T(8,128)(2,1)} async-done(((bf16[32,128,128]{1,2,0:T(8,128)(2,1)}), bf16[32,128,128]{1,2,0:T(8,128)(2,1)}, u32[]{:S(2)}, u32[]{:S(2)}) %all-to-all-start.2) | async-done | bytes 1048608 | tf_op jit(solution)/shard_map/all_to_all | solution.py:30
  119.9 5.2 %all-to-all-start.4 = ((bf16[32,128,128]{2,1,0:T(8,128)(2,1)}), bf16[32,128,128]{2,1,0:T(8,128)(2,1)}, u32[]{:S(2)}, u32[]{:S(2)}) async-start(bf16[32,128,128]{2,1,0:T(8,128)(2,1)} %bitcast.171), calls=%async_computation.4 | async-start | bytes 2097152 | tf_op jit(solution)/shard_map/all_to_all | solution.py:24
  125.1 0.1 copy.55
  125.2 0.1 copy.56
  125.4 0.1 copy.58
  125.5 0.3 fusion.46
  125.8 1.6 convolution_convert_fusion.1
  127.4 0.2 fusion.18
  127.6 0.2 fusion.13
  127.8 0.1 convolution_convert_fusion
  128.0 23.8 %all-to-all-done.4 = bf16[32,128,128]{2,1,0:T(8,128)(2,1)} async-done(((bf16[32,128,128]{2,1,0:T(8,128)(2,1)}), bf16[32,128,128]{2,1,0:T(8,128)(2,1)}, u32[]{:S(2)}, u32[]{:S(2)}) %all-to-all-start.4) | async-done | bytes 1048608 | tf_op jit(solution)/shard_map/all_to_all | solution.py:24
  151.8 1.2 broadcast_in_dim.27
  153.0 5.2 %all-to-all-start.3 = ((bf16[32,128,128]{1,2,0:T(8,128)(2,1)}), bf16[32,128,128]{1,2,0:T(8,128)(2,1)S(1)}, u32[]{:S(2)}, u32[]{:S(2)}) async-start(bf16[32,128,128]{1,2,0:T(8,128)(2,1)} %broadcast_in_dim.27), calls=%async_computation.3 | async-start | bytes 2097152 | tf_op jit(solution)/shard_map/all_to_all | solution.py:30
  158.2 0.0 copy-start.4
  158.2 0.1 convolution_convert_fusion.5
  158.4 0.2 convolution_convert_fusion.4
  158.5 0.5 fusion.21
  159.0 0.4 copy-done.4
  159.5 0.5 fusion.4
  159.9 1.3 copy.82
  161.2 23.6 %all-to-all-done.3 = bf16[32,128,128]{1,2,0:T(8,128)(2,1)S(1)} async-done(((bf16[32,128,128]{1,2,0:T(8,128)(2,1)}), bf16[32,128,128]{1,2,0:T(8,128)(2,1)S(1)}, u32[]{:S(2)}, u32[]{:S(2)}) %all-to-all-start.3) | async-done | bytes 1048608 | tf_op jit(solution)/shard_map/all_to_all | solution.py:30
  184.8 5.3 %all-to-all-start.5 = ((bf16[32,128,128]{2,1,0:T(8,128)(2,1)}), bf16[32,128,128]{2,1,0:T(8,128)(2,1)}, u32[]{:S(2)}, u32[]{:S(2)}) async-start(bf16[32,128,128]{2,1,0:T(8,128)(2,1)} %bitcast.173), calls=%async_computation.5 | async-start | bytes 2097152 | tf_op jit(solution)/shard_map/all_to_all | solution.py:24
  190.1 1.4 convert_reduce_fusion.1
  191.5 8.2 %collective-permute-start.1 = (bf16[128,128]{1,0:T(8,128)(2,1)S(1)}, bf16[128,128]{1,0:T(8,128)(2,1)S(1)}, u32[]{:S(2)}, u32[]{:S(2)}) collective-permute-start(bf16[128,128]{1,0:T(8,128)(2,1)S(1)} %fusion.30), channel_id=1, source_target_pairs={{32,0},{64,32},{96,64},{128,96},{160,128},{192,160},{224,192},{256... | collective-permute-start | bytes 98312 | tf_op jit(solution)/shard_map/ppermute | solution.py:13
  199.7 1.1 fusion.33
  200.8 18.1 %all-to-all-done.5 = bf16[32,128,128]{2,1,0:T(8,128)(2,1)} async-done(((bf16[32,128,128]{2,1,0:T(8,128)(2,1)}), bf16[32,128,128]{2,1,0:T(8,128)(2,1)}, u32[]{:S(2)}, u32[]{:S(2)}) %all-to-all-start.5) | async-done | bytes 1048608 | tf_op jit(solution)/shard_map/all_to_all | solution.py:24
  218.8 1.4 convert_reduce_fusion
  220.2 0.6 add_bitcast_fusion
  (21 shorter events, 0.1 us)
Async XLA Ops:
  0.6 92.9 %copy-start = (bf16[1,4096,128]{2,1,0:T(8,128)(2,1)S(1)}, bf16[1,4096,128]{2,1,0:T(8,128)(2,1)}, u32[]{:S(2)}) copy-start(bf16[1,4096,128]{2,1,0:T(8,128)(2,1)} %param.17) | copy-start | bytes 3145732
  0.6 11.5 %copy-start.6 = (bf16[1,2,128,128]{3,2,1,0:T(8,128)(2,1)S(1)}, bf16[1,2,128,128]{3,2,1,0:T(8,128)(2,1)}, u32[]{:S(2)}) copy-start(bf16[1,2,128,128]{3,2,1,0:T(8,128)(2,1)} %param.13) | copy-start | bytes 196612
  0.7 11.6 %copy-start.7 = (bf16[1,2,128,128]{3,2,1,0:T(8,128)(2,1)S(1)}, bf16[1,2,128,128]{3,2,1,0:T(8,128)(2,1)}, u32[]{:S(2)}) copy-start(bf16[1,2,128,128]{3,2,1,0:T(8,128)(2,1)} %param.14) | copy-start | bytes 196612
  0.7 11.7 %copy-start.8 = (bf16[1,2,128,128]{3,2,1,0:T(8,128)(2,1)S(1)}, bf16[1,2,128,128]{3,2,1,0:T(8,128)(2,1)}, u32[]{:S(2)}) copy-start(bf16[1,2,128,128]{3,2,1,0:T(8,128)(2,1)} %param.15) | copy-start | bytes 196612
  0.7 38.0 %copy-start.1 = (bf16[1,128,4096]{2,1,0:T(8,128)(2,1)S(1)}, bf16[1,128,4096]{2,1,0:T(8,128)(2,1)}, u32[]{:S(2)}) copy-start(bf16[1,128,4096]{2,1,0:T(8,128)(2,1)} %param.19) | copy-start | bytes 3145732
  2.9 35.8 %all-to-all-start = ((bf16[32,128,128]{1,2,0:T(8,128)(2,1)}), bf16[32,128,128]{1,2,0:T(8,128)(2,1)S(1)}, u32[]{:S(2)}, u32[]{:S(2)}) async-start(bf16[32,128,128]{1,2,0:T(8,128)(2,1)} %broadcast_in_dim.24), calls=%async_computation | async-start | bytes 2097152 | tf_op jit(solution)/shard_map/all_to_all | solution.py:30
  12.5 26.8 %copy-start.13 = (bf16[1,1,128,128]{2,3,1,0:T(8,128)(2,1)}, bf16[1,1,128,128]{2,3,1,0:T(8,128)(2,1)S(1)}, u32[]{:S(2)}) copy-start(bf16[1,1,128,128]{2,3,1,0:T(8,128)(2,1)S(1)} %copy.51) | copy-start | bytes 98308
  39.1 0.6 copy-start.10
  39.1 33.6 %copy-start.2 = (bf16[1,128,4096]{2,1,0:T(8,128)(2,1)S(1)}, bf16[1,128,4096]{2,1,0:T(8,128)(2,1)}, u32[]{:S(2)}) copy-start(bf16[1,128,4096]{2,1,0:T(8,128)(2,1)} %param.16) | copy-start | bytes 3145732
  39.2 33.6 %copy-start.5 = (bf16[1,128,128]{2,1,0:T(8,128)(2,1)S(1)}, bf16[1,128,128]{2,1,0:T(8,128)(2,1)}, u32[]{:S(2)}) copy-start(bf16[1,128,128]{2,1,0:T(8,128)(2,1)} %param.10) | copy-start | bytes 98308
  41.1 43.1 %copy-start.12 = (bf16[1,128,128]{2,1,0:T(8,128)(2,1)S(1)}, bf16[1,128,128]{2,1,0:T(8,128)(2,1)}, u32[]{:S(2)}) copy-start(bf16[1,128,128]{2,1,0:T(8,128)(2,1)} %param.11) | copy-start | bytes 98308
  73.2 10.9 %collective-permute-start = (bf16[128,128]{1,0:T(8,128)(2,1)S(1)}, bf16[128,128]{1,0:T(8,128)(2,1)}, u32[]{:S(2)}, u32[]{:S(2)}) collective-permute-start(bf16[128,128]{1,0:T(8,128)(2,1)S(1)} %fusion.16), channel_id=1, source_target_pairs={{32,0},{64,32},{96,64},{128,96},{160,128},{192,160},{224,192},{256... | collective-permute-start | bytes 98312 | tf_op jit(solution)/shard_map/ppermute | solution.py:13
  86.3 7.1 %copy-start.11 = (bf16[128,128]{0,1:T(8,128)(2,1)S(1)}, bf16[128,128]{0,1:T(8,128)(2,1)}, u32[]{:S(2)}) copy-start(bf16[128,128]{0,1:T(8,128)(2,1)} %copy-done.10) | copy-start | bytes 98308
  86.3 33.7 %all-to-all-start.2 = ((bf16[32,128,128]{1,2,0:T(8,128)(2,1)}), bf16[32,128,128]{1,2,0:T(8,128)(2,1)}, u32[]{:S(2)}, u32[]{:S(2)}) async-start(bf16[32,128,128]{1,2,0:T(8,128)(2,1)} %broadcast_in_dim.26), calls=%async_computation.2 | async-start | bytes 2097152 | tf_op jit(solution)/shard_map/all_to_all | solution.py:30
  93.2 1.2 copy-start.3
  119.9 31.8 %all-to-all-start.4 = ((bf16[32,128,128]{2,1,0:T(8,128)(2,1)}), bf16[32,128,128]{2,1,0:T(8,128)(2,1)}, u32[]{:S(2)}, u32[]{:S(2)}) async-start(bf16[32,128,128]{2,1,0:T(8,128)(2,1)} %bitcast.171), calls=%async_computation.4 | async-start | bytes 2097152 | tf_op jit(solution)/shard_map/all_to_all | solution.py:24
  153.0 31.8 %all-to-all-start.3 = ((bf16[32,128,128]{1,2,0:T(8,128)(2,1)}), bf16[32,128,128]{1,2,0:T(8,128)(2,1)S(1)}, u32[]{:S(2)}, u32[]{:S(2)}) async-start(bf16[32,128,128]{1,2,0:T(8,128)(2,1)} %broadcast_in_dim.27), calls=%async_computation.3 | async-start | bytes 2097152 | tf_op jit(solution)/shard_map/all_to_all | solution.py:30
  158.2 1.2 copy-start.4
  161.2 30.2 %copy-start.9 = (f32[1,128,128]{2,1,0:T(8,128)S(1)}, f32[1,128,128]{2,1,0:T(8,128)}, u32[]{:S(2)}) copy-start(f32[1,128,128]{2,1,0:T(8,128)} %param.12) | copy-start | bytes 196612
  184.8 34.0 %all-to-all-start.5 = ((bf16[32,128,128]{2,1,0:T(8,128)(2,1)}), bf16[32,128,128]{2,1,0:T(8,128)(2,1)}, u32[]{:S(2)}, u32[]{:S(2)}) async-start(bf16[32,128,128]{2,1,0:T(8,128)(2,1)} %bitcast.173), calls=%async_computation.5 | async-start | bytes 2097152 | tf_op jit(solution)/shard_map/all_to_all | solution.py:24
  191.5 28.7 %collective-permute-start.1 = (bf16[128,128]{1,0:T(8,128)(2,1)S(1)}, bf16[128,128]{1,0:T(8,128)(2,1)S(1)}, u32[]{:S(2)}, u32[]{:S(2)}) collective-permute-start(bf16[128,128]{1,0:T(8,128)(2,1)S(1)} %fusion.30), channel_id=1, source_target_pairs={{32,0},{64,32},{96,64},{128,96},{160,128},{192,160},{224,192},{256... | collective-permute-start | bytes 98312 | tf_op jit(solution)/shard_map/ppermute | solution.py:13
where the time goes:
time: 222 us; the launch traced here: 221 us
  waiting for transfers between devices  116 us (52%)
  starting transfers between devices  49.9 us (22%)
  blocking collectives  31.6 us (14%)
  local copies, waits for them, and re-layouts  9.69 us (4%)
  matrix products  8.4 us (4%)
  other arithmetic  4.18 us (2%)
    all_to_all x3, waiting for transfers between devices, from_everyone(): return lax.all_to_all(copies, axis, split_axis=0, concat_axis=0, tiled=True)  73.2 us
    all_to_all x2, waiting for transfers between devices, sum_at_owner(): lax.all_to_all(parts, axis, split_axis=0, concat_axis=0, tiled=True)  41.9 us
    all_to_all x1, blocking collectives, from_everyone(): return lax.all_to_all(copies, axis, split_axis=0, concat_axis=0, tiled=True)  31.6 us
    all_to_all x3, starting transfers between devices, from_everyone(): return lax.all_to_all(copies, axis, split_axis=0, concat_axis=0, tiled=True)  21.3 us
    ppermute x2, starting transfers between devices, passed_along(): lax.ppermute(value, axis, [(source, source + steps) for source in range(l...  18.1 us
    all_to_all x2, starting transfers between devices, sum_at_owner(): lax.all_to_all(parts, axis, split_axis=0, concat_axis=0, tiled=True)  10.5 us
    dot_general x8, matrix products, transpose_product(): lax.dot_general(left, right, (((1,), (1,)), ((), ())), preferred_element_...  5.49 us
  transfers between devices with their start and end apart: 7, of which 6 were waited for; matrix products, arithmetic and copies ran while one was open for 6% of the time, Pallas kernels for 0%

commit v1 on v0

v1 whole, which is shorter than its diff:
```python
import jax
import jax.numpy as jnp
from jax import lax
from jax.sharding import PartitionSpec as P

HEAD_DIM = 64
CORES = 2


def passed_along(value, axis, steps):
    count = lax.axis_size(axis)
    leading, last = (max(0, -steps), min(count, count - steps))
    return lax.ppermute(value, axis, [(source, source + steps) for source in range(leading, last)])


def chip_groups():
    chips = lax.axis_size("tp") // CORES
    return [[chip * CORES + core for chip in range(chips)] for core in range(CORES)]


def core_groups():
    chips = lax.axis_size("tp") // CORES
    return [[chip * CORES + core for core in range(CORES)] for chip in range(chips)]


def chip_exchange(parts):
    return lax.all_to_all(
        parts, "tp", split_axis=0, concat_axis=0, tiled=True, axis_index_groups=chip_groups()
    )


def chip_gather(x):
    chips = lax.axis_size("tp") // CORES
    return chip_exchange(jnp.broadcast_to(x, (chips, *x.shape)))


def sibling_swap(x):
    count = lax.axis_size("tp")
    return lax.ppermute(x, "tp", [(source, source ^ 1) for source in range(count)])


def from_sibling(x):
    both = lax.all_gather(x, "tp", axis=0, tiled=False, axis_index_groups=core_groups())
    return jnp.where(lax.axis_index("tp") % CORES == 0, both[1], both[0])


def of_core(blocks, dim, core):
    return lax.dynamic_index_in_dim(blocks, core, dim, keepdims=False)


def product(gathered, weight):
    return lax.dot_general(
        gathered, weight, (((0, 2), (1, 2)), ((), ())), preferred_element_type=jnp.float32
    )


def pair_product(gathered, own, other):
    mine = product(gathered, own)
    theirs = product(gathered, other)
    return mine + from_sibling(theirs)


def attention_grads(upstream, queries, keys, values):
    rows, columns = queries.shape
    heads = columns // HEAD_DIM
    query_grads, key_grads, value_grads = [], [], []

    def dot(a, b, da, db):
        return lax.dot_general(a, b, (((da,), (db,)), ((), ())), preferred_element_type=jnp.float32)

    for head in range(heads):
        cols = slice(head * HEAD_DIM, (head + 1) * HEAD_DIM)
        q, k, v, u = queries[:, cols], keys[:, cols], values[:, cols], upstream[:, cols]
        attention = jax.nn.softmax(dot(q, k, 1, 1), axis=-1)
        weights = attention.astype(jnp.bfloat16)
        output = dot(weights, v, 1, 0)
        delta = jnp.sum(u.astype(jnp.float32) * output, axis=-1, keepdims=True)
        prob_grad = dot(u, v, 1, 1)
        score_grad = (attention * (prob_grad - delta)).astype(jnp.bfloat16)
        query_grads.append(dot(score_grad, k, 1, 0))
        key_grads.append(dot(score_grad, q, 0, 0))
        value_grads.append(dot(weights, u, 0, 0))
    return tuple(
        jnp.concatenate(parts, axis=1).astype(jnp.bfloat16)
        for parts in (query_grads, key_grads, value_grads)
    )


def body(
    grad_in,
    fresh_grads,
    acc_in,
    queries,
    keys,
    values,
    query_weight,
    key_weight,
    value_weight,
    out_weight,
):
    chips = lax.axis_size("tp") // CORES
    core = lax.axis_index("tp") % CORES
    is_top = lax.axis_index("section") == lax.axis_size("section") - 1
    slot_count = queries.shape[1]
    width = queries.shape[3]

    grad_slice = grad_in[0]
    gathered = chip_gather(grad_slice)

    def by_features_last(weight):
        blocks = weight[0].reshape(width, chips, CORES, width)
        own = of_core(blocks, 2, core)
        return own, sibling_swap(of_core(blocks, 2, 1 - core))

    def by_features_first(weight):
        blocks = weight[0].reshape(chips, CORES, width, width)
        own = of_core(blocks, 1, core)
        return own, sibling_swap(of_core(blocks, 1, 1 - core))

    w_out = by_features_last(out_weight)
    w_query = by_features_last(query_weight)
    w_key = by_features_first(key_weight)
    w_value = by_features_first(value_weight)
    w_term = jnp.concatenate([w_key[0], w_value[0], w_key[1], w_value[1]], axis=2)

    def term_parts(key_grad, value_grad):
        own = jnp.concatenate([key_grad, value_grad], axis=1)
        both = jnp.concatenate([own, from_sibling(own)], axis=1)
        parts = jnp.einsum("cfk,rk->crf", w_term, both, preferred_element_type=jnp.float32)
        return parts.astype(jnp.bfloat16)

    carried = acc_in[0]
    passed = grad_slice
    for slot in range(slot_count):
        last = slot + 1 == slot_count
        upstream = pair_product(gathered, *w_out).astype(jnp.bfloat16)
        query_grad, key_grad, value_grad = attention_grads(
            upstream, queries[0, slot], keys[0, slot], values[0, slot]
        )
        if last:
            terms = term_parts(key_grad, value_grad)
            queries_out = jnp.broadcast_to(query_grad, terms.shape)
            arrived = chip_exchange(jnp.stack([queries_out, terms], axis=1))
            all_queries, arrived_terms = arrived[:, 0], arrived[:, 1]
        else:
            all_queries = chip_gather(query_grad)
        branch = pair_product(all_queries, *w_query)
        passed = (grad_slice.astype(jnp.float32) + branch).astype(jnp.bfloat16)
        if not last:
            received = passed_along(passed, "section", -1)
            arrived_terms = chip_exchange(term_parts(key_grad, value_grad))
        carried = carried + arrived_terms.astype(jnp.float32).sum(axis=0)
        if not last:
            carried = passed_along(carried.astype(jnp.bfloat16), "section", -1).astype(jnp.float32)
            grad_slice = jnp.where(is_top, fresh_grads[slot], received)
            gathered = chip_gather(grad_slice)
    return (passed[None], carried[None])


def solution(mesh):
    in_specs = (
        P("section", None, "tp"),
        P(None, None, "tp"),
        P("section", None, "tp"),
        P("section", None, None, "tp"),
        P("section", None, None, "tp"),
        P("section", None, None, "tp"),
        P("section", "tp", None),
        P("section", None, "tp"),
        P("section", None, "tp"),
        P("section", "tp", None),
    )
    out_specs = (P("section", None, "tp"), P("section", None, "tp"))
    return jax.shard_map(body, mesh=mesh, in_specs=in_specs, out_specs=out_specs, check_vma=False)
```

time: 222 us -> 147 us (0.66)
  waiting for transfers between devices: 116 us -> 30 us
  blocking collectives: 31.6 us -> 19.6 us
  starting transfers between devices: 49.9 us -> 60.7 us
  local copies, waits for them, and re-layouts: 9.69 us -> 17.6 us
  matrix products: 8.4 us -> 13.9 us
  other arithmetic: 4.18 us -> 1.29 us
    all_to_all x5, waiting for transfers between devices: 115 us -> 28.3 us  [chip_exchange(): lax.all_to_all(parts, 'tp', split_axis=0, concat_axis=0, tiled=True, axis...]
    all_to_all x1 -> x0, blocking collectives: 31.6 us -> none  [from_everyone(): return lax.all_to_all(copies, axis, split_axis=0, concat_axis=0, tiled=True)]
    all_gather x0 -> x6, blocking collectives: none -> 19.6 us  [from_sibling(): lax.all_gather(x, 'tp', axis=0, tiled=False, axis_index_groups=core_group...]
    ppermute x0 -> x4, starting transfers between devices: none -> 9.83 us  [sibling_swap(): lax.ppermute(x, 'tp', [(source, source ^ 1) for source in range(count)])]
    dot_general x18 -> x34, matrix products: 7.85 us -> 13.9 us  [the longest x24 4.92 us: dot(): lax.dot_general(a, b, (((da,), (db,)), ((), ())), preferred_element_type=...]
    dynamic_slice x0 -> x2, local copies, waits for them, and re-layouts: none -> 5.3 us  [of_core(): return lax.dynamic_index_in_dim(blocks, core, dim, keepdims=False)]
    another operation x0 -> x4, local copies, waits for them, and re-layouts: none -> 3.75 us  [the longest x2 2.56 us: by_features_last(): blocks = weight[0].reshape(width, chips, CORES, width)]
    reshape x2 -> x0, local copies, waits for them, and re-layouts: 2.6 us -> none  [cut_along(): x.reshape(*lengths[:dim], length, lengths[dim] // length, *lengths[dim +...]
  transfers between devices with their start and end apart: 7 -> 11, of which waited for: 6 -> 5; matrix products, arithmetic and copies ran while one was open for 6% -> 19% of each run, Pallas kernels for 0% -> 0%
where the time goes in v1:
time: 147 us; the launch traced here: 145 us
  starting transfers between devices  60.7 us (41%)
  waiting for transfers between devices  30 us (20%)
  blocking collectives  19.6 us (13%)
  local copies, waits for them, and re-layouts  17.6 us (12%)
  matrix products  13.9 us (9%)
    all_to_all x5, starting transfers between devices, chip_exchange(): lax.all_to_all(parts, 'tp', split_axis=0, concat_axis=0, tiled=True, axis...  32.3 us
    all_to_all x5, waiting for transfers between devices, chip_exchange(): lax.all_to_all(parts, 'tp', split_axis=0, concat_axis=0, tiled=True, axis...  28.3 us
    all_gather x6, blocking collectives, from_sibling(): lax.all_gather(x, 'tp', axis=0, tiled=False, axis_index_groups=core_group...  19.6 us
    ppermute x2, starting transfers between devices, passed_along(): lax.ppermute(value, axis, [(source, source + steps) for source in range(l...  18.6 us
    ppermute x4, starting transfers between devices, sibling_swap(): lax.ppermute(x, 'tp', [(source, source ^ 1) for source in range(count)])  9.83 us
    dynamic_slice x2, local copies, waits for them, and re-layouts, of_core(): return lax.dynamic_index_in_dim(blocks, core, dim, keepdims=False)  5.3 us
    dot_general x24, matrix products, dot(): lax.dot_general(a, b, (((da,), (db,)), ((), ())), preferred_element_type=...  4.92 us
    dot_general x2, matrix products, term_parts(): jnp.einsum('cfk,rk->crf', w_term, both, preferred_element_type=jnp.float32)  4.84 us
  transfers between devices with their start and end apart: 11, of which 5 were waited for; matrix products, arithmetic and copies ran while one was open for 19% of the time, Pallas kernels for 0%

profile of v1, /device:TPU:25, one launch (start us, length us, event | category | flops | bytes accessed | tf_op | source)
XLA Modules:
  0.0 144.5 jit_solution(3711624130152856424)
XLA Ops:
  0.6 1.7 %broadcast_in_dim.10 = bf16[16,128,128]{2,1,0:T(8,128)(2,1)} broadcast(bf16[128,128]{1,0:T(8,128)(2,1)} %bitcast.138), dimensions={1,2} | broadcast | bytes 557056 | tf_op jit(solution)/shard_map/broadcast_in_dim | solution.py:34
  2.4 8.2 %all-to-all-start = ((bf16[16,128,128]{2,1,0:T(8,128)(2,1)}), bf16[16,128,128]{2,1,0:T(8,128)(2,1)S(1)}, u32[]{:S(2)}, u32[]{:S(2)}) async-start(bf16[16,128,128]{2,1,0:T(8,128)(2,1)} %broadcast_in_dim.10), calls=%async_computation | async-start | bytes 1048576 | tf_op jit(solution)/shard_map/all_to_all | solution.py:27
  10.6 0.8 reshape_squeeze.12
  11.4 2.2 %constant_dynamic-slice_fusion.2 = (bf16[128,16,1,128]{3,2,1,0:T(2,128)(2,1)S(1)}, bf16[128,16,1,128]{3,2,1,0:T(2,128)(2,1)S(1)}) fusion(bf16[128,16,2,128]{3,2,1,0:T(2,128)(2,1)S(1)} %reshape_squeeze.12, s32[]{:T(128)S(6)} %select_n.95, s32[]{:T(128)S(6)} %select_n.93), kind=kLoop, calls=%fused_computation.154 | loop fusion | bytes 2097160 | tf_op jit(solution)/shard_map/jit(dynamic_index_in_dim)/dynamic_slice | solution.py:48
  13.6 0.3 copy.109
  14.0 2.9 %collective-permute-start = (bf16[128,16,128]{2,0,1:T(8,128)(2,1)S(1)}, bf16[128,16,128]{2,0,1:T(8,128)(2,1)S(1)}, u32[]{:S(2)}, u32[]{:S(2)}) collective-permute-start(bf16[128,16,128]{2,0,1:T(8,128)(2,1)S(1)} %bitcast.137), channel_id=1, source_target_pairs={{0,1},{1,0},{2,3},{3,2},{4,5},{5,4},{6,7},{7,6},{8,9},{9,8},{10,11... | collective-permute-start | bytes 1572872 | tf_op jit(solution)/shard_map/ppermute | solution.py:39
  16.9 0.2 fusion.81
  17.2 0.2 fusion.82
  17.5 0.9 collective-permute-done
  18.3 6.0 %all-to-all-done = bf16[16,128,128]{2,1,0:T(8,128)(2,1)S(1)} async-done(((bf16[16,128,128]{2,1,0:T(8,128)(2,1)}), bf16[16,128,128]{2,1,0:T(8,128)(2,1)S(1)}, u32[]{:S(2)}, u32[]{:S(2)}) %all-to-all-start) | async-done | bytes 524320 | tf_op jit(solution)/shard_map/all_to_all | solution.py:27
  24.3 0.3 convolution_bitcast_fusion.6
  24.6 4.2 %all-gather = f32[256,128]{0,1:T(8,128)S(1)} all-gather(f32[128,128]{0,1:T(8,128)S(1)} %convolution_bitcast_fusion.6), channel_id=2, replica_groups={{0,1},{2,3},{4,5},{6,7},{8,9},{10,11},{12,13},{14,15},{16,17},{18,19},{..., dimensions={0}, use_global_device_ids=true | all-gather | bytes 196608 | tf_op jit(solution)/shard_map/all_gather | solution.py:43
  28.8 0.4 fusion.27
  29.3 0.2 fusion.12
  29.6 0.3 fusion.13
  29.9 0.2 fusion.9
  30.1 0.2 convolution_convert_fusion.12
  30.4 0.2 convolution_convert_fusion.13
  30.7 0.9 broadcast_in_dim.11
  31.6 4.2 %all-to-all-start.1 = ((bf16[16,128,128]{2,1,0:T(8,128)(2,1)}), bf16[16,128,128]{2,1,0:T(8,128)(2,1)S(1)}, u32[]{:S(2)}, u32[]{:S(2)}) async-start(bf16[16,128,128]{2,1,0:T(8,128)(2,1)} %broadcast_in_dim.11), calls=%async_computation.1 | async-start | bytes 1048576 | tf_op jit(solution)/shard_map/all_to_all | solution.py:27
  35.8 1.8 %reshape_squeeze.13 = bf16[128,16,2,128]{3,2,1,0:T(2,128)(2,1)S(1)} reshape(bf16[1,128,4096]{2,1,0:T(8,128)(2,1)} %param.16) | data formatting | bytes 2097152 | tf_op jit(solution)/shard_map/reshape;squeeze | solution.py:111
  37.6 3.1 %constant_dynamic-slice_fusion = (bf16[128,16,1,128]{3,2,1,0:T(2,128)(2,1)S(1)}, bf16[128,16,1,128]{3,2,1,0:T(2,128)(2,1)}) fusion(bf16[128,16,2,128]{3,2,1,0:T(2,128)(2,1)S(1)} %reshape_squeeze.13, s32[]{:T(128)S(6)} %select_n.95, s32[]{:T(128)S(6)} %select_n.93), kind=kLoop, calls=%fused_computation.152 | loop fusion | bytes 2097160 | tf_op jit(solution)/shard_map/jit(dynamic_index_in_dim)/dynamic_slice | solution.py:48
  40.7 1.2 copy.108
  41.9 2.5 %collective-permute-start.1 = (bf16[128,16,128]{2,0,1:T(8,128)(2,1)}, bf16[128,16,128]{2,0,1:T(8,128)(2,1)S(1)}, u32[]{:S(2)}, u32[]{:S(2)}) collective-permute-start(bf16[128,16,128]{2,0,1:T(8,128)(2,1)} %bitcast.133), channel_id=1, source_target_pairs={{0,1},{1,0},{2,3},{3,2},{4,5},{5,4},{6,7},{7,6},{8,9},{9,8},{10,11... | collective-permute-start | bytes 1572872 | tf_op jit(solution)/shard_map/ppermute | solution.py:39
  44.4 1.1 dynamic-slice_bitcast_fusion.3
  45.5 1.9 %collective-permute-start.3 = (bf16[16,128,128]{2,1,0:T(8,128)(2,1)}, bf16[16,128,128]{2,1,0:T(8,128)(2,1)}, u32[]{:S(2)}, u32[]{:S(2)}) collective-permute-start(bf16[16,128,128]{2,1,0:T(8,128)(2,1)} %get-tuple-element.11), channel_id=1, source_target_pairs={{0,1},{1,0},{2,3},{3,2},{4,5},{5,4},{6,7},{7,6},{8,9},{9,8},{10,11... | collective-permute-start | bytes 1572872 | tf_op jit(solution)/shard_map/ppermute | solution.py:39
  47.4 1.1 dynamic-slice_bitcast_fusion.2
  48.5 2.5 %collective-permute-start.4 = (bf16[16,128,128]{2,1,0:T(8,128)(2,1)}, bf16[16,128,128]{2,1,0:T(8,128)(2,1)}, u32[]{:S(2)}, u32[]{:S(2)}) collective-permute-start(bf16[16,128,128]{2,1,0:T(8,128)(2,1)} %get-tuple-element.13), channel_id=1, source_target_pairs={{0,1},{1,0},{2,3},{3,2},{4,5},{5,4},{6,7},{7,6},{8,9},{9,8},{10,11... | collective-permute-start | bytes 1572872 | tf_op jit(solution)/shard_map/ppermute | solution.py:39
  51.2 0.3 fusion.83
  51.4 0.2 fusion.80
  51.6 0.3 convolution_bitcast_fusion.4
  51.9 2.1 %all-gather.1 = f32[256,128]{0,1:T(8,128)S(1)} all-gather(f32[128,128]{0,1:T(8,128)S(1)} %convolution_bitcast_fusion.4), channel_id=3, replica_groups={{0,1},{2,3},{4,5},{6,7},{8,9},{10,11},{12,13},{14,15},{16,17},{18,19},{..., dimensions={0}, use_global_device_ids=true | all-gather | bytes 196608 | tf_op jit(solution)/shard_map/all_gather | solution.py:43
  54.0 0.4 fusion.25
  54.4 9.9 %collective-permute-start.2 = (bf16[128,128]{0,1:T(8,128)(2,1)S(1)}, bf16[128,128]{0,1:T(8,128)(2,1)S(1)}, u32[]{:S(2)}, u32[]{:S(2)}) collective-permute-start(bf16[128,128]{0,1:T(8,128)(2,1)S(1)} %fusion.25), channel_id=1, source_target_pairs={{32,0},{64,32},{96,64},{128,96},{160,128},{192,160},{224,192},{256... | collective-permute-start | bytes 98312 | tf_op jit(solution)/shard_map/ppermute | solution.py:13
  64.6 0.8 collective-permute-done.2
  65.5 0.9 broadcast_in_dim.12
  66.4 7.2 %all-to-all-start.2 = ((bf16[16,128,128]{2,1,0:T(8,128)(2,1)}), bf16[16,128,128]{2,1,0:T(8,128)(2,1)S(1)}, u32[]{:S(2)}, u32[]{:S(2)}) async-start(bf16[16,128,128]{2,1,0:T(8,128)(2,1)} %broadcast_in_dim.12), calls=%async_computation.2 | async-start | bytes 1048576 | tf_op jit(solution)/shard_map/all_to_all | solution.py:27
  73.7 0.2 constant_dynamic-update-slice_fusion.7
  73.9 0.3 constant_dynamic-update-slice_fusion.6
  74.6 2.8 %all-gather.5 = bf16[256,256]{0,1:T(8,128)(2,1)S(1)} all-gather(bf16[128,256]{0,1:T(8,128)(2,1)S(1)} %pad_maximum_fusion.5), channel_id=7, replica_groups={{0,1},{2,3},{4,5},{6,7},{8,9},{10,11},{12,13},{14,15},{16,17},{18,19},{..., dimensions={0}, use_global_device_ids=true | all-gather | bytes 196608 | tf_op jit(solution)/shard_map/all_gather | solution.py:43
  77.5 2.8 %fusion.1 = bf16[16,128,128]{2,1,0:T(8,128)(2,1)} fusion(bf16[16,128,128]{2,1,0:T(8,128)(2,1)} %collective-permute-done.4, bf16[16,128,128]{2,1,0:T(8,128)(2,1)} %collective-permute-done.3, bf16[16,128,128]{2,1,0:T(8,128)(2,1)S(1)} %copy-done.7, bf16[16,128,128]{2,1,0:T(8,128)(2,1)S(1)} %copy-done.6, bf16[128,512]{0,1:T(8,128)(2,1)S(1)} %fusion.18), kind=kOutput, calls=%fused_computation.4 | convolution fusion | flops 277086208 | bytes 2752512 | tf_op jit(solution)/shard_map/cfk,rk->crf/dot_general | solution.py:129
  80.3 6.9 %all-to-all-done.2 = bf16[16,128,128]{2,1,0:T(8,128)(2,1)S(1)} async-done(((bf16[16,128,128]{2,1,0:T(8,128)(2,1)}), bf16[16,128,128]{2,1,0:T(8,128)(2,1)S(1)}, u32[]{:S(2)}, u32[]{:S(2)}) %all-to-all-start.2) | async-done | bytes 524320 | tf_op jit(solution)/shard_map/all_to_all | solution.py:27
  87.2 5.4 %all-to-all-start.4 = ((bf16[16,128,128]{2,1,0:T(8,128)(2,1)}), bf16[16,128,128]{2,1,0:T(8,128)(2,1)S(1)}, u32[]{:S(2)}, u32[]{:S(2)}) async-start(bf16[16,128,128]{2,1,0:T(8,128)(2,1)} %fusion.1), calls=%async_computation.4 | async-start | bytes 1048576 | tf_op jit(solution)/shard_map/all_to_all | solution.py:27
  92.7 0.3 convolution_bitcast_fusion.2
  93.0 3.6 %all-gather.2 = f32[256,128]{0,1:T(8,128)S(1)} all-gather(f32[128,128]{0,1:T(8,128)S(1)} %convolution_bitcast_fusion.2), channel_id=4, replica_groups={{0,1},{2,3},{4,5},{6,7},{8,9},{10,11},{12,13},{14,15},{16,17},{18,19},{..., dimensions={0}, use_global_device_ids=true | all-gather | bytes 196608 | tf_op jit(solution)/shard_map/all_gather | solution.py:43
  96.5 1.7 %fusion.7 = bf16[128,128]{0,1:T(8,128)(2,1)S(1)} fusion(bf16[16,128,128]{2,1,0:T(8,128)(2,1)S(1)} %all-to-all-done.2, bf16[128,16,1,128]{3,2,1,0:T(2,128)(2,1)} %copy-done.2, f32[256,128]{0,1:T(8,128)S(1)} %all-gather.2, pred[]{:T(512)S(6)} %eq.20), kind=kOutput, calls=%fused_computation.22 | convolution fusion | flops 67158016 | bytes 1212417 | tf_op jit(solution)/shard_map/dot_general | solution.py:52
  98.2 0.2 fusion.14
  98.6 0.3 fusion.15
  98.8 0.2 fusion.11
  99.1 0.2 convolution_convert_fusion.10
  99.3 0.2 convolution_convert_fusion.11
  99.6 0.2 constant_dynamic-update-slice_fusion.3
  99.9 0.3 constant_dynamic-update-slice_fusion.2
  100.5 1.9 %all-gather.3 = bf16[256,256]{0,1:T(8,128)(2,1)S(1)} all-gather(bf16[128,256]{0,1:T(8,128)(2,1)S(1)} %pad_maximum_fusion.4), channel_id=5, replica_groups={{0,1},{2,3},{4,5},{6,7},{8,9},{10,11},{12,13},{14,15},{16,17},{18,19},{..., dimensions={0}, use_global_device_ids=true | all-gather | bytes 196608 | tf_op jit(solution)/shard_map/all_gather | solution.py:43
  102.4 2.0 %fusion = bf16[16,1,128,128]{3,2,0,1:T(8,128)(2,1)S(1)} fusion(bf16[16,128,128]{2,1,0:T(8,128)(2,1)} %collective-permute-done.4, bf16[16,128,128]{2,1,0:T(8,128)(2,1)} %collective-permute-done.3, bf16[16,128,128]{2,1,0:T(8,128)(2,1)S(1)} %copy-done.8, bf16[16,128,128]{2,1,0:T(8,128)(2,1)S(1)} %copy-done.6, bf16[128,512]{0,1:T(8,128)(2,1)S(1)} %fusion.22), kind=kOutput, calls=%fused_computation.3 | convolution fusion | flops 277086208 | bytes 2752512 | tf_op jit(solution)/shard_map/cfk,rk->crf/dot_general | solution.py:129
  104.7 1.1 copy.60
  105.8 7.3 %all-to-all-start.3 = ((bf16[16,2,128,128]{3,2,1,0:T(8,128)(2,1)}), bf16[16,2,128,128]{3,2,1,0:T(8,128)(2,1)S(1)}, u32[]{:S(2)}, u32[]{:S(2)}) async-start(bf16[16,2,128,128]{3,2,1,0:T(8,128)(2,1)} %copy.60), calls=%async_computation.3 | async-start | bytes 2097152 | tf_op jit(solution)/shard_map/all_to_all | solution.py:27
  113.3 8.7 %collective-permute-start.5 = (bf16[128,128]{1,0:T(8,128)(2,1)S(1)}, bf16[128,128]{1,0:T(8,128)(2,1)S(1)}, u32[]{:S(2)}, u32[]{:S(2)}) collective-permute-start(bf16[128,128]{1,0:T(8,128)(2,1)S(1)} %fusion.28), channel_id=1, source_target_pairs={{32,0},{64,32},{96,64},{128,96},{160,128},{192,160},{224,192},{256... | collective-permute-start | bytes 98312 | tf_op jit(solution)/shard_map/ppermute | solution.py:13
  121.9 15.3 %all-to-all-done.3 = bf16[16,2,128,128]{3,2,1,0:T(8,128)(2,1)S(1)} async-done(((bf16[16,2,128,128]{3,2,1,0:T(8,128)(2,1)}), bf16[16,2,128,128]{3,2,1,0:T(8,128)(2,1)S(1)}, u32[]{:S(2)}, u32[]{:S(2)}) %all-to-all-start.3) | async-done | bytes 1048608 | tf_op jit(solution)/shard_map/all_to_all | solution.py:27
  137.2 0.3 convolution_bitcast_fusion
  137.5 5.1 %all-gather.4 = f32[256,128]{0,1:T(8,128)S(1)} all-gather(f32[128,128]{0,1:T(8,128)S(1)} %convolution_bitcast_fusion), channel_id=6, replica_groups={{0,1},{2,3},{4,5},{6,7},{8,9},{10,11},{12,13},{14,15},{16,17},{18,19},{..., dimensions={0}, use_global_device_ids=true | all-gather | bytes 196608 | tf_op jit(solution)/shard_map/all_gather | solution.py:43
  142.6 0.4 fusion.37
  143.2 0.7 copy.65
  143.9 0.6 add_bitcast_fusion
  (69 shorter events, 2.3 us)
Async XLA Ops:
  0.6 10.0 %copy-start.3 = (bf16[1,128,4096]{2,1,0:T(8,128)(2,1)S(1)}, bf16[1,128,4096]{2,1,0:T(8,128)(2,1)}, u32[]{:S(2)}) copy-start(bf16[1,128,4096]{2,1,0:T(8,128)(2,1)} %param.19) | copy-start | bytes 3145732
  2.4 22.0 %all-to-all-start = ((bf16[16,128,128]{2,1,0:T(8,128)(2,1)}), bf16[16,128,128]{2,1,0:T(8,128)(2,1)S(1)}, u32[]{:S(2)}, u32[]{:S(2)}) async-start(bf16[16,128,128]{2,1,0:T(8,128)(2,1)} %broadcast_in_dim.10), calls=%async_computation | async-start | bytes 1048576 | tf_op jit(solution)/shard_map/all_to_all | solution.py:27
  13.6 18.1 %copy-start.2 = (bf16[128,16,1,128]{3,2,1,0:T(2,128)(2,1)}, bf16[128,16,1,128]{3,2,1,0:T(2,128)(2,1)S(1)}, u32[]{:S(2)}) copy-start(bf16[128,16,1,128]{3,2,1,0:T(2,128)(2,1)S(1)} %get-tuple-element.9) | copy-start | bytes 1572868
  13.6 3.3 %copy-start.12 = (bf16[1,2,128,128]{3,2,1,0:T(8,128)(2,1)S(1)}, bf16[1,2,128,128]{3,2,1,0:T(8,128)(2,1)}, u32[]{:S(2)}) copy-start(bf16[1,2,128,128]{3,2,1,0:T(8,128)(2,1)} %param.14) | copy-start | bytes 196612
  13.6 3.3 %copy-start.13 = (bf16[1,2,128,128]{3,2,1,0:T(8,128)(2,1)S(1)}, bf16[1,2,128,128]{3,2,1,0:T(8,128)(2,1)}, u32[]{:S(2)}) copy-start(bf16[1,2,128,128]{3,2,1,0:T(8,128)(2,1)} %param.13) | copy-start | bytes 196612
  13.6 3.6 %copy-start.10 = (bf16[1,2,128,128]{3,2,1,0:T(8,128)(2,1)S(1)}, bf16[1,2,128,128]{3,2,1,0:T(8,128)(2,1)}, u32[]{:S(2)}) copy-start(bf16[1,2,128,128]{3,2,1,0:T(8,128)(2,1)} %param.15) | copy-start | bytes 196612
  14.0 4.4 %collective-permute-start = (bf16[128,16,128]{2,0,1:T(8,128)(2,1)S(1)}, bf16[128,16,128]{2,0,1:T(8,128)(2,1)S(1)}, u32[]{:S(2)}, u32[]{:S(2)}) collective-permute-start(bf16[128,16,128]{2,0,1:T(8,128)(2,1)S(1)} %bitcast.137), channel_id=1, source_target_pairs={{0,1},{1,0},{2,3},{3,2},{4,5},{5,4},{6,7},{7,6},{8,9},{9,8},{10,11... | collective-permute-start | bytes 1572872 | tf_op jit(solution)/shard_map/ppermute | solution.py:39
  31.6 20.0 %all-to-all-start.1 = ((bf16[16,128,128]{2,1,0:T(8,128)(2,1)}), bf16[16,128,128]{2,1,0:T(8,128)(2,1)S(1)}, u32[]{:S(2)}, u32[]{:S(2)}) async-start(bf16[16,128,128]{2,1,0:T(8,128)(2,1)} %broadcast_in_dim.11), calls=%async_computation.1 | async-start | bytes 1048576 | tf_op jit(solution)/shard_map/all_to_all | solution.py:27
  40.7 3.7 %copy-start.4 = (bf16[1,4096,128]{2,1,0:T(8,128)(2,1)S(1)}, bf16[1,4096,128]{2,1,0:T(8,128)(2,1)}, u32[]{:S(2)}) copy-start(bf16[1,4096,128]{2,1,0:T(8,128)(2,1)} %param.17) | copy-start | bytes 3145732
  41.9 9.7 %collective-permute-start.1 = (bf16[128,16,128]{2,0,1:T(8,128)(2,1)}, bf16[128,16,128]{2,0,1:T(8,128)(2,1)S(1)}, u32[]{:S(2)}, u32[]{:S(2)}) collective-permute-start(bf16[128,16,128]{2,0,1:T(8,128)(2,1)} %bitcast.133), channel_id=1, source_target_pairs={{0,1},{1,0},{2,3},{3,2},{4,5},{5,4},{6,7},{7,6},{8,9},{9,8},{10,11... | collective-permute-start | bytes 1572872 | tf_op jit(solution)/shard_map/ppermute | solution.py:39
  44.4 3.0 %copy-start.5 = (bf16[1,4096,128]{2,1,0:T(8,128)(2,1)S(1)}, bf16[1,4096,128]{2,1,0:T(8,128)(2,1)}, u32[]{:S(2)}) copy-start(bf16[1,4096,128]{2,1,0:T(8,128)(2,1)} %param.18) | copy-start | bytes 3145732
  45.5 31.9 %collective-permute-start.3 = (bf16[16,128,128]{2,1,0:T(8,128)(2,1)}, bf16[16,128,128]{2,1,0:T(8,128)(2,1)}, u32[]{:S(2)}, u32[]{:S(2)}) collective-permute-start(bf16[16,128,128]{2,1,0:T(8,128)(2,1)} %get-tuple-element.11), channel_id=1, source_target_pairs={{0,1},{1,0},{2,3},{3,2},{4,5},{5,4},{6,7},{7,6},{8,9},{9,8},{10,11... | collective-permute-start | bytes 1572872 | tf_op jit(solution)/shard_map/ppermute | solution.py:39
  47.4 3.6 %copy-start.9 = (bf16[1,128,128]{2,1,0:T(8,128)(2,1)S(1)}, bf16[1,128,128]{2,1,0:T(8,128)(2,1)}, u32[]{:S(2)}) copy-start(bf16[1,128,128]{2,1,0:T(8,128)(2,1)} %param.10) | copy-start | bytes 98308
  48.5 5.5 %copy-start = (bf16[128,16,1,128]{3,2,1,0:T(2,128)(2,1)S(1)}, bf16[128,16,1,128]{3,2,1,0:T(2,128)(2,1)}, u32[]{:S(2)}) copy-start(bf16[128,16,1,128]{3,2,1,0:T(2,128)(2,1)} %get-tuple-element.7) | copy-start | bytes 1572868
  48.5 28.9 %collective-permute-start.4 = (bf16[16,128,128]{2,1,0:T(8,128)(2,1)}, bf16[16,128,128]{2,1,0:T(8,128)(2,1)}, u32[]{:S(2)}, u32[]{:S(2)}) collective-permute-start(bf16[16,128,128]{2,1,0:T(8,128)(2,1)} %get-tuple-element.13), channel_id=1, source_target_pairs={{0,1},{1,0},{2,3},{3,2},{4,5},{5,4},{6,7},{7,6},{8,9},{9,8},{10,11... | collective-permute-start | bytes 1572872 | tf_op jit(solution)/shard_map/ppermute | solution.py:39
  51.6 12.8 %copy-start.14 = (bf16[1,128,128]{2,1,0:T(8,128)(2,1)S(1)}, bf16[1,128,128]{2,1,0:T(8,128)(2,1)}, u32[]{:S(2)}) copy-start(bf16[1,128,128]{2,1,0:T(8,128)(2,1)} %param.11) | copy-start | bytes 98308
  54.4 10.9 %collective-permute-start.2 = (bf16[128,128]{0,1:T(8,128)(2,1)S(1)}, bf16[128,128]{0,1:T(8,128)(2,1)S(1)}, u32[]{:S(2)}, u32[]{:S(2)}) collective-permute-start(bf16[128,128]{0,1:T(8,128)(2,1)S(1)} %fusion.25), channel_id=1, source_target_pairs={{32,0},{64,32},{96,64},{128,96},{160,128},{192,160},{224,192},{256... | collective-permute-start | bytes 98312 | tf_op jit(solution)/shard_map/ppermute | solution.py:13
  66.4 11.0 %copy-start.6 = (bf16[16,128,128]{2,1,0:T(8,128)(2,1)S(1)}, bf16[16,128,128]{2,1,0:T(8,128)(2,1)}, u32[]{:S(2)}) copy-start(bf16[16,128,128]{2,1,0:T(8,128)(2,1)} %get-tuple-element.10) | copy-start | bytes 1572868
  66.4 11.0 %copy-start.7 = (bf16[16,128,128]{2,1,0:T(8,128)(2,1)S(1)}, bf16[16,128,128]{2,1,0:T(8,128)(2,1)}, u32[]{:S(2)}) copy-start(bf16[16,128,128]{2,1,0:T(8,128)(2,1)} %get-tuple-element.12) | copy-start | bytes 1572868
  66.4 20.8 %all-to-all-start.2 = ((bf16[16,128,128]{2,1,0:T(8,128)(2,1)}), bf16[16,128,128]{2,1,0:T(8,128)(2,1)S(1)}, u32[]{:S(2)}, u32[]{:S(2)}) async-start(bf16[16,128,128]{2,1,0:T(8,128)(2,1)} %broadcast_in_dim.12), calls=%async_computation.2 | async-start | bytes 1048576 | tf_op jit(solution)/shard_map/all_to_all | solution.py:27
  87.2 18.6 %all-to-all-start.4 = ((bf16[16,128,128]{2,1,0:T(8,128)(2,1)}), bf16[16,128,128]{2,1,0:T(8,128)(2,1)S(1)}, u32[]{:S(2)}, u32[]{:S(2)}) async-start(bf16[16,128,128]{2,1,0:T(8,128)(2,1)} %fusion.1), calls=%async_computation.4 | async-start | bytes 1048576 | tf_op jit(solution)/shard_map/all_to_all | solution.py:27
  98.2 4.2 %copy-start.8 = (bf16[16,128,128]{2,1,0:T(8,128)(2,1)S(1)}, bf16[16,128,128]{2,1,0:T(8,128)(2,1)}, u32[]{:S(2)}) copy-start(bf16[16,128,128]{2,1,0:T(8,128)(2,1)} %get-tuple-element.12) | copy-start | bytes 1572868
  105.8 7.5 %copy-start.11 = (f32[1,128,128]{2,1,0:T(8,128)S(1)}, f32[1,128,128]{2,1,0:T(8,128)}, u32[]{:S(2)}) copy-start(f32[1,128,128]{2,1,0:T(8,128)} %param.12) | copy-start | bytes 196612
  105.8 31.4 %all-to-all-start.3 = ((bf16[16,2,128,128]{3,2,1,0:T(8,128)(2,1)}), bf16[16,2,128,128]{3,2,1,0:T(8,128)(2,1)S(1)}, u32[]{:S(2)}, u32[]{:S(2)}) async-start(bf16[16,2,128,128]{3,2,1,0:T(8,128)(2,1)} %copy.60), calls=%async_computation.3 | async-start | bytes 2097152 | tf_op jit(solution)/shard_map/all_to_all | solution.py:27
  113.2 29.4 %copy-start.1 = (bf16[128,16,1,128]{3,2,1,0:T(2,128)(2,1)S(1)}, bf16[128,16,1,128]{3,2,1,0:T(2,128)(2,1)}, u32[]{:S(2)}) copy-start(bf16[128,16,1,128]{3,2,1,0:T(2,128)(2,1)} %get-tuple-element.7) | copy-start | bytes 1572868
  113.3 30.6 %collective-permute-start.5 = (bf16[128,128]{1,0:T(8,128)(2,1)S(1)}, bf16[128,128]{1,0:T(8,128)(2,1)S(1)}, u32[]{:S(2)}, u32[]{:S(2)}) collective-permute-start(bf16[128,128]{1,0:T(8,128)(2,1)S(1)} %fusion.28), channel_id=1, source_target_pairs={{32,0},{64,32},{96,64},{128,96},{160,128},{192,160},{224,192},{256... | collective-permute-start | bytes 98312 | tf_op jit(solution)/shard_map/ppermute | solution.py:13

commit v2 on v0

v2 whole, which is shorter than its diff:
```python
import functools

import jax
import jax.numpy as jnp
from jax import lax
from jax.experimental import pallas as pl
from jax.experimental.pallas import tpu as pltpu
from jax.sharding import PartitionSpec as P

HEAD_DIM = 64
CORES = 2
X = 4
Z = 4
CHIPS = X * Z
W = 128
F32 = jnp.float32
BF16 = jnp.bfloat16
PARAMS = pltpu.CompilerParams(vmem_limit_bytes=24 * 1024 * 1024)


def vmem():
    return pl.BlockSpec(memory_space=pltpu.VMEM)


def anywhere():
    return pl.BlockSpec(memory_space=pl.ANY)


def passed_along(value, axis, steps):
    count = lax.axis_size(axis)
    leading, last = (max(0, -steps), min(count, count - steps))
    return lax.ppermute(value, axis, [(source, source + steps) for source in range(leading, last)])


def member(z, x, core):
    return (z * X + x) * CORES + core


def chip_exchange(parts):
    groups = [[chip * CORES + core for chip in range(CHIPS)] for core in range(CORES)]
    return lax.all_to_all(
        parts, "tp", split_axis=0, concat_axis=0, tiled=True, axis_index_groups=groups
    )


def sibling_swap(value):
    return lax.ppermute(value, "tp", [(i, i ^ 1) for i in range(CHIPS * CORES)])


def core_pair(value):
    groups = [[chip * CORES + core for core in range(CORES)] for chip in range(CHIPS)]
    return lax.all_gather(value, "tp", axis=0, tiled=False, axis_index_groups=groups)


def along_x(value, steps):
    return lax.ppermute(
        value,
        "tp",
        [
            (member(z, x, core), member(z, (x + steps) % X, core))
            for z in range(Z)
            for x in range(X)
            for core in range(CORES)
        ],
    )


def along_z(value, steps):
    return lax.ppermute(
        value,
        "tp",
        [
            (member(z, x, core), member((z + steps) % Z, x, core))
            for z in range(Z)
            for x in range(X)
            for core in range(CORES)
        ],
    )


def dot(a, b, da, db):
    return lax.dot_general(a, b, (((da,), (db,)), ((), ())), preferred_element_type=F32)


def core_index():
    return lax.rem(lax.axis_index("tp"), CORES)


def pack_kernel(wo, wq, wk, wv, oo, oq, ok, ov, so, sq, sk, sv):
    core = core_index()
    for chip in range(CHIPS):
        own = pl.ds(pl.multiple_of((chip * CORES + core) * W, W), W)
        other = pl.ds(pl.multiple_of((chip * CORES + 1 - core) * W, W), W)
        oo[chip] = wo[0, :, own]
        so[chip] = wo[0, :, other]
        oq[chip] = wq[0, :, own]
        sq[chip] = wq[0, :, other]
        ok[chip] = wk[0, own, :]
        sk[chip] = wk[0, other, :]
        ov[chip] = wv[0, own, :]
        sv[chip] = wv[0, other, :]


def pack(wo, wq, wk, wv):
    return pl.pallas_call(
        pack_kernel,
        out_shape=[jax.ShapeDtypeStruct((CHIPS, W, W), BF16)] * 8,
        in_specs=[vmem()] * 4,
        out_specs=[vmem()] * 8,
        compiler_params=PARAMS,
        cost_estimate=pl.CostEstimate(flops=0, bytes_accessed=8 << 20, transcendentals=0),
    )(wo, wq, wk, wv)


def pair_kernel(g, own, other, *rest):
    mine, theirs = rest[-2:]
    total = dot(g[0], other[0], 1, 1)
    for chip in range(1, CHIPS):
        total += dot(g[chip], other[chip], 1, 1)
    theirs[...] = total
    total = dot(g[0], own[0], 1, 1)
    for chip in range(1, CHIPS):
        total += dot(g[chip], own[chip], 1, 1)
    mine[...] = total


def pair_product(gathered, own, other, after=()):
    mine, theirs = pl.pallas_call(
        pair_kernel,
        out_shape=[jax.ShapeDtypeStruct((W, W), F32)] * 2,
        in_specs=[vmem()] * 3 + [anywhere()] * len(after),
        out_specs=[vmem()] * 2,
        compiler_params=PARAMS,
        cost_estimate=pl.CostEstimate(flops=2 * 2 * W * W * W * CHIPS, bytes_accessed=2 << 20, transcendentals=0),
    )(gathered, own, other, *after)
    return mine, core_pair(theirs)


def attention_kernel(slot, mine, both, queries, keys, values, *rest):
    qbc, kv = rest[-2:]
    upstream = (mine[...] + both[1 - core_index()]).astype(BF16)
    q_all, k_all, v_all = queries[0, slot], keys[0, slot], values[0, slot]
    lane = lax.broadcasted_iota(jnp.int32, (W, W), 1)
    zero = jnp.zeros((W, W), BF16)
    query_grad = key_grad = value_grad = None
    for head in range(W // HEAD_DIM):
        inside = (lane // HEAD_DIM) == head
        q = jnp.where(inside, q_all, zero)
        k = jnp.where(inside, k_all, zero)
        u = jnp.where(inside, upstream, zero)
        scores = dot(q, k_all, 1, 1)
        prob_grad = dot(u, v_all, 1, 1)
        top = jnp.max(scores, axis=-1, keepdims=True)
        raised = jnp.exp(scores - top)
        attention = raised / jnp.sum(raised, axis=-1, keepdims=True)
        weights = attention.astype(BF16)
        delta = jnp.sum(weights.astype(F32) * prob_grad, axis=-1, keepdims=True)
        score_grad = (attention * (prob_grad - delta)).astype(BF16)
        parts = (dot(score_grad, k, 1, 0), dot(score_grad, q, 0, 0), dot(weights, u, 0, 0))
        if head == 0:
            query_grad, key_grad, value_grad = parts
        else:
            query_grad, key_grad, value_grad = (
                query_grad + parts[0],
                key_grad + parts[1],
                value_grad + parts[2],
            )
    query_grad = query_grad.astype(BF16)
    for chip in range(CHIPS):
        qbc[chip] = query_grad
    kv[:, :W] = key_grad.astype(BF16)
    kv[:, W:] = value_grad.astype(BF16)


def attention_grads(mine, both, queries, keys, values, slot, after=()):
    return pl.pallas_call(
        functools.partial(attention_kernel, slot),
        out_shape=[
            jax.ShapeDtypeStruct((CHIPS, W, W), BF16),
            jax.ShapeDtypeStruct((W, 2 * W), BF16),
        ],
        in_specs=[vmem()] * 5 + [anywhere()] * len(after),
        out_specs=[vmem()] * 2,
        compiler_params=PARAMS,
        cost_estimate=pl.CostEstimate(flops=20 * W * W * W, bytes_accessed=1 << 20, transcendentals=2 * W * W),
    )(mine, both, queries, keys, values, *after)


def term_kernel(kv, both, ok, ov, rk, rv, *outs):
    own = kv[...]
    other = both[1 - core_index()]
    index = lax.axis_index("tp") // CORES
    z, x = index // X, lax.rem(index, X)
    for step in range(X):
        for j in range(Z):
            chip = lax.rem(z + j, Z) * X + lax.rem(x + step, X)
            total = dot(own[:, :W], ok[chip], 1, 1)
            total += dot(own[:, W:], ov[chip], 1, 1)
            total += dot(other[:, :W], rk[chip], 1, 1)
            total += dot(other[:, W:], rv[chip], 1, 1)
            outs[step][j] = total.astype(BF16)


def term_parts(kv, w_key, w_value):
    return pl.pallas_call(
        term_kernel,
        out_shape=[jax.ShapeDtypeStruct((Z, W, W), BF16)] * X,
        in_specs=[vmem()] * 6,
        out_specs=[vmem()] * X,
        compiler_params=PARAMS,
        cost_estimate=pl.CostEstimate(flops=2 * W * W * 4 * W * CHIPS, bytes_accessed=3 << 20, transcendentals=0),
    )(kv, core_pair(kv), w_key[0], w_value[0], w_key[1], w_value[1])


def spread_kernel(x, *rest):
    out = rest[-1]
    value = x[...].reshape(W, W)
    for chip in range(CHIPS):
        out[chip] = value


def spread(x, after=()):
    return pl.pallas_call(
        spread_kernel,
        out_shape=jax.ShapeDtypeStruct((CHIPS, W, W), BF16),
        in_specs=[vmem()] + [anywhere()] * len(after),
        out_specs=vmem(),
        compiler_params=PARAMS,
    )(x, *after)


def across_x(parts):
    arrived = [parts[0]] + [along_x(parts[step], step) for step in range(1, X)]
    return sum(part.astype(F32) for part in arrived).astype(BF16)


def sum_kernel(start, p0, p1, p2, p3, *rest):
    total = start[...].reshape(W, W)
    for part in (p0, p1, p2, p3):
        total += part[...].astype(F32)
    rest[-1][...] = total


def across_z(start, parts, after=()):
    arrived = [parts[0]] + [along_z(parts[step], step) for step in range(1, Z)]
    return pl.pallas_call(
        sum_kernel,
        out_shape=jax.ShapeDtypeStruct((W, W), F32),
        in_specs=[vmem()] * (1 + Z) + [anywhere()] * len(after),
        out_specs=vmem(),
        compiler_params=PARAMS,
    )(start, *arrived, *after)


def body(
    grad_in,
    fresh_grads,
    acc_in,
    queries,
    keys,
    values,
    query_weight,
    key_weight,
    value_weight,
    out_weight,
):
    is_top = lax.axis_index("section") == lax.axis_size("section") - 1
    is_core_0 = core_index() == 0
    slot_count = queries.shape[1]

    grad_slice = grad_in[0]
    gathered = chip_exchange(spread(grad_in))
    oo, oq, ok, ov, so, sq, sk, sv = pack(out_weight, query_weight, key_weight, value_weight)
    w_out = oo, sibling_swap(so)
    w_query = oq, sibling_swap(sq)
    w_key = ok, sibling_swap(sk)
    w_value = ov, sibling_swap(sv)

    carried = acc_in[0]
    passed = grad_slice
    ready = (w_query[1], w_key[1], w_value[1])
    summed_z = ()
    for slot in range(slot_count):
        last = slot + 1 == slot_count
        mine, both = pair_product(gathered, *w_out, after=ready)
        query_parts, kv = attention_grads(mine, both, queries, keys, values, slot, after=summed_z)
        all_queries = chip_exchange(query_parts)
        parts = term_parts(kv, w_key, w_value)
        mine, both = pair_product(all_queries, *w_query, after=() if last else parts)
        other = jnp.where(is_core_0, both[1], both[0])
        passed = (grad_slice.astype(F32) + mine + other).astype(BF16)
        terms = across_x(parts)
        if not last:
            received = passed_along(passed, "section", -1)
            grad_slice = jnp.where(is_top, fresh_grads[slot], received)
            gathered = chip_exchange(spread(grad_slice, after=(terms,)))
        carried = across_z(carried, terms, after=(both,) if last else ())
        if not last:
            carried = carried.astype(BF16)
            ready = (carried,)
            carried = passed_along(carried, "section", -1)
            summed_z = (carried,)
            carried = carried.astype(F32)
    return (passed[None], carried[None])


def solution(mesh):
    in_specs = (
        P("section", None, "tp"),
        P(None, None, "tp"),
        P("section", None, "tp"),
        P("section", None, None, "tp"),
        P("section", None, None, "tp"),
        P("section", None, None, "tp"),
        P("section", "tp", None),
        P("section", None, "tp"),
        P("section", None, "tp"),
        P("section", "tp", None),
    )
    out_specs = (P("section", None, "tp"), P("section", None, "tp"))
    return jax.shard_map(body, mesh=mesh, in_specs=in_specs, out_specs=out_specs, check_vma=False)
```

time: 222 us -> 154 us (0.69)
  waiting for transfers between devices: 116 us -> 13.9 us
  starting transfers between devices: 49.9 us -> 94.4 us
  blocking collectives: 31.6 us -> 16.2 us
  Pallas kernels: 0 us -> 11.7 us
  matrix products: 8.4 us -> 0 us
  local copies, waits for them, and re-layouts: 9.69 us -> 12.6 us
  other arithmetic: 4.18 us -> 1.86 us
    all_to_all x5 -> x4, waiting for transfers between devices: 115 us -> 0.01 us  [chip_exchange(): lax.all_to_all(parts, 'tp', split_axis=0, concat_axis=0, tiled=True, axis...]
    ppermute x0 -> x16, starting transfers between devices: none -> 48.8 us  [the longest x6 20.2 us: along_z(): lax.ppermute(value, 'tp', [(member(z, x, core), member((z + steps) % Z, x...]
    all_to_all x1 -> x0, blocking collectives: 31.6 us -> none  [from_everyone(): return lax.all_to_all(copies, axis, split_axis=0, concat_axis=0, tiled=True)]
    all_gather x0 -> x6, blocking collectives: none -> 16.2 us  [core_pair(): lax.all_gather(value, 'tp', axis=0, tiled=False, axis_index_groups=groups)]
    ppermute x0 -> x16, waiting for transfers between devices: none -> 13.9 us  [the longest x6 6.43 us: along_x(): lax.ppermute(value, 'tp', [(member(z, x, core), member(z, (x + steps) % X...]
    pallas_call x0 -> x13, Pallas kernels: none -> 11.7 us  [the longest x4 4.31 us: pair_product(): pl.pallas_call(pair_kernel, out_shape=[jax.ShapeDtypeStruct((W, W), F32)]...]
    unnamed x28 -> x46, local copies, waits for them, and re-layouts: 1.37 us -> 12.6 us
    dot_general x18 -> x0, matrix products: 7.85 us -> none  [the longest x8 5.49 us: transpose_product(): lax.dot_general(left, right, (((1,), (1,)), ((), ())), preferred_element_...]
  transfers between devices with their start and end apart: 7 -> 22, of which waited for: 6 -> 5; matrix products, arithmetic and copies ran while one was open for 6% -> 1% of each run, Pallas kernels for 0% -> 5%
where the time goes in v2:
time: 154 us; the launch traced here: 152 us
  starting transfers between devices  94.4 us (61%)
  blocking collectives  16.2 us (11%)
  waiting for transfers between devices  13.9 us (9%)
  local copies, waits for them, and re-layouts  12.6 us (8%)
  Pallas kernels  11.7 us (8%)
  other arithmetic  1.86 us (1%)
    all_to_all x4, starting transfers between devices, chip_exchange(): lax.all_to_all(parts, 'tp', split_axis=0, concat_axis=0, tiled=True, axis...  27.3 us
    ppermute x6, starting transfers between devices, along_z(): lax.ppermute(value, 'tp', [(member(z, x, core), member((z + steps) % Z, x...  20.2 us
    ppermute x6, starting transfers between devices, along_x(): lax.ppermute(value, 'tp', [(member(z, x, core), member(z, (x + steps) % X...  19.4 us
    ppermute x2, starting transfers between devices, passed_along(): lax.ppermute(value, axis, [(source, source + steps) for source in range(l...  18.3 us
    all_gather x6, blocking collectives, core_pair(): lax.all_gather(value, 'tp', axis=0, tiled=False, axis_index_groups=groups)  16.2 us
    unnamed x46, local copies, waits for them, and re-layouts  12.6 us
    ppermute x4, starting transfers between devices, sibling_swap(): return lax.ppermute(value, 'tp', [(i, i ^ 1) for i in range(CHIPS * CORES)])  9.1 us
    ppermute x6, waiting for transfers between devices, along_x(): lax.ppermute(value, 'tp', [(member(z, x, core), member(z, (x + steps) % X...  6.43 us
  transfers between devices with their start and end apart: 22, of which 5 were waited for; matrix products, arithmetic and copies ran while one was open for 1% of the time, Pallas kernels for 5%

profile of v2, /device:TPU:25, one launch (start us, length us, event | category | flops | bytes accessed | tf_op | source)
XLA Modules:
  0.0 151.9 jit_solution(2954567439969234022)
XLA Ops:
  0.6 0.7 copy-done.19
  1.4 0.9 shard_map.113
  2.3 8.4 %all-to-all-start = ((bf16[16,128,128]{2,1,0:T(8,128)(2,1)}), bf16[16,128,128]{2,1,0:T(8,128)(2,1)}, u32[]{:S(2)}, u32[]{:S(2)}) async-start(bf16[16,128,128]{2,1,0:T(8,128)(2,1)} %shard_map.113), calls=%async_computation | async-start | bytes 1048576 | tf_op jit(solution)/shard_map/all_to_all | solution.py:41
  10.7 0.0 copy-start.10
  10.7 1.2 copy-done.10
  11.9 1.2 copy-done.11
  13.1 1.2 copy-done.12
  14.4 0.7 shard_map.114
  15.0 0.8 copy-done.3
  15.8 0.8 copy-done.6
  16.6 2.9 %collective-permute-start = (bf16[16,128,128]{2,1,0:T(8,128)(2,1)S(1)}, bf16[16,128,128]{2,1,0:T(8,128)(2,1)S(1)}, u32[]{:S(2)}, u32[]{:S(2)}) collective-permute-start(bf16[16,128,128]{2,1,0:T(8,128)(2,1)S(1)} %get-tuple-element.31), channel_id=1, source_target_pairs={{0,1},{1,0},{2,3},{3,2},{4,5},{5,4},{6,7},{7,6},{8,9},{9,8},{10,11... | collective-permute-start | bytes 1572872 | tf_op jit(solution)/shard_map/ppermute | solution.py:47
  19.5 1.9 %collective-permute-start.1 = (bf16[16,128,128]{2,1,0:T(8,128)(2,1)S(1)}, bf16[16,128,128]{2,1,0:T(8,128)(2,1)S(1)}, u32[]{:S(2)}, u32[]{:S(2)}) collective-permute-start(bf16[16,128,128]{2,1,0:T(8,128)(2,1)S(1)} %get-tuple-element.32), channel_id=1, source_target_pairs={{0,1},{1,0},{2,3},{3,2},{4,5},{5,4},{6,7},{7,6},{8,9},{9,8},{10,11... | collective-permute-start | bytes 1572872 | tf_op jit(solution)/shard_map/ppermute | solution.py:47
  21.4 2.4 %collective-permute-start.2 = (bf16[16,128,128]{2,1,0:T(8,128)(2,1)S(1)}, bf16[16,128,128]{2,1,0:T(8,128)(2,1)S(1)}, u32[]{:S(2)}, u32[]{:S(2)}) collective-permute-start(bf16[16,128,128]{2,1,0:T(8,128)(2,1)S(1)} %get-tuple-element.33), channel_id=1, source_target_pairs={{0,1},{1,0},{2,3},{3,2},{4,5},{5,4},{6,7},{7,6},{8,9},{9,8},{10,11... | collective-permute-start | bytes 1572872 | tf_op jit(solution)/shard_map/ppermute | solution.py:47
  23.8 1.9 %collective-permute-start.3 = (bf16[16,128,128]{2,1,0:T(8,128)(2,1)S(1)}, bf16[16,128,128]{2,1,0:T(8,128)(2,1)S(1)}, u32[]{:S(2)}, u32[]{:S(2)}) collective-permute-start(bf16[16,128,128]{2,1,0:T(8,128)(2,1)S(1)} %get-tuple-element.34), channel_id=1, source_target_pairs={{0,1},{1,0},{2,3},{3,2},{4,5},{5,4},{6,7},{7,6},{8,9},{9,8},{10,11... | collective-permute-start | bytes 1572872 | tf_op jit(solution)/shard_map/ppermute | solution.py:47
  25.8 1.8 %collective-permute-done.3.rest_2_.rv = bf16[16,128,128]{2,1,0:T(8,128)(2,1)S(1)} collective-permute-done((bf16[16,128,128]{2,1,0:T(8,128)(2,1)S(1)}, bf16[16,128,128]{2,1,0:T(8,128)(2,1)S(1)}, u32[]{:S(2)}, u32[]{:S(2)}) %collective-permute-start.3) | collective-permute-done | bytes 524320 | tf_op jit(solution)/shard_map/ppermute | solution.py:47
  27.6 1.9 %shard_map.115 = (f32[128,128]{1,0:T(8,128)S(1)}, f32[128,128]{1,0:T(8,128)S(1)}) custom-call(bf16[16,128,128]{2,1,0:T(8,128)(2,1)} %all-to-all-done.g, bf16[16,128,128]{2,1,0:T(8,128)(2,1)S(1)} %get-tuple-element.30.own, bf16[16,128,128]{2,1,0:T(8,128)(2,1)S(1)} %collective-permute-done.other, ...), custom_call_target="tpu_custom_call" | custom-call | flops 134217728 | bytes 2097152 | tf_op jit(solution)/shard_map/pallas_call | solution.py:128
  29.5 0.0 copy-start.17
  29.5 2.0 %all-gather = f32[256,128]{1,0:T(8,128)S(1)} all-gather(f32[128,128]{1,0:T(8,128)S(1)} %get-tuple-element.36), channel_id=2, replica_groups={{0,1},{2,3},{4,5},{6,7},{8,9},{10,11},{12,13},{14,15},{16,17},{18,19},{..., dimensions={0}, use_global_device_ids=true | all-gather | bytes 196608 | tf_op jit(solution)/shard_map/all_gather | solution.py:52
  31.6 0.7 shard_map.116
  32.3 0.8 copy-done.14
  33.1 7.2 %all-to-all-start.1 = ((bf16[16,128,128]{2,1,0:T(8,128)(2,1)}), bf16[16,128,128]{2,1,0:T(8,128)(2,1)S(1)}, u32[]{:S(2)}, u32[]{:S(2)}) async-start(bf16[16,128,128]{2,1,0:T(8,128)(2,1)} %copy-done.14), calls=%async_computation.1 | async-start | bytes 1048576 | tf_op jit(solution)/shard_map/all_to_all | solution.py:41
  40.3 2.0 %all-gather.1 = bf16[256,256]{1,0:T(8,128)(2,1)S(1)} all-gather(bf16[128,256]{1,0:T(8,128)(2,1)S(1)} %get-tuple-element.39.kv), channel_id=3, replica_groups={{0,1},{2,3},{4,5},{6,7},{8,9},{10,11},{12,13},{14,15},{16,17},{18,19},{..., dimensions={0}, use_global_device_ids=true | all-gather | bytes 196608 | tf_op jit(solution)/shard_map/all_gather | solution.py:52
  42.3 1.0 copy-done.4
  43.3 1.0 copy-done.7
  44.4 2.2 %shard_map.117 = (bf16[4,128,128]{2,1,0:T(8,128)(2,1)S(1)}, bf16[4,128,128]{2,1,0:T(8,128)(2,1)}, bf16[4,128,128]{2,1,0:T(8,128)(2,1)}, bf16[4,128,128]{2,1,0:T(8,128)(2,1)}) custom-call(bf16[128,256]{1,0:T(8,128)(2,1)S(1)} %get-tuple-element.39.kv, bf16[2,128,256]{2,1,0:T(8,128)(2,1)S(1)} %bitcast.33, bf16[16,128,128]{2,1,0:T(8,128)(2,1)S(1)} %copy-done.4, ...), custom_call_target="tpu_custom_call" | custom-call | flops 268435456 | bytes 3145728 | tf_op jit(solution)/shard_map/pallas_call | solution.py:205
  46.5 4.7 %collective-permute-start.7 = (bf16[4,128,128]{2,1,0:T(8,128)(2,1)}, bf16[4,128,128]{2,1,0:T(8,128)(2,1)}, u32[]{:S(2)}, u32[]{:S(2)}) collective-permute-start(bf16[4,128,128]{2,1,0:T(8,128)(2,1)} %get-tuple-element.45.rest_3_), channel_id=1, source_target_pairs={{0,6},{1,7},{2,0},{3,1},{4,2},{5,3},{6,4},{7,5},{8,14},{9,15},{10,... | collective-permute-start | bytes 393224 | tf_op jit(solution)/shard_map/ppermute | solution.py:56
  51.3 2.5 %collective-permute-start.6 = (bf16[4,128,128]{2,1,0:T(8,128)(2,1)}, bf16[4,128,128]{2,1,0:T(8,128)(2,1)}, u32[]{:S(2)}, u32[]{:S(2)}) collective-permute-start(bf16[4,128,128]{2,1,0:T(8,128)(2,1)} %get-tuple-element.44.rest_2_), channel_id=1, source_target_pairs={{0,4},{1,5},{2,6},{3,7},{4,0},{5,1},{6,2},{7,3},{8,12},{9,13},{10,... | collective-permute-start | bytes 393224 | tf_op jit(solution)/shard_map/ppermute | solution.py:56
  53.8 2.5 %collective-permute-start.5 = (bf16[4,128,128]{2,1,0:T(8,128)(2,1)}, bf16[4,128,128]{2,1,0:T(8,128)(2,1)}, u32[]{:S(2)}, u32[]{:S(2)}) collective-permute-start(bf16[4,128,128]{2,1,0:T(8,128)(2,1)} %get-tuple-element.43.rest_1_), channel_id=1, source_target_pairs={{0,2},{1,3},{2,4},{3,5},{4,6},{5,7},{6,0},{7,1},{8,10},{9,11},{10,... | collective-permute-start | bytes 393224 | tf_op jit(solution)/shard_map/ppermute | solution.py:56
  56.3 0.8 shard_map.118
  57.1 2.7 %all-gather.2 = f32[256,128]{1,0:T(8,128)S(1)} all-gather(f32[128,128]{1,0:T(8,128)S(1)} %get-tuple-element.47), channel_id=4, replica_groups={{0,1},{2,3},{4,5},{6,7},{8,9},{10,11},{12,13},{14,15},{16,17},{18,19},{..., dimensions={0}, use_global_device_ids=true | all-gather | bytes 196608 | tf_op jit(solution)/shard_map/all_gather | solution.py:52
  59.9 9.9 %collective-permute-start.4 = (bf16[128,128]{1,0:T(8,128)(2,1)S(1)}, bf16[128,128]{1,0:T(8,128)(2,1)S(1)}, u32[]{:S(2)}, u32[]{:S(2)}) collective-permute-start(bf16[128,128]{1,0:T(8,128)(2,1)S(1)} %fusion.3), channel_id=1, source_target_pairs={{32,0},{64,32},{96,64},{128,96},{160,128},{192,160},{224,192},{256... | collective-permute-start | bytes 98312 | tf_op jit(solution)/shard_map/ppermute | solution.py:32
  69.9 1.1 add_convert_fusion.1.rest_0_
  71.0 0.1 shard_map.119
  71.1 0.8 copy-done.2
  71.9 6.2 %all-to-all-start.2 = ((bf16[16,128,128]{2,1,0:T(8,128)(2,1)}), bf16[16,128,128]{2,1,0:T(8,128)(2,1)S(1)}, u32[]{:S(2)}, u32[]{:S(2)}) async-start(bf16[16,128,128]{2,1,0:T(8,128)(2,1)} %copy-done.2), calls=%async_computation.2 | async-start | bytes 1048576 | tf_op jit(solution)/shard_map/all_to_all | solution.py:41
  78.2 3.3 %collective-permute-start.8 = (bf16[128,128]{1,0:T(8,128)(2,1)S(1)}, bf16[128,128]{1,0:T(8,128)(2,1)S(1)}, u32[]{:S(2)}, u32[]{:S(2)}) collective-permute-start(bf16[128,128]{1,0:T(8,128)(2,1)S(1)} %get-tuple-element.64), channel_id=1, source_target_pairs={{0,8},{1,9},{2,10},{3,11},{4,12},{5,13},{6,14},{7,15},{8,16},{9,17... | collective-permute-start | bytes 98312 | tf_op jit(solution)/shard_map/ppermute | solution.py:69
  81.4 4.0 %collective-permute-start.9 = (bf16[128,128]{1,0:T(8,128)(2,1)S(1)}, bf16[128,128]{1,0:T(8,128)(2,1)S(1)}, u32[]{:S(2)}, u32[]{:S(2)}) collective-permute-start(bf16[128,128]{1,0:T(8,128)(2,1)S(1)} %get-tuple-element.63), channel_id=1, source_target_pairs={{0,16},{1,17},{2,18},{3,19},{4,20},{5,21},{6,22},{7,23},{8,24},{9,... | collective-permute-start | bytes 98312 | tf_op jit(solution)/shard_map/ppermute | solution.py:69
  85.4 3.1 %collective-permute-start.10 = (bf16[128,128]{1,0:T(8,128)(2,1)S(1)}, bf16[128,128]{1,0:T(8,128)(2,1)S(1)}, u32[]{:S(2)}, u32[]{:S(2)}) collective-permute-start(bf16[128,128]{1,0:T(8,128)(2,1)S(1)} %get-tuple-element.62), channel_id=1, source_target_pairs={{0,24},{1,25},{2,26},{3,27},{4,28},{5,29},{6,30},{7,31},{8,0},{9,1... | collective-permute-start | bytes 98312 | tf_op jit(solution)/shard_map/ppermute | solution.py:69
  88.5 1.6 %collective-permute-done.8.p1 = bf16[128,128]{1,0:T(8,128)(2,1)S(1)} collective-permute-done((bf16[128,128]{1,0:T(8,128)(2,1)S(1)}, bf16[128,128]{1,0:T(8,128)(2,1)S(1)}, u32[]{:S(2)}, u32[]{:S(2)}) %collective-permute-start.8) | collective-permute-done | bytes 32800 | tf_op jit(solution)/shard_map/ppermute | solution.py:69
  90.1 4.0 %collective-permute-done.9.p2 = bf16[128,128]{1,0:T(8,128)(2,1)S(1)} collective-permute-done((bf16[128,128]{1,0:T(8,128)(2,1)S(1)}, bf16[128,128]{1,0:T(8,128)(2,1)S(1)}, u32[]{:S(2)}, u32[]{:S(2)}) %collective-permute-start.9) | collective-permute-done | bytes 32800 | tf_op jit(solution)/shard_map/ppermute | solution.py:69
  94.2 8.4 %collective-permute-start.11 = (bf16[128,128]{1,0:T(8,128)(2,1)S(1)}, bf16[128,128]{1,0:T(8,128)(2,1)S(1)}, u32[]{:S(2)}, u32[]{:S(2)}) collective-permute-start(bf16[128,128]{1,0:T(8,128)(2,1)S(1)} %convert_element_type.60.rest_0_), channel_id=1, source_target_pairs={{32,0},{64,32},{96,64},{128,96},{160,128},{192,160},{224,192},{256... | collective-permute-start | bytes 98312 | tf_op jit(solution)/shard_map/ppermute | solution.py:32
  102.6 1.0 copy-done.1
  103.6 0.8 shard_map.121
  104.4 0.0 copy-start.18
  104.5 3.8 %all-gather.3 = f32[256,128]{1,0:T(8,128)S(1)} all-gather(f32[128,128]{1,0:T(8,128)S(1)} %get-tuple-element.49), channel_id=5, replica_groups={{0,1},{2,3},{4,5},{6,7},{8,9},{10,11},{12,13},{14,15},{16,17},{18,19},{..., dimensions={0}, use_global_device_ids=true | all-gather | bytes 196608 | tf_op jit(solution)/shard_map/all_gather | solution.py:52
  108.2 0.7 shard_map.122
  108.9 0.8 copy-done.13
  109.7 5.5 %all-to-all-start.3 = ((bf16[16,128,128]{2,1,0:T(8,128)(2,1)}), bf16[16,128,128]{2,1,0:T(8,128)(2,1)S(1)}, u32[]{:S(2)}, u32[]{:S(2)}) async-start(bf16[16,128,128]{2,1,0:T(8,128)(2,1)} %copy-done.13), calls=%async_computation.3 | async-start | bytes 1048576 | tf_op jit(solution)/shard_map/all_to_all | solution.py:41
  115.3 2.2 %all-gather.5 = bf16[256,256]{1,0:T(8,128)(2,1)S(1)} all-gather(bf16[128,256]{1,0:T(8,128)(2,1)S(1)} %get-tuple-element.53.kv), channel_id=7, replica_groups={{0,1},{2,3},{4,5},{6,7},{8,9},{10,11},{12,13},{14,15},{16,17},{18,19},{..., dimensions={0}, use_global_device_ids=true | all-gather | bytes 196608 | tf_op jit(solution)/shard_map/all_gather | solution.py:52
  117.4 1.0 copy-done.8
  118.5 1.5 %shard_map.124 = (bf16[4,128,128]{2,1,0:T(8,128)(2,1)S(1)}, bf16[4,128,128]{2,1,0:T(8,128)(2,1)S(1)}, bf16[4,128,128]{2,1,0:T(8,128)(2,1)S(1)}, bf16[4,128,128]{2,1,0:T(8,128)(2,1)S(1)}) custom-call(bf16[128,256]{1,0:T(8,128)(2,1)S(1)} %get-tuple-element.53.kv, bf16[2,128,256]{2,1,0:T(8,128)(2,1)S(1)} %bitcast.31, bf16[16,128,128]{2,1,0:T(8,128)(2,1)S(1)} %copy-done.5, ...), custom_call_target="tpu_custom_call" | custom-call | flops 268435456 | bytes 3145728 | tf_op jit(solution)/shard_map/pallas_call | solution.py:205
  120.0 4.8 %collective-permute-start.14 = (bf16[4,128,128]{2,1,0:T(8,128)(2,1)S(1)}, bf16[4,128,128]{2,1,0:T(8,128)(2,1)S(1)}, u32[]{:S(2)}, u32[]{:S(2)}) collective-permute-start(bf16[4,128,128]{2,1,0:T(8,128)(2,1)S(1)} %get-tuple-element.57), channel_id=1, source_target_pairs={{0,6},{1,7},{2,0},{3,1},{4,2},{5,3},{6,4},{7,5},{8,14},{9,15},{10,... | collective-permute-start | bytes 393224 | tf_op jit(solution)/shard_map/ppermute | solution.py:56
  124.8 2.5 %collective-permute-start.13 = (bf16[4,128,128]{2,1,0:T(8,128)(2,1)S(1)}, bf16[4,128,128]{2,1,0:T(8,128)(2,1)S(1)}, u32[]{:S(2)}, u32[]{:S(2)}) collective-permute-start(bf16[4,128,128]{2,1,0:T(8,128)(2,1)S(1)} %get-tuple-element.56), channel_id=1, source_target_pairs={{0,4},{1,5},{2,6},{3,7},{4,0},{5,1},{6,2},{7,3},{8,12},{9,13},{10,... | collective-permute-start | bytes 393224 | tf_op jit(solution)/shard_map/ppermute | solution.py:56
  127.3 2.5 %collective-permute-start.12 = (bf16[4,128,128]{2,1,0:T(8,128)(2,1)S(1)}, bf16[4,128,128]{2,1,0:T(8,128)(2,1)S(1)}, u32[]{:S(2)}, u32[]{:S(2)}) collective-permute-start(bf16[4,128,128]{2,1,0:T(8,128)(2,1)S(1)} %get-tuple-element.55), channel_id=1, source_target_pairs={{0,2},{1,3},{2,4},{3,5},{4,6},{5,7},{6,0},{7,1},{8,10},{9,11},{10,... | collective-permute-start | bytes 393224 | tf_op jit(solution)/shard_map/ppermute | solution.py:56
  129.8 3.5 %collective-permute-done.13 = bf16[4,128,128]{2,1,0:T(8,128)(2,1)S(1)} collective-permute-done((bf16[4,128,128]{2,1,0:T(8,128)(2,1)S(1)}, bf16[4,128,128]{2,1,0:T(8,128)(2,1)S(1)}, u32[]{:S(2)}, u32[]{:S(2)}) %collective-permute-start.13) | collective-permute-done | bytes 131104 | tf_op jit(solution)/shard_map/ppermute | solution.py:56
  133.3 2.9 %collective-permute-done.12 = bf16[4,128,128]{2,1,0:T(8,128)(2,1)S(1)} collective-permute-done((bf16[4,128,128]{2,1,0:T(8,128)(2,1)S(1)}, bf16[4,128,128]{2,1,0:T(8,128)(2,1)S(1)}, u32[]{:S(2)}, u32[]{:S(2)}) %collective-permute-start.12) | collective-permute-done | bytes 131104 | tf_op jit(solution)/shard_map/ppermute | solution.py:56
  136.2 0.1 add_convert_fusion
  136.3 3.1 %collective-permute-start.15 = (bf16[128,128]{1,0:T(8,128)(2,1)S(1)}, bf16[128,128]{1,0:T(8,128)(2,1)S(1)}, u32[]{:S(2)}, u32[]{:S(2)}) collective-permute-start(bf16[128,128]{1,0:T(8,128)(2,1)S(1)} %get-tuple-element.60), channel_id=1, source_target_pairs={{0,8},{1,9},{2,10},{3,11},{4,12},{5,13},{6,14},{7,15},{8,16},{9,17... | collective-permute-start | bytes 98312 | tf_op jit(solution)/shard_map/ppermute | solution.py:69
  139.4 3.7 %collective-permute-start.16 = (bf16[128,128]{1,0:T(8,128)(2,1)S(1)}, bf16[128,128]{1,0:T(8,128)(2,1)S(1)}, u32[]{:S(2)}, u32[]{:S(2)}) collective-permute-start(bf16[128,128]{1,0:T(8,128)(2,1)S(1)} %get-tuple-element.59), channel_id=1, source_target_pairs={{0,16},{1,17},{2,18},{3,19},{4,20},{5,21},{6,22},{7,23},{8,24},{9,... | collective-permute-start | bytes 98312 | tf_op jit(solution)/shard_map/ppermute | solution.py:69
  143.1 3.1 %collective-permute-start.17 = (bf16[128,128]{1,0:T(8,128)(2,1)S(1)}, bf16[128,128]{1,0:T(8,128)(2,1)S(1)}, u32[]{:S(2)}, u32[]{:S(2)}) collective-permute-start(bf16[128,128]{1,0:T(8,128)(2,1)S(1)} %get-tuple-element.58), channel_id=1, source_target_pairs={{0,24},{1,25},{2,26},{3,27},{4,28},{5,29},{6,30},{7,31},{8,0},{9,1... | collective-permute-start | bytes 98312 | tf_op jit(solution)/shard_map/ppermute | solution.py:69
  146.2 0.8 shard_map.123
  147.1 3.5 %all-gather.4 = f32[256,128]{1,0:T(8,128)S(1)} all-gather(f32[128,128]{1,0:T(8,128)S(1)} %get-tuple-element.52), channel_id=6, replica_groups={{0,1},{2,3},{4,5},{6,7},{8,9},{10,11},{12,13},{14,15},{16,17},{18,19},{..., dimensions={0}, use_global_device_ids=true | all-gather | bytes 196608 | tf_op jit(solution)/shard_map/all_gather | solution.py:52
  150.6 0.6 fusion.4
  151.2 0.7 shard_map.125
  (54 shorter events, 0.2 us)
Async XLA Ops:
  0.6 0.8 copy-start.19
  2.3 8.4 %copy-start.9 = (bf16[1,128,4096]{2,1,0:T(8,128)(2,1)S(1)}, bf16[1,128,4096]{2,1,0:T(8,128)(2,1)}, u32[]{:S(2)}) copy-start(bf16[1,128,4096]{2,1,0:T(8,128)(2,1)} %wo.1) | copy-start | bytes 3145732
  2.3 25.3 %all-to-all-start = ((bf16[16,128,128]{2,1,0:T(8,128)(2,1)}), bf16[16,128,128]{2,1,0:T(8,128)(2,1)}, u32[]{:S(2)}, u32[]{:S(2)}) async-start(bf16[16,128,128]{2,1,0:T(8,128)(2,1)} %shard_map.113), calls=%async_computation | async-start | bytes 1048576 | tf_op jit(solution)/shard_map/all_to_all | solution.py:41
  10.7 1.2 copy-start.10
  11.9 1.2 copy-start.11
  13.1 1.2 copy-start.12
  15.0 0.8 copy-start.3
  15.8 0.8 copy-start.6
  16.6 9.1 %collective-permute-start = (bf16[16,128,128]{2,1,0:T(8,128)(2,1)S(1)}, bf16[16,128,128]{2,1,0:T(8,128)(2,1)S(1)}, u32[]{:S(2)}, u32[]{:S(2)}) collective-permute-start(bf16[16,128,128]{2,1,0:T(8,128)(2,1)S(1)} %get-tuple-element.31), channel_id=1, source_target_pairs={{0,1},{1,0},{2,3},{3,2},{4,5},{5,4},{6,7},{7,6},{8,9},{9,8},{10,11... | collective-permute-start | bytes 1572872 | tf_op jit(solution)/shard_map/ppermute | solution.py:47
  19.5 6.3 %collective-permute-start.1 = (bf16[16,128,128]{2,1,0:T(8,128)(2,1)S(1)}, bf16[16,128,128]{2,1,0:T(8,128)(2,1)S(1)}, u32[]{:S(2)}, u32[]{:S(2)}) collective-permute-start(bf16[16,128,128]{2,1,0:T(8,128)(2,1)S(1)} %get-tuple-element.32), channel_id=1, source_target_pairs={{0,1},{1,0},{2,3},{3,2},{4,5},{5,4},{6,7},{7,6},{8,9},{9,8},{10,11... | collective-permute-start | bytes 1572872 | tf_op jit(solution)/shard_map/ppermute | solution.py:47
  21.4 4.4 %collective-permute-start.2 = (bf16[16,128,128]{2,1,0:T(8,128)(2,1)S(1)}, bf16[16,128,128]{2,1,0:T(8,128)(2,1)S(1)}, u32[]{:S(2)}, u32[]{:S(2)}) collective-permute-start(bf16[16,128,128]{2,1,0:T(8,128)(2,1)S(1)} %get-tuple-element.33), channel_id=1, source_target_pairs={{0,1},{1,0},{2,3},{3,2},{4,5},{5,4},{6,7},{7,6},{8,9},{9,8},{10,11... | collective-permute-start | bytes 1572872 | tf_op jit(solution)/shard_map/ppermute | solution.py:47
  23.8 3.8 %collective-permute-start.3 = (bf16[16,128,128]{2,1,0:T(8,128)(2,1)S(1)}, bf16[16,128,128]{2,1,0:T(8,128)(2,1)S(1)}, u32[]{:S(2)}, u32[]{:S(2)}) collective-permute-start(bf16[16,128,128]{2,1,0:T(8,128)(2,1)S(1)} %get-tuple-element.34), channel_id=1, source_target_pairs={{0,1},{1,0},{2,3},{3,2},{4,5},{5,4},{6,7},{7,6},{8,9},{9,8},{10,11... | collective-permute-start | bytes 1572872 | tf_op jit(solution)/shard_map/ppermute | solution.py:47
  25.8 3.7 %copy-start = (bf16[16,128,128]{2,1,0:T(8,128)(2,1)}, bf16[16,128,128]{2,1,0:T(8,128)(2,1)S(1)}, u32[]{:S(2)}) copy-start(bf16[16,128,128]{2,1,0:T(8,128)(2,1)S(1)} %collective-permute-done.other) | copy-start | bytes 1572868
  29.5 2.1 %copy-start.15 = (bf16[1,2,128,128]{3,2,1,0:T(8,128)(2,1)S(1)}, bf16[1,2,128,128]{3,2,1,0:T(8,128)(2,1)}, u32[]{:S(2)}) copy-start(bf16[1,2,128,128]{3,2,1,0:T(8,128)(2,1)} %queries.3) | copy-start | bytes 196612
  29.5 2.1 %copy-start.16 = (bf16[1,2,128,128]{3,2,1,0:T(8,128)(2,1)S(1)}, bf16[1,2,128,128]{3,2,1,0:T(8,128)(2,1)}, u32[]{:S(2)}) copy-start(bf16[1,2,128,128]{3,2,1,0:T(8,128)(2,1)} %keys.3) | copy-start | bytes 196612
  29.5 2.1 %copy-start.17 = (bf16[1,2,128,128]{3,2,1,0:T(8,128)(2,1)S(1)}, bf16[1,2,128,128]{3,2,1,0:T(8,128)(2,1)}, u32[]{:S(2)}) copy-start(bf16[1,2,128,128]{3,2,1,0:T(8,128)(2,1)} %values.3) | copy-start | bytes 196612
  32.3 0.8 copy-start.14
  33.1 23.2 %all-to-all-start.1 = ((bf16[16,128,128]{2,1,0:T(8,128)(2,1)}), bf16[16,128,128]{2,1,0:T(8,128)(2,1)S(1)}, u32[]{:S(2)}, u32[]{:S(2)}) async-start(bf16[16,128,128]{2,1,0:T(8,128)(2,1)} %copy-done.14), calls=%async_computation.1 | async-start | bytes 1048576 | tf_op jit(solution)/shard_map/all_to_all | solution.py:41
  42.3 1.0 copy-start.4
  43.3 1.0 copy-start.7
  46.5 23.3 %collective-permute-start.7 = (bf16[4,128,128]{2,1,0:T(8,128)(2,1)}, bf16[4,128,128]{2,1,0:T(8,128)(2,1)}, u32[]{:S(2)}, u32[]{:S(2)}) collective-permute-start(bf16[4,128,128]{2,1,0:T(8,128)(2,1)} %get-tuple-element.45.rest_3_), channel_id=1, source_target_pairs={{0,6},{1,7},{2,0},{3,1},{4,2},{5,3},{6,4},{7,5},{8,14},{9,15},{10,... | collective-permute-start | bytes 393224 | tf_op jit(solution)/shard_map/ppermute | solution.py:56
  51.3 18.6 %collective-permute-start.6 = (bf16[4,128,128]{2,1,0:T(8,128)(2,1)}, bf16[4,128,128]{2,1,0:T(8,128)(2,1)}, u32[]{:S(2)}, u32[]{:S(2)}) collective-permute-start(bf16[4,128,128]{2,1,0:T(8,128)(2,1)} %get-tuple-element.44.rest_2_), channel_id=1, source_target_pairs={{0,4},{1,5},{2,6},{3,7},{4,0},{5,1},{6,2},{7,3},{8,12},{9,13},{10,... | collective-permute-start | bytes 393224 | tf_op jit(solution)/shard_map/ppermute | solution.py:56
  53.8 16.1 %collective-permute-start.5 = (bf16[4,128,128]{2,1,0:T(8,128)(2,1)}, bf16[4,128,128]{2,1,0:T(8,128)(2,1)}, u32[]{:S(2)}, u32[]{:S(2)}) collective-permute-start(bf16[4,128,128]{2,1,0:T(8,128)(2,1)} %get-tuple-element.43.rest_1_), channel_id=1, source_target_pairs={{0,2},{1,3},{2,4},{3,5},{4,6},{5,7},{6,0},{7,1},{8,10},{9,11},{10,... | collective-permute-start | bytes 393224 | tf_op jit(solution)/shard_map/ppermute | solution.py:56
  57.1 2.7 %copy-start.20 = (bf16[1,128,128]{2,1,0:T(8,128)(2,1)S(1)}, bf16[1,128,128]{2,1,0:T(8,128)(2,1)}, u32[]{:S(2)}) copy-start(bf16[1,128,128]{2,1,0:T(8,128)(2,1)} %x.1) | copy-start | bytes 98308
  59.9 11.1 %copy-start.22 = (bf16[1,128,128]{2,1,0:T(8,128)(2,1)S(1)}, bf16[1,128,128]{2,1,0:T(8,128)(2,1)}, u32[]{:S(2)}) copy-start(bf16[1,128,128]{2,1,0:T(8,128)(2,1)} %param.11) | copy-start | bytes 98308
  59.9 11.1 %collective-permute-start.4 = (bf16[128,128]{1,0:T(8,128)(2,1)S(1)}, bf16[128,128]{1,0:T(8,128)(2,1)S(1)}, u32[]{:S(2)}, u32[]{:S(2)}) collective-permute-start(bf16[128,128]{1,0:T(8,128)(2,1)S(1)} %fusion.3), channel_id=1, source_target_pairs={{32,0},{64,32},{96,64},{128,96},{160,128},{192,160},{224,192},{256... | collective-permute-start | bytes 98312 | tf_op jit(solution)/shard_map/ppermute | solution.py:32
  71.1 0.8 copy-start.2
  71.9 30.6 %all-to-all-start.2 = ((bf16[16,128,128]{2,1,0:T(8,128)(2,1)}), bf16[16,128,128]{2,1,0:T(8,128)(2,1)S(1)}, u32[]{:S(2)}, u32[]{:S(2)}) async-start(bf16[16,128,128]{2,1,0:T(8,128)(2,1)} %copy-done.2), calls=%async_computation.2 | async-start | bytes 1048576 | tf_op jit(solution)/shard_map/all_to_all | solution.py:41
  78.1 16.0 %copy-start.21 = (f32[1,128,128]{2,1,0:T(8,128)S(1)}, f32[1,128,128]{2,1,0:T(8,128)}, u32[]{:S(2)}) copy-start(f32[1,128,128]{2,1,0:T(8,128)} %param.12) | copy-start | bytes 196612
  78.2 12.0 %collective-permute-start.8 = (bf16[128,128]{1,0:T(8,128)(2,1)S(1)}, bf16[128,128]{1,0:T(8,128)(2,1)S(1)}, u32[]{:S(2)}, u32[]{:S(2)}) collective-permute-start(bf16[128,128]{1,0:T(8,128)(2,1)S(1)} %get-tuple-element.64), channel_id=1, source_target_pairs={{0,8},{1,9},{2,10},{3,11},{4,12},{5,13},{6,14},{7,15},{8,16},{9,17... | collective-permute-start | bytes 98312 | tf_op jit(solution)/shard_map/ppermute | solution.py:69
  81.4 12.7 %collective-permute-start.9 = (bf16[128,128]{1,0:T(8,128)(2,1)S(1)}, bf16[128,128]{1,0:T(8,128)(2,1)S(1)}, u32[]{:S(2)}, u32[]{:S(2)}) collective-permute-start(bf16[128,128]{1,0:T(8,128)(2,1)S(1)} %get-tuple-element.63), channel_id=1, source_target_pairs={{0,16},{1,17},{2,18},{3,19},{4,20},{5,21},{6,22},{7,23},{8,24},{9,... | collective-permute-start | bytes 98312 | tf_op jit(solution)/shard_map/ppermute | solution.py:69
  85.4 8.7 %collective-permute-start.10 = (bf16[128,128]{1,0:T(8,128)(2,1)S(1)}, bf16[128,128]{1,0:T(8,128)(2,1)S(1)}, u32[]{:S(2)}, u32[]{:S(2)}) collective-permute-start(bf16[128,128]{1,0:T(8,128)(2,1)S(1)} %get-tuple-element.62), channel_id=1, source_target_pairs={{0,24},{1,25},{2,26},{3,27},{4,28},{5,29},{6,30},{7,31},{8,0},{9,1... | collective-permute-start | bytes 98312 | tf_op jit(solution)/shard_map/ppermute | solution.py:69
  94.2 14.1 %collective-permute-start.11 = (bf16[128,128]{1,0:T(8,128)(2,1)S(1)}, bf16[128,128]{1,0:T(8,128)(2,1)S(1)}, u32[]{:S(2)}, u32[]{:S(2)}) collective-permute-start(bf16[128,128]{1,0:T(8,128)(2,1)S(1)} %convert_element_type.60.rest_0_), channel_id=1, source_target_pairs={{32,0},{64,32},{96,64},{128,96},{160,128},{192,160},{224,192},{256... | collective-permute-start | bytes 98312 | tf_op jit(solution)/shard_map/ppermute | solution.py:32
  102.6 1.0 copy-start.1
  104.4 3.8 %copy-start.18 = (bf16[1,2,128,128]{3,2,1,0:T(8,128)(2,1)S(1)}, bf16[1,2,128,128]{3,2,1,0:T(8,128)(2,1)}, u32[]{:S(2)}) copy-start(bf16[1,2,128,128]{3,2,1,0:T(8,128)(2,1)} %values.3) | copy-start | bytes 196612
  108.9 0.8 copy-start.13
  109.7 7.7 %copy-start.5 = (bf16[16,128,128]{2,1,0:T(8,128)(2,1)S(1)}, bf16[16,128,128]{2,1,0:T(8,128)(2,1)}, u32[]{:S(2)}) copy-start(bf16[16,128,128]{2,1,0:T(8,128)(2,1)} %copy-done.3) | copy-start | bytes 1572868
  109.7 36.5 %all-to-all-start.3 = ((bf16[16,128,128]{2,1,0:T(8,128)(2,1)}), bf16[16,128,128]{2,1,0:T(8,128)(2,1)S(1)}, u32[]{:S(2)}, u32[]{:S(2)}) async-start(bf16[16,128,128]{2,1,0:T(8,128)(2,1)} %copy-done.13), calls=%async_computation.3 | async-start | bytes 1048576 | tf_op jit(solution)/shard_map/all_to_all | solution.py:41
  117.4 1.0 copy-start.8
  120.0 9.8 %collective-permute-start.14 = (bf16[4,128,128]{2,1,0:T(8,128)(2,1)S(1)}, bf16[4,128,128]{2,1,0:T(8,128)(2,1)S(1)}, u32[]{:S(2)}, u32[]{:S(2)}) collective-permute-start(bf16[4,128,128]{2,1,0:T(8,128)(2,1)S(1)} %get-tuple-element.57), channel_id=1, source_target_pairs={{0,6},{1,7},{2,0},{3,1},{4,2},{5,3},{6,4},{7,5},{8,14},{9,15},{10,... | collective-permute-start | bytes 393224 | tf_op jit(solution)/shard_map/ppermute | solution.py:56
  124.8 8.5 %collective-permute-start.13 = (bf16[4,128,128]{2,1,0:T(8,128)(2,1)S(1)}, bf16[4,128,128]{2,1,0:T(8,128)(2,1)S(1)}, u32[]{:S(2)}, u32[]{:S(2)}) collective-permute-start(bf16[4,128,128]{2,1,0:T(8,128)(2,1)S(1)} %get-tuple-element.56), channel_id=1, source_target_pairs={{0,4},{1,5},{2,6},{3,7},{4,0},{5,1},{6,2},{7,3},{8,12},{9,13},{10,... | collective-permute-start | bytes 393224 | tf_op jit(solution)/shard_map/ppermute | solution.py:56
  127.3 8.9 %collective-permute-start.12 = (bf16[4,128,128]{2,1,0:T(8,128)(2,1)S(1)}, bf16[4,128,128]{2,1,0:T(8,128)(2,1)S(1)}, u32[]{:S(2)}, u32[]{:S(2)}) collective-permute-start(bf16[4,128,128]{2,1,0:T(8,128)(2,1)S(1)} %get-tuple-element.55), channel_id=1, source_target_pairs={{0,2},{1,3},{2,4},{3,5},{4,6},{5,7},{6,0},{7,1},{8,10},{9,11},{10,... | collective-permute-start | bytes 393224 | tf_op jit(solution)/shard_map/ppermute | solution.py:56
  136.3 14.9 %collective-permute-start.15 = (bf16[128,128]{1,0:T(8,128)(2,1)S(1)}, bf16[128,128]{1,0:T(8,128)(2,1)S(1)}, u32[]{:S(2)}, u32[]{:S(2)}) collective-permute-start(bf16[128,128]{1,0:T(8,128)(2,1)S(1)} %get-tuple-element.60), channel_id=1, source_target_pairs={{0,8},{1,9},{2,10},{3,11},{4,12},{5,13},{6,14},{7,15},{8,16},{9,17... | collective-permute-start | bytes 98312 | tf_op jit(solution)/shard_map/ppermute | solution.py:69
  139.4 11.8 %collective-permute-start.16 = (bf16[128,128]{1,0:T(8,128)(2,1)S(1)}, bf16[128,128]{1,0:T(8,128)(2,1)S(1)}, u32[]{:S(2)}, u32[]{:S(2)}) collective-permute-start(bf16[128,128]{1,0:T(8,128)(2,1)S(1)} %get-tuple-element.59), channel_id=1, source_target_pairs={{0,16},{1,17},{2,18},{3,19},{4,20},{5,21},{6,22},{7,23},{8,24},{9,... | collective-permute-start | bytes 98312 | tf_op jit(solution)/shard_map/ppermute | solution.py:69
  143.1 8.1 %collective-permute-start.17 = (bf16[128,128]{1,0:T(8,128)(2,1)S(1)}, bf16[128,128]{1,0:T(8,128)(2,1)S(1)}, u32[]{:S(2)}, u32[]{:S(2)}) collective-permute-start(bf16[128,128]{1,0:T(8,128)(2,1)S(1)} %get-tuple-element.58), channel_id=1, source_target_pairs={{0,24},{1,25},{2,26},{3,27},{4,28},{5,29},{6,30},{7,31},{8,0},{9,1... | collective-permute-start | bytes 98312 | tf_op jit(solution)/shard_map/ppermute | solution.py:69

commit v3 on v2

v3 whole, which is shorter than its diff:
```python
import functools

import jax
import jax.numpy as jnp
from jax import lax
from jax.experimental import pallas as pl
from jax.experimental.pallas import tpu as pltpu
from jax.sharding import PartitionSpec as P

HEAD_DIM = 64
CORES = 2
X = 4
Z = 4
CHIPS = X * Z
W = 128
F32 = jnp.float32
BF16 = jnp.bfloat16
PARAMS = pltpu.CompilerParams(vmem_limit_bytes=24 * 1024 * 1024)


def vmem():
    return pl.BlockSpec(memory_space=pltpu.VMEM)


def hbm():
    return pl.BlockSpec(memory_space=pltpu.HBM)


def anywhere():
    return pl.BlockSpec(memory_space=pl.ANY)


def passed_along(value, axis, steps):
    count = lax.axis_size(axis)
    leading, last = (max(0, -steps), min(count, count - steps))
    return lax.ppermute(value, axis, [(source, source + steps) for source in range(leading, last)])


def chip_exchange(parts):
    groups = [[chip * CORES + core for chip in range(CHIPS)] for core in range(CORES)]
    return lax.all_to_all(
        parts, "tp", split_axis=0, concat_axis=0, tiled=True, axis_index_groups=groups
    )


def member(z, x, core):
    return (z * X + x) * CORES + core


def exchange(parts, groups):
    return lax.all_to_all(
        parts, "tp", split_axis=0, concat_axis=0, tiled=True, axis_index_groups=groups
    )


def x_exchange(parts):
    return exchange(
        parts,
        [[member(z, x, core) for x in range(X)] for z in range(Z) for core in range(CORES)],
    )


def z_exchange(parts):
    return exchange(
        parts,
        [[member(z, x, core) for z in range(Z)] for x in range(X) for core in range(CORES)],
    )


def sibling_swap(value):
    return lax.ppermute(value, "tp", [(i, i ^ 1) for i in range(CHIPS * CORES)])


def core_pair(value):
    groups = [[chip * CORES + core for core in range(CORES)] for chip in range(CHIPS)]
    return lax.all_gather(value, "tp", axis=0, tiled=False, axis_index_groups=groups)


def dot(a, b, da, db):
    return lax.dot_general(a, b, (((da,), (db,)), ((), ())), preferred_element_type=F32)


def core_index():
    return lax.rem(lax.axis_index("tp"), CORES)


def halves():
    core = core_index()
    for chip in range(CHIPS):
        own = pl.ds(pl.multiple_of((chip * CORES + core) * W, W), W)
        other = pl.ds(pl.multiple_of((chip * CORES + 1 - core) * W, W), W)
        yield chip, own, other


def pack_columns_kernel(a, b, own_a, own_b, other_a, other_b):
    for chip, own, other in halves():
        other_a[chip] = a[0, :, other]
        other_b[chip] = b[0, :, other]
        own_a[chip] = a[0, :, own]
        own_b[chip] = b[0, :, own]


def pack_rows_kernel(a, b, *rest):
    own_a, own_b, other_a, other_b = rest[-4:]
    for chip, own, other in halves():
        other_a[chip] = a[0, other, :]
        other_b[chip] = b[0, other, :]
        own_a[chip] = a[0, own, :]
        own_b[chip] = b[0, own, :]


def pack(kernel, a, b, after=()):
    own_a, own_b, other_a, other_b = pl.pallas_call(
        kernel,
        out_shape=[jax.ShapeDtypeStruct((CHIPS, W, W), BF16)] * 4,
        in_specs=[vmem()] * 2 + [anywhere()] * len(after),
        out_specs=[vmem()] * 4,
        compiler_params=PARAMS,
        cost_estimate=pl.CostEstimate(flops=0, bytes_accessed=4 << 20, transcendentals=0),
    )(a, b, *after)
    return (own_a, sibling_swap(other_a)), (own_b, sibling_swap(other_b))


def pair_kernel(after, g, own, other, *rest):
    mine, theirs = rest[after:][:2]
    for out, weight in ((theirs, other), (mine, own)):
        out[...] = sum(dot(g[chip], weight[chip], 1, 1) for chip in range(CHIPS))


def last_pair_kernel(arrived, own, other, start, mine, theirs, total):
    for out, weight in ((theirs, other), (mine, own)):
        out[...] = sum(dot(arrived[chip, 0], weight[chip], 1, 1) for chip in range(CHIPS))
    total[...] = start[...].astype(F32) + sum(arrived[chip, 1].astype(F32) for chip in range(CHIPS))


def last_pair_product(arrived, own, other, start):
    mine, theirs, total = pl.pallas_call(
        last_pair_kernel,
        out_shape=[jax.ShapeDtypeStruct((W, W), F32)] * 3,
        in_specs=[vmem()] * 4,
        out_specs=[vmem()] * 3,
        compiler_params=PARAMS,
        cost_estimate=pl.CostEstimate(flops=2 * 2 * W * W * W * CHIPS, bytes_accessed=2 << 20, transcendentals=0),
    )(arrived, own, other, start)
    return mine, core_pair(theirs), total


def pair_product(gathered, own, other, after=(), held=()):
    fixed = 3 + len(after)
    mine, theirs, *freed = pl.pallas_call(
        functools.partial(pair_kernel, len(after + held)),
        out_shape=[jax.ShapeDtypeStruct((W, W), F32)] * 2
        + [jax.ShapeDtypeStruct(x.shape, x.dtype) for x in held],
        in_specs=[vmem()] * 3 + [anywhere()] * len(after + held),
        out_specs=[vmem()] * 2 + [anywhere()] * len(held),
        input_output_aliases={fixed + i: 2 + i for i in range(len(held))},
        compiler_params=PARAMS,
        cost_estimate=pl.CostEstimate(flops=2 * 2 * W * W * W * CHIPS, bytes_accessed=2 << 20, transcendentals=0),
    )(gathered, own, other, *after, *held)
    return mine, core_pair(theirs), *freed


def passed_kernel(grad, mine, both, passed):
    total = grad[...].reshape(W, W).astype(F32) + mine[...] + both[1 - core_index()]
    passed[...] = total.astype(BF16)


def passed_grad(grad, mine, both):
    return pl.pallas_call(
        passed_kernel,
        out_shape=jax.ShapeDtypeStruct((W, W), BF16),
        in_specs=[vmem()] * 3,
        out_specs=vmem(),
        compiler_params=PARAMS,
    )(grad, mine, both)


def send_to_all(value, out, sems):
    copies = [pltpu.make_async_copy(value, out.at[chip], sems.at[chip]) for chip in range(CHIPS)]
    for copy in copies:
        copy.start()
    return copies


def attention_kernel(slot, copied, mine, both, queries, keys, values, out, kv, *scratch):
    upstream = (mine[...] + both[1 - core_index()]).astype(BF16)
    q_all, k_all, v_all = queries[0, slot], keys[0, slot], values[0, slot]
    lane = lax.broadcasted_iota(jnp.int32, (W, W), 1)
    zero = jnp.zeros((W, W), BF16)
    query_grad = jnp.zeros((W, W), F32)
    kept = []
    for head in range(W // HEAD_DIM):
        inside = (lane // HEAD_DIM) == head
        q = jnp.where(inside, q_all, zero)
        k = jnp.where(inside, k_all, zero)
        u = jnp.where(inside, upstream, zero)
        scores = dot(q, k_all, 1, 1)
        prob_grad = dot(u, v_all, 1, 1)
        top = jnp.max(scores, axis=-1, keepdims=True)
        raised = jnp.exp(scores - top)
        attention = raised / jnp.sum(raised, axis=-1, keepdims=True)
        weights = attention.astype(BF16)
        delta = jnp.sum(weights.astype(F32) * prob_grad, axis=-1, keepdims=True)
        score_grad = (attention * (prob_grad - delta)).astype(BF16)
        query_grad += dot(score_grad, k, 1, 0)
        kept.append((score_grad, q, weights, u))
    copies = []
    if copied:
        held, sems = scratch
        held[...] = query_grad.astype(BF16)
        copies = send_to_all(held, out, sems)
    else:
        out[...] = query_grad.astype(BF16)
    key_grad = sum(dot(score_grad, q, 0, 0) for score_grad, q, _, _ in kept)
    value_grad = sum(dot(weights, u, 0, 0) for _, _, weights, u in kept)
    kv[:, :W] = key_grad.astype(BF16)
    kv[:, W:] = value_grad.astype(BF16)
    for copy in copies:
        copy.wait()


def attention_grads(mine, both, queries, keys, values, slot, copied):
    return pl.pallas_call(
        functools.partial(attention_kernel, slot, copied),
        out_shape=[
            pltpu.HBM((CHIPS, W, W), BF16) if copied else jax.ShapeDtypeStruct((W, W), BF16),
            jax.ShapeDtypeStruct((W, 2 * W), BF16),
        ],
        in_specs=[vmem()] * 5,
        out_specs=[hbm() if copied else vmem(), vmem()],
        scratch_shapes=[pltpu.VMEM((W, W), BF16), pltpu.SemaphoreType.DMA((CHIPS,))] if copied else [],
        compiler_params=PARAMS,
        cost_estimate=pl.CostEstimate(flops=20 * W * W * W, bytes_accessed=1 << 20, transcendentals=2 * W * W),
    )(mine, both, queries, keys, values)


def term_of(chip, own, other, ok, ov, rk, rv):
    total = dot(own[:, :W], ok[chip], 1, 1)
    total += dot(own[:, W:], ov[chip], 1, 1)
    total += dot(other[:, :W], rk[chip], 1, 1)
    total += dot(other[:, W:], rv[chip], 1, 1)
    return total.astype(BF16)


def term_kernel(kv, both, ok, ov, rk, rv, out):
    own, other = kv[...], both[1 - core_index()]
    for chip in range(CHIPS):
        out[chip % X, chip // X] = term_of(chip, own, other, ok, ov, rk, rv)


def last_kernel(kv, both, query_grad, ok, ov, rk, rv, *rest):
    out, held, term_sems, query_sems = rest[-4:]
    copies = [
        pltpu.make_async_copy(query_grad, out.at[chip, 0], query_sems.at[chip])
        for chip in range(CHIPS)
    ]
    for copy in copies:
        copy.start()
    own, other = kv[...], both[1 - core_index()]
    for chip in range(CHIPS):
        held[chip] = term_of(chip, own, other, ok, ov, rk, rv)
        copies.append(pltpu.make_async_copy(held.at[chip], out.at[chip, 1], term_sems.at[chip]))
        copies[-1].start()
    for copy in copies:
        copy.wait()


TERM_COST = pl.CostEstimate(flops=2 * W * W * 4 * W * CHIPS, bytes_accessed=3 << 20, transcendentals=0)


def term_parts(kv, w_key, w_value):
    return pl.pallas_call(
        term_kernel,
        out_shape=jax.ShapeDtypeStruct((X, Z, W, W), BF16),
        in_specs=[vmem()] * 6,
        out_specs=vmem(),
        compiler_params=PARAMS,
        cost_estimate=TERM_COST,
    )(kv, core_pair(kv), w_key[0], w_value[0], w_key[1], w_value[1])


def last_parts(kv, query_grad, w_key, w_value, after):
    return pl.pallas_call(
        last_kernel,
        out_shape=pltpu.HBM((CHIPS, 2, W, W), BF16),
        in_specs=[vmem()] * 7 + [anywhere()] * len(after),
        out_specs=hbm(),
        scratch_shapes=[
            pltpu.VMEM((CHIPS, W, W), BF16),
            pltpu.SemaphoreType.DMA((CHIPS,)),
            pltpu.SemaphoreType.DMA((CHIPS,)),
        ],
        compiler_params=PARAMS,
        cost_estimate=TERM_COST,
    )(kv, core_pair(kv), query_grad, w_key[0], w_value[0], w_key[1], w_value[1], *after)


def x_sum_kernel(parts, out):
    for z in range(Z):
        out[z] = sum(parts[x, z].astype(F32) for x in range(X)).astype(BF16)


def x_sum(parts):
    return pl.pallas_call(
        x_sum_kernel,
        out_shape=jax.ShapeDtypeStruct((Z, W, W), BF16),
        in_specs=[vmem()],
        out_specs=vmem(),
        compiler_params=PARAMS,
    )(parts)


def z_sum_kernel(start, parts, out):
    total = start[0] + sum(parts[z].astype(F32) for z in range(Z))
    out[...] = total.astype(BF16)


def z_sum(start, parts):
    return pl.pallas_call(
        z_sum_kernel,
        out_shape=jax.ShapeDtypeStruct((W, W), BF16),
        in_specs=[vmem()] * 2,
        out_specs=vmem(),
        compiler_params=PARAMS,
    )(start, parts)


def spread_kernel(x, *rest):
    out, sems = rest[-2:]
    for copy in send_to_all(x, out, sems):
        copy.wait()


def spread(x, after=()):
    return pl.pallas_call(
        spread_kernel,
        out_shape=pltpu.HBM((CHIPS, W, W), BF16),
        in_specs=[anywhere()] * (1 + len(after)),
        out_specs=hbm(),
        scratch_shapes=[pltpu.SemaphoreType.DMA((CHIPS,))],
        compiler_params=PARAMS,
    )(x, *after)


def next_kernel(slot, received, fresh, chosen):
    top = lax.axis_size("section") - 1
    chosen[...] = jnp.where(lax.axis_index("section") == top, fresh[slot], received[...])


def next_grad(received, fresh, slot):
    return pl.pallas_call(
        functools.partial(next_kernel, slot),
        out_shape=jax.ShapeDtypeStruct((W, W), BF16),
        in_specs=[vmem()] * 2,
        out_specs=vmem(),
        compiler_params=PARAMS,
        cost_estimate=pl.CostEstimate(flops=40_000_000_000, bytes_accessed=1 << 17, transcendentals=0),
    )(received, fresh)


def body(
    grad_in,
    fresh_grads,
    acc_in,
    queries,
    keys,
    values,
    query_weight,
    key_weight,
    value_weight,
    out_weight,
):
    slot_count = queries.shape[1]

    grad_slice = grad_in[0]
    gathered = chip_exchange(spread(grad_slice))
    w_out, w_query = pack(pack_columns_kernel, out_weight, query_weight)
    ready = (w_query[1],)
    passed = grad_slice
    for slot in range(slot_count):
        last = slot + 1 == slot_count
        mine, both = pair_product(gathered, *w_out, after=() if slot else ready)
        query_grad, kv = attention_grads(mine, both, queries, keys, values, slot, copied=not last)
        if slot == 0:
            w_key, w_value = pack(pack_rows_kernel, key_weight, value_weight, after=(mine,))
        if last:
            arrived = chip_exchange(last_parts(kv, query_grad, w_key, w_value, ready))
            mine, both, carried = last_pair_product(arrived, *w_query, carried)
        else:
            all_queries = chip_exchange(query_grad)
            terms = term_parts(kv, w_key, w_value)
            mine, both, terms = pair_product(all_queries, *w_query, held=(terms,))
        passed = passed_grad(grad_slice, mine, both)
        if not last:
            received = passed_along(passed, "section", -1)
            along_z = z_exchange(x_sum(x_exchange(terms)))
            grad_slice = next_grad(received, fresh_grads, slot)
            gathered = chip_exchange(spread(grad_slice, after=(along_z,)))
            carried = passed_along(z_sum(acc_in, along_z), "section", -1)
            ready = (carried,)
    return (passed[None], carried[None])


def solution(mesh):
    in_specs = (
        P("section", None, "tp"),
        P(None, None, "tp"),
        P("section", None, "tp"),
        P("section", None, None, "tp"),
        P("section", None, None, "tp"),
        P("section", None, None, "tp"),
        P("section", "tp", None),
        P("section", None, "tp"),
        P("section", None, "tp"),
        P("section", "tp", None),
    )
    out_specs = (P("section", None, "tp"), P("section", None, "tp"))
    return jax.shard_map(body, mesh=mesh, in_specs=in_specs, out_specs=out_specs, check_vma=False)
```

time: 154 us -> 147 us (0.955)
  starting transfers between devices: 94.4 us -> 51 us
  blocking collectives: 16.2 us -> 50.7 us
  waiting for transfers between devices: 13.9 us -> 19 us
  local copies, waits for them, and re-layouts: 12.6 us -> 8.91 us
  Pallas kernels: 11.7 us -> 14.9 us
  other arithmetic: 1.86 us -> 0 us
    ppermute x12 -> x0, starting transfers between devices: 39.7 us -> none  [the longest x6 20.2 us: along_z(): lax.ppermute(value, 'tp', [(member(z, x, core), member((z + steps) % Z, x...]
    all_to_all x0 -> x1, blocking collectives: none -> 28.9 us  [chip_exchange(): lax.all_to_all(parts, 'tp', split_axis=0, concat_axis=0, tiled=True, axis...]
    all_to_all x4 -> x3, waiting for transfers between devices: 0.01 us -> 12.3 us  [chip_exchange(): lax.all_to_all(parts, 'tp', split_axis=0, concat_axis=0, tiled=True, axis...]
    ppermute x12 -> x0, waiting for transfers between devices: 12 us -> none  [the longest x6 6.43 us: along_x(): lax.ppermute(value, 'tp', [(member(z, x, core), member(z, (x + steps) % X...]
    all_to_all x4 -> x3, starting transfers between devices: 27.3 us -> 18.9 us  [chip_exchange(): lax.all_to_all(parts, 'tp', split_axis=0, concat_axis=0, tiled=True, axis...]
    all_to_all x0 -> x2, starting transfers between devices: none -> 7.77 us  [exchange(): lax.all_to_all(parts, 'tp', split_axis=0, concat_axis=0, tiled=True, axis...]
    all_gather x6, blocking collectives: 16.2 us -> 21.8 us  [core_pair(): lax.all_gather(value, 'tp', axis=0, tiled=False, axis_index_groups=groups)]
    all_to_all x0 -> x2, waiting for transfers between devices: none -> 4.78 us  [exchange(): lax.all_to_all(parts, 'tp', split_axis=0, concat_axis=0, tiled=True, axis...]
  transfers between devices with their start and end apart: 22 -> 11, of which waited for: 5 -> 5; matrix products, arithmetic and copies ran while one was open for 1% -> 0% of each run, Pallas kernels for 5% -> 4%
where the time goes in v3:
time: 147 us; the launch traced here: 145 us
  starting transfers between devices  51 us (35%)
  blocking collectives  50.7 us (34%)
  waiting for transfers between devices  19 us (13%)
  Pallas kernels  14.9 us (10%)
  local copies, waits for them, and re-layouts  8.91 us (6%)
    all_to_all x1, blocking collectives, chip_exchange(): lax.all_to_all(parts, 'tp', split_axis=0, concat_axis=0, tiled=True, axis...  28.9 us
    all_gather x6, blocking collectives, core_pair(): lax.all_gather(value, 'tp', axis=0, tiled=False, axis_index_groups=groups)  21.8 us
    all_to_all x3, starting transfers between devices, chip_exchange(): lax.all_to_all(parts, 'tp', split_axis=0, concat_axis=0, tiled=True, axis...  18.9 us
    ppermute x2, starting transfers between devices, passed_along(): lax.ppermute(value, axis, [(source, source + steps) for source in range(l...  15.1 us
    all_to_all x3, waiting for transfers between devices, chip_exchange(): lax.all_to_all(parts, 'tp', split_axis=0, concat_axis=0, tiled=True, axis...  12.3 us
    ppermute x4, starting transfers between devices, sibling_swap(): return lax.ppermute(value, 'tp', [(i, i ^ 1) for i in range(CHIPS * CORES)])  9.25 us
    unnamed x34, local copies, waits for them, and re-layouts  8.91 us
    all_to_all x2, starting transfers between devices, exchange(): lax.all_to_all(parts, 'tp', split_axis=0, concat_axis=0, tiled=True, axis...  7.77 us
  transfers between devices with their start and end apart: 11, of which 5 were waited for; matrix products, arithmetic and copies ran while one was open for 0% of the time, Pallas kernels for 4%

profile of v3, /device:TPU:25, one launch (start us, length us, event | category | flops | bytes accessed | tf_op | source)
XLA Modules:
  0.0 145.3 jit_solution(1943217680462870593)
XLA Ops:
  0.6 0.0 copy-start.13
  0.6 0.7 copy-done.13
  1.4 0.9 shard_map.113
  2.3 8.2 %all-to-all-start = ((bf16[16,128,128]{2,1,0:T(8,128)(2,1)}), bf16[16,128,128]{2,1,0:T(8,128)(2,1)S(1)}, u32[]{:S(2)}, u32[]{:S(2)}) async-start(bf16[16,128,128]{2,1,0:T(8,128)(2,1)} %shard_map.113), calls=%async_computation | async-start | bytes 1048576 | tf_op jit(solution)/shard_map/all_to_all | solution.py:41
  10.5 0.0 copy-start.6
  10.6 1.2 copy-done.6
  11.8 1.2 copy-done.7
  13.0 0.5 shard_map.114
  13.5 2.9 %collective-permute-start = (bf16[16,128,128]{2,1,0:T(8,128)(2,1)S(1)}, bf16[16,128,128]{2,1,0:T(8,128)(2,1)S(1)}, u32[]{:S(2)}, u32[]{:S(2)}) collective-permute-start(bf16[16,128,128]{2,1,0:T(8,128)(2,1)S(1)} %get-tuple-element.25), channel_id=1, source_target_pairs={{0,1},{1,0},{2,3},{3,2},{4,5},{5,4},{6,7},{7,6},{8,9},{9,8},{10,11... | collective-permute-start | bytes 1572872 | tf_op jit(solution)/shard_map/ppermute | solution.py:71
  16.4 1.9 %collective-permute-start.1 = (bf16[16,128,128]{2,1,0:T(8,128)(2,1)S(1)}, bf16[16,128,128]{2,1,0:T(8,128)(2,1)S(1)}, u32[]{:S(2)}, u32[]{:S(2)}) collective-permute-start(bf16[16,128,128]{2,1,0:T(8,128)(2,1)S(1)} %get-tuple-element.26), channel_id=1, source_target_pairs={{0,1},{1,0},{2,3},{3,2},{4,5},{5,4},{6,7},{7,6},{8,9},{9,8},{10,11... | collective-permute-start | bytes 1572872 | tf_op jit(solution)/shard_map/ppermute | solution.py:71
  18.3 0.0 collective-permute-done.other
  18.4 1.9 %collective-permute-done.1.rest_0_.other = bf16[16,128,128]{2,1,0:T(8,128)(2,1)S(1)} collective-permute-done((bf16[16,128,128]{2,1,0:T(8,128)(2,1)S(1)}, bf16[16,128,128]{2,1,0:T(8,128)(2,1)S(1)}, u32[]{:S(2)}, u32[]{:S(2)}) %collective-permute-start.1) | collective-permute-done | bytes 524320 | tf_op jit(solution)/shard_map/ppermute | solution.py:71
  20.2 4.1 %all-to-all-done.g = bf16[16,128,128]{2,1,0:T(8,128)(2,1)S(1)} async-done(((bf16[16,128,128]{2,1,0:T(8,128)(2,1)}), bf16[16,128,128]{2,1,0:T(8,128)(2,1)S(1)}, u32[]{:S(2)}, u32[]{:S(2)}) %all-to-all-start) | async-done | bytes 524320 | tf_op jit(solution)/shard_map/all_to_all | solution.py:41
  24.3 0.8 shard_map.115
  25.1 0.0 copy-start.10
  25.2 0.0 copy-start.11
  25.2 0.0 copy-start.12
  25.2 4.3 %all-gather = f32[256,128]{1,0:T(8,128)S(1)} all-gather(f32[128,128]{1,0:T(8,128)S(1)} %get-tuple-element.28), channel_id=2, replica_groups={{0,1},{2,3},{4,5},{6,7},{8,9},{10,11},{12,13},{14,15},{16,17},{18,19},{..., dimensions={0}, use_global_device_ids=true | all-gather | bytes 196608 | tf_op jit(solution)/shard_map/all_gather | solution.py:76
  29.5 0.0 copy-done.10
  29.5 0.0 copy-done.11
  29.5 0.0 copy-done.12
  29.5 1.5 %shard_map.116 = (bf16[16,128,128]{2,1,0:T(8,128)(2,1)}, bf16[128,256]{1,0:T(8,128)(2,1)S(1)}) custom-call(f32[128,128]{1,0:T(8,128)S(1)} %get-tuple-element.27.mine.rest_0_, f32[2,128,128]{2,1,0:T(8,128)S(1)} %bitcast.11, bf16[1,2,128,128]{3,2,1,0:T(8,128)(2,1)S(1)} %copy-done.10, bf16[1,2,128,128]{3,2,1,0:T(8,128)(2,1)S(1)} %copy-done.11, ...), custom_call_target="tpu_custom_call" | custom-call | flops 41943040 | bytes 1048576 | tf_op jit(solution)/shard_map/pallas_call | solution.py:223
  31.1 4.2 %all-to-all-start.1 = ((bf16[16,128,128]{2,1,0:T(8,128)(2,1)}), bf16[16,128,128]{2,1,0:T(8,128)(2,1)S(1)}, u32[]{:S(2)}, u32[]{:S(2)}) async-start(bf16[16,128,128]{2,1,0:T(8,128)(2,1)} %get-tuple-element.29), calls=%async_computation.1 | async-start | bytes 1048576 | tf_op jit(solution)/shard_map/all_to_all | solution.py:41
  35.2 0.0 copy-start.8
  35.2 1.2 copy-done.8
  36.5 1.2 copy-done.9
  37.7 0.1 shard_map.117
  37.8 2.5 %collective-permute-start.2 = (bf16[16,128,128]{2,1,0:T(8,128)(2,1)S(1)}, bf16[16,128,128]{2,1,0:T(8,128)(2,1)S(1)}, u32[]{:S(2)}, u32[]{:S(2)}) collective-permute-start(bf16[16,128,128]{2,1,0:T(8,128)(2,1)S(1)} %get-tuple-element.34), channel_id=1, source_target_pairs={{0,1},{1,0},{2,3},{3,2},{4,5},{5,4},{6,7},{7,6},{8,9},{9,8},{10,11... | collective-permute-start | bytes 1572872 | tf_op jit(solution)/shard_map/ppermute | solution.py:71
  40.4 1.9 %collective-permute-start.3 = (bf16[16,128,128]{2,1,0:T(8,128)(2,1)S(1)}, bf16[16,128,128]{2,1,0:T(8,128)(2,1)S(1)}, u32[]{:S(2)}, u32[]{:S(2)}) collective-permute-start(bf16[16,128,128]{2,1,0:T(8,128)(2,1)S(1)} %get-tuple-element.35), channel_id=1, source_target_pairs={{0,1},{1,0},{2,3},{3,2},{4,5},{5,4},{6,7},{7,6},{8,9},{9,8},{10,11... | collective-permute-start | bytes 1572872 | tf_op jit(solution)/shard_map/ppermute | solution.py:71
  42.3 2.0 %all-gather.1 = bf16[256,256]{1,0:T(8,128)(2,1)S(1)} all-gather(bf16[128,256]{1,0:T(8,128)(2,1)S(1)} %get-tuple-element.31.kv), channel_id=3, replica_groups={{0,1},{2,3},{4,5},{6,7},{8,9},{10,11},{12,13},{14,15},{16,17},{18,19},{..., dimensions={0}, use_global_device_ids=true | all-gather | bytes 196608 | tf_op jit(solution)/shard_map/all_gather | solution.py:76
  44.4 0.0 collective-permute-done.2.rk
  44.4 0.0 collective-permute-done.3.rv
  44.4 2.4 %shard_map.118.rest_0_ = bf16[4,4,128,128]{3,2,1,0:T(8,128)(2,1)} custom-call(bf16[128,256]{1,0:T(8,128)(2,1)S(1)} %get-tuple-element.31.kv, bf16[2,128,256]{2,1,0:T(8,128)(2,1)S(1)} %bitcast.9, bf16[16,128,128]{2,1,0:T(8,128)(2,1)S(1)} %get-tuple-element.32.ok, bf16[16,128,128]{2,1,0:T(8,128)(2,1)S(1)} %get-tuple-element.33.ov, ...), custom_call_target="tpu_custom_call" | custom-call | flops 268435456 | bytes 3145728 | tf_op jit(solution)/shard_map/pallas_call | solution.py:272
  46.7 0.8 copy-done
  47.5 0.8 copy-done.2
  48.3 0.8 copy-done.4
  49.1 0.3 all-to-all-done.1.g
  49.4 0.8 shard_map.119
  50.2 4.2 %all-to-all-start.2 = ((bf16[4,4,128,128]{3,2,1,0:T(8,128)(2,1)}), bf16[4,4,128,128]{3,2,1,0:T(8,128)(2,1)S(1)}, u32[]{:S(2)}, u32[]{:S(2)}) async-start(bf16[4,4,128,128]{3,2,1,0:T(8,128)(2,1)} %get-tuple-element.38), calls=%async_computation.2 | async-start | bytes 1048576 | tf_op jit(solution)/shard_map/all_to_all | solution.py:51
  54.4 3.1 %all-gather.2 = f32[256,128]{1,0:T(8,128)S(1)} all-gather(f32[128,128]{1,0:T(8,128)S(1)} %get-tuple-element.37), channel_id=4, replica_groups={{0,1},{2,3},{4,5},{6,7},{8,9},{10,11},{12,13},{14,15},{16,17},{18,19},{..., dimensions={0}, use_global_device_ids=true | all-gather | bytes 196608 | tf_op jit(solution)/shard_map/all_gather | solution.py:76
  57.5 0.0 copy-done.14
  57.5 9.9 %collective-permute-start.4 = (bf16[128,128]{1,0:T(8,128)(2,1)S(1)}, bf16[128,128]{1,0:T(8,128)(2,1)S(1)}, u32[]{:S(2)}, u32[]{:S(2)}) collective-permute-start(bf16[128,128]{1,0:T(8,128)(2,1)S(1)} %shard_map.120), channel_id=1, source_target_pairs={{32,0},{64,32},{96,64},{128,96},{160,128},{192,160},{224,192},{256... | collective-permute-start | bytes 98312 | tf_op jit(solution)/shard_map/ppermute | solution.py:36
  67.4 0.0 all-to-all-done.2.parts
  67.4 0.7 shard_map.122
  68.2 3.6 %all-to-all-start.3 = ((bf16[4,128,128]{2,1,0:T(8,128)(2,1)}), bf16[4,128,128]{2,1,0:T(8,128)(2,1)S(1)}, u32[]{:S(2)}, u32[]{:S(2)}) async-start(bf16[4,128,128]{2,1,0:T(8,128)(2,1)} %shard_map.122), calls=%async_computation.3 | async-start | bytes 262144 | tf_op jit(solution)/shard_map/all_to_all | solution.py:51
  71.8 0.0 collective-permute-done.4.received
  71.8 4.8 %all-to-all-done.3.rest_0_.parts = bf16[4,128,128]{2,1,0:T(8,128)(2,1)S(1)} async-done(((bf16[4,128,128]{2,1,0:T(8,128)(2,1)}), bf16[4,128,128]{2,1,0:T(8,128)(2,1)S(1)}, u32[]{:S(2)}, u32[]{:S(2)}) %all-to-all-start.3) | async-done | bytes 131104 | tf_op jit(solution)/shard_map/all_to_all | solution.py:51
  76.6 1.0 shard_map.123
  77.5 6.5 %all-to-all-start.4 = ((bf16[16,128,128]{2,1,0:T(8,128)(2,1)}), bf16[16,128,128]{2,1,0:T(8,128)(2,1)S(1)}, u32[]{:S(2)}, u32[]{:S(2)}) async-start(bf16[16,128,128]{2,1,0:T(8,128)(2,1)} %shard_map.123), calls=%async_computation.4 | async-start | bytes 1048576 | tf_op jit(solution)/shard_map/all_to_all | solution.py:41
  84.1 0.0 copy-start.15
  84.1 0.8 copy-done.15
  84.9 5.2 %collective-permute-start.5 = (bf16[128,128]{1,0:T(8,128)(2,1)S(1)}, bf16[128,128]{1,0:T(8,128)(2,1)S(1)}, u32[]{:S(2)}, u32[]{:S(2)}) collective-permute-start(bf16[128,128]{1,0:T(8,128)(2,1)S(1)} %shard_map.126), channel_id=1, source_target_pairs={{32,0},{64,32},{96,64},{128,96},{160,128},{192,160},{224,192},{256... | collective-permute-start | bytes 98312 | tf_op jit(solution)/shard_map/ppermute | solution.py:36
  90.1 7.9 %all-to-all-done.4.g = bf16[16,128,128]{2,1,0:T(8,128)(2,1)S(1)} async-done(((bf16[16,128,128]{2,1,0:T(8,128)(2,1)}), bf16[16,128,128]{2,1,0:T(8,128)(2,1)S(1)}, u32[]{:S(2)}, u32[]{:S(2)}) %all-to-all-start.4) | async-done | bytes 524320 | tf_op jit(solution)/shard_map/all_to_all | solution.py:41
  98.1 0.8 shard_map.124
  98.9 6.2 %all-gather.3 = f32[256,128]{1,0:T(8,128)S(1)} all-gather(f32[128,128]{1,0:T(8,128)S(1)} %get-tuple-element.40), channel_id=5, replica_groups={{0,1},{2,3},{4,5},{6,7},{8,9},{10,11},{12,13},{14,15},{16,17},{18,19},{..., dimensions={0}, use_global_device_ids=true | all-gather | bytes 196608 | tf_op jit(solution)/shard_map/all_gather | solution.py:76
  105.1 0.7 shard_map.125
  105.8 1.9 %all-gather.4 = bf16[256,256]{1,0:T(8,128)(2,1)S(1)} all-gather(bf16[128,256]{1,0:T(8,128)(2,1)S(1)} %get-tuple-element.41.kv), channel_id=6, replica_groups={{0,1},{2,3},{4,5},{6,7},{8,9},{10,11},{12,13},{14,15},{16,17},{18,19},{..., dimensions={0}, use_global_device_ids=true | all-gather | bytes 196608 | tf_op jit(solution)/shard_map/all_gather | solution.py:76
  107.7 0.0 collective-permute-done.5.rest_0_.start
  107.7 0.0 copy-done.1
  107.7 2.5 %shard_map.127 = bf16[16,2,128,128]{3,2,1,0:T(8,128)(2,1)} custom-call(bf16[128,256]{1,0:T(8,128)(2,1)S(1)} %get-tuple-element.41.kv, bf16[2,128,256]{2,1,0:T(8,128)(2,1)S(1)} %bitcast.14, bf16[128,128]{1,0:T(8,128)(2,1)S(1)} %get-tuple-element.42.query_grad, bf16[16,128,128]{2,1,0:T(8,128)(2,1)S(1)} %get-tuple-element.32.ok, ...), custom_call_target="tpu_custom_call" | custom-call | flops 268435456 | bytes 3145728 | tf_op jit(solution)/shard_map/pallas_call | solution.py:283
  110.2 28.9 %all_to_all.30.arrived = bf16[16,2,128,128]{3,2,1,0:T(8,128)(2,1)S(1)} all-to-all(bf16[16,2,128,128]{3,2,1,0:T(8,128)(2,1)} %shard_map.127), channel_id=1, replica_groups={{0,2,4,6,8,10,12,14,16,18,20,22,24,26,28,30},{1,3,5,7,9,11,13,15,17,19,..., dimensions={0} | all-to-all | bytes 2097152 | tf_op jit(solution)/shard_map/all_to_all | solution.py:41
  139.0 1.4 shard_map.128
  140.4 4.2 %all-gather.5 = f32[256,128]{1,0:T(8,128)S(1)} all-gather(f32[128,128]{1,0:T(8,128)S(1)} %get-tuple-element.44), channel_id=7, replica_groups={{0,1},{2,3},{4,5},{6,7},{8,9},{10,11},{12,13},{14,15},{16,17},{18,19},{..., dimensions={0}, use_global_device_ids=true | all-gather | bytes 196608 | tf_op jit(solution)/shard_map/all_gather | solution.py:76
  144.7 0.6 shard_map.129
  (16 shorter events, 0.1 us)
Async XLA Ops:
  0.6 0.8 copy-start.13
  2.3 22.0 %all-to-all-start = ((bf16[16,128,128]{2,1,0:T(8,128)(2,1)}), bf16[16,128,128]{2,1,0:T(8,128)(2,1)S(1)}, u32[]{:S(2)}, u32[]{:S(2)}) async-start(bf16[16,128,128]{2,1,0:T(8,128)(2,1)} %shard_map.113), calls=%async_computation | async-start | bytes 1048576 | tf_op jit(solution)/shard_map/all_to_all | solution.py:41
  10.5 1.2 copy-start.6
  11.8 1.2 copy-start.7
  13.5 4.8 %collective-permute-start = (bf16[16,128,128]{2,1,0:T(8,128)(2,1)S(1)}, bf16[16,128,128]{2,1,0:T(8,128)(2,1)S(1)}, u32[]{:S(2)}, u32[]{:S(2)}) collective-permute-start(bf16[16,128,128]{2,1,0:T(8,128)(2,1)S(1)} %get-tuple-element.25), channel_id=1, source_target_pairs={{0,1},{1,0},{2,3},{3,2},{4,5},{5,4},{6,7},{7,6},{8,9},{9,8},{10,11... | collective-permute-start | bytes 1572872 | tf_op jit(solution)/shard_map/ppermute | solution.py:71
  16.4 3.8 %collective-permute-start.1 = (bf16[16,128,128]{2,1,0:T(8,128)(2,1)S(1)}, bf16[16,128,128]{2,1,0:T(8,128)(2,1)S(1)}, u32[]{:S(2)}, u32[]{:S(2)}) collective-permute-start(bf16[16,128,128]{2,1,0:T(8,128)(2,1)S(1)} %get-tuple-element.26), channel_id=1, source_target_pairs={{0,1},{1,0},{2,3},{3,2},{4,5},{5,4},{6,7},{7,6},{8,9},{9,8},{10,11... | collective-permute-start | bytes 1572872 | tf_op jit(solution)/shard_map/ppermute | solution.py:71
  25.1 4.3 %copy-start.10 = (bf16[1,2,128,128]{3,2,1,0:T(8,128)(2,1)S(1)}, bf16[1,2,128,128]{3,2,1,0:T(8,128)(2,1)}, u32[]{:S(2)}) copy-start(bf16[1,2,128,128]{3,2,1,0:T(8,128)(2,1)} %queries.3) | copy-start | bytes 196612
  25.2 4.3 %copy-start.11 = (bf16[1,2,128,128]{3,2,1,0:T(8,128)(2,1)S(1)}, bf16[1,2,128,128]{3,2,1,0:T(8,128)(2,1)}, u32[]{:S(2)}) copy-start(bf16[1,2,128,128]{3,2,1,0:T(8,128)(2,1)} %keys.3) | copy-start | bytes 196612
  25.2 4.3 %copy-start.12 = (bf16[1,2,128,128]{3,2,1,0:T(8,128)(2,1)S(1)}, bf16[1,2,128,128]{3,2,1,0:T(8,128)(2,1)}, u32[]{:S(2)}) copy-start(bf16[1,2,128,128]{3,2,1,0:T(8,128)(2,1)} %values.3) | copy-start | bytes 196612
  31.1 18.3 %all-to-all-start.1 = ((bf16[16,128,128]{2,1,0:T(8,128)(2,1)}), bf16[16,128,128]{2,1,0:T(8,128)(2,1)S(1)}, u32[]{:S(2)}, u32[]{:S(2)}) async-start(bf16[16,128,128]{2,1,0:T(8,128)(2,1)} %get-tuple-element.29), calls=%async_computation.1 | async-start | bytes 1048576 | tf_op jit(solution)/shard_map/all_to_all | solution.py:41
  35.2 1.2 copy-start.8
  36.5 1.2 copy-start.9
  37.8 6.5 %collective-permute-start.2 = (bf16[16,128,128]{2,1,0:T(8,128)(2,1)S(1)}, bf16[16,128,128]{2,1,0:T(8,128)(2,1)S(1)}, u32[]{:S(2)}, u32[]{:S(2)}) collective-permute-start(bf16[16,128,128]{2,1,0:T(8,128)(2,1)S(1)} %get-tuple-element.34), channel_id=1, source_target_pairs={{0,1},{1,0},{2,3},{3,2},{4,5},{5,4},{6,7},{7,6},{8,9},{9,8},{10,11... | collective-permute-start | bytes 1572872 | tf_op jit(solution)/shard_map/ppermute | solution.py:71
  40.4 4.0 %collective-permute-start.3 = (bf16[16,128,128]{2,1,0:T(8,128)(2,1)S(1)}, bf16[16,128,128]{2,1,0:T(8,128)(2,1)S(1)}, u32[]{:S(2)}, u32[]{:S(2)}) collective-permute-start(bf16[16,128,128]{2,1,0:T(8,128)(2,1)S(1)} %get-tuple-element.35), channel_id=1, source_target_pairs={{0,1},{1,0},{2,3},{3,2},{4,5},{5,4},{6,7},{7,6},{8,9},{9,8},{10,11... | collective-permute-start | bytes 1572872 | tf_op jit(solution)/shard_map/ppermute | solution.py:71
  46.7 0.8 copy-start
  47.5 0.8 copy-start.2
  48.3 0.8 copy-start.4
  50.2 17.2 %all-to-all-start.2 = ((bf16[4,4,128,128]{3,2,1,0:T(8,128)(2,1)}), bf16[4,4,128,128]{3,2,1,0:T(8,128)(2,1)S(1)}, u32[]{:S(2)}, u32[]{:S(2)}) async-start(bf16[4,4,128,128]{3,2,1,0:T(8,128)(2,1)} %get-tuple-element.38), calls=%async_computation.2 | async-start | bytes 1048576 | tf_op jit(solution)/shard_map/all_to_all | solution.py:51
  54.4 3.1 %copy-start.14 = (bf16[1,128,128]{2,1,0:T(8,128)(2,1)S(1)}, bf16[1,128,128]{2,1,0:T(8,128)(2,1)}, u32[]{:S(2)}) copy-start(bf16[1,128,128]{2,1,0:T(8,128)(2,1)} %param.10) | copy-start | bytes 98308
  57.5 14.3 %collective-permute-start.4 = (bf16[128,128]{1,0:T(8,128)(2,1)S(1)}, bf16[128,128]{1,0:T(8,128)(2,1)S(1)}, u32[]{:S(2)}, u32[]{:S(2)}) collective-permute-start(bf16[128,128]{1,0:T(8,128)(2,1)S(1)} %shard_map.120), channel_id=1, source_target_pairs={{32,0},{64,32},{96,64},{128,96},{160,128},{192,160},{224,192},{256... | collective-permute-start | bytes 98312 | tf_op jit(solution)/shard_map/ppermute | solution.py:36
  68.2 3.6 %copy-start.16 = (bf16[1,128,128]{2,1,0:T(8,128)(2,1)S(1)}, bf16[1,128,128]{2,1,0:T(8,128)(2,1)}, u32[]{:S(2)}) copy-start(bf16[1,128,128]{2,1,0:T(8,128)(2,1)} %fresh.1) | copy-start | bytes 98308
  68.2 8.4 %all-to-all-start.3 = ((bf16[4,128,128]{2,1,0:T(8,128)(2,1)}), bf16[4,128,128]{2,1,0:T(8,128)(2,1)S(1)}, u32[]{:S(2)}, u32[]{:S(2)}) async-start(bf16[4,128,128]{2,1,0:T(8,128)(2,1)} %shard_map.122), calls=%async_computation.3 | async-start | bytes 262144 | tf_op jit(solution)/shard_map/all_to_all | solution.py:51
  77.5 20.5 %all-to-all-start.4 = ((bf16[16,128,128]{2,1,0:T(8,128)(2,1)}), bf16[16,128,128]{2,1,0:T(8,128)(2,1)S(1)}, u32[]{:S(2)}, u32[]{:S(2)}) async-start(bf16[16,128,128]{2,1,0:T(8,128)(2,1)} %shard_map.123), calls=%async_computation.4 | async-start | bytes 1048576 | tf_op jit(solution)/shard_map/all_to_all | solution.py:41
  84.1 0.8 copy-start.15
  84.9 22.7 %collective-permute-start.5 = (bf16[128,128]{1,0:T(8,128)(2,1)S(1)}, bf16[128,128]{1,0:T(8,128)(2,1)S(1)}, u32[]{:S(2)}, u32[]{:S(2)}) collective-permute-start(bf16[128,128]{1,0:T(8,128)(2,1)S(1)} %shard_map.126), channel_id=1, source_target_pairs={{32,0},{64,32},{96,64},{128,96},{160,128},{192,160},{224,192},{256... | collective-permute-start | bytes 98312 | tf_op jit(solution)/shard_map/ppermute | solution.py:36
  98.1 9.6 %copy-start.3 = (bf16[16,128,128]{2,1,0:T(8,128)(2,1)S(1)}, bf16[16,128,128]{2,1,0:T(8,128)(2,1)}, u32[]{:S(2)}) copy-start(bf16[16,128,128]{2,1,0:T(8,128)(2,1)} %copy-done.2) | copy-start | bytes 1572868
  98.1 9.6 %copy-start.5 = (bf16[16,128,128]{2,1,0:T(8,128)(2,1)S(1)}, bf16[16,128,128]{2,1,0:T(8,128)(2,1)}, u32[]{:S(2)}) copy-start(bf16[16,128,128]{2,1,0:T(8,128)(2,1)} %copy-done.4) | copy-start | bytes 1572868
  98.9 8.8 %copy-start.1 = (bf16[16,128,128]{2,1,0:T(8,128)(2,1)S(1)}, bf16[16,128,128]{2,1,0:T(8,128)(2,1)}, u32[]{:S(2)}) copy-start(bf16[16,128,128]{2,1,0:T(8,128)(2,1)} %copy-done) | copy-start | bytes 1572868

commit v4 on v3

--- a/solution.py
+++ b/solution.py
@@ -12,6 +12,7 @@
 X = 4
 Z = 4
 CHIPS = X * Z
+Z_HI = 4
 W = 128
 F32 = jnp.float32
 BF16 = jnp.bfloat16
@@ -30,10 +31,8 @@
     return pl.BlockSpec(memory_space=pl.ANY)
 
 
-def passed_along(value, axis, steps):
-    count = lax.axis_size(axis)
-    leading, last = (max(0, -steps), min(count, count - steps))
-    return lax.ppermute(value, axis, [(source, source + steps) for source in range(leading, last)])
+def below(value, sources):
+    return lax.ppermute(value, "section", [(source, source - 1) for source in sources])
 
 
 def chip_exchange(parts):
@@ -60,11 +59,22 @@
     )
 
 
-def z_exchange(parts):
-    return exchange(
-        parts,
-        [[member(z, x, core) for z in range(Z)] for x in range(X) for core in range(CORES)],
+def along(value, x_steps, z_steps):
+    return lax.ppermute(
+        value,
+        "tp",
+        [
+            (member(z, x, core), member((z + z_steps) % Z, (x + x_steps) % X, core))
+            for z in range(Z)
+            for x in range(X)
+            for core in range(CORES)
+        ],
     )
+
+
+def place():
+    chip = lax.axis_index("tp") // CORES
+    return chip // X, lax.rem(chip, X)
 
 
 def sibling_swap(value):
@@ -127,52 +137,51 @@
         out[...] = sum(dot(g[chip], weight[chip], 1, 1) for chip in range(CHIPS))
 
 
-def last_pair_kernel(arrived, own, other, start, mine, theirs, total):
+def last_pair_kernel(arrived, own, other, near, far, mine, theirs, total):
     for out, weight in ((theirs, other), (mine, own)):
         out[...] = sum(dot(arrived[chip, 0], weight[chip], 1, 1) for chip in range(CHIPS))
-    total[...] = start[...].astype(F32) + sum(arrived[chip, 1].astype(F32) for chip in range(CHIPS))
-
-
-def last_pair_product(arrived, own, other, start):
+    total[...] = near[...] + far[...].astype(F32) + sum(arrived[chip, 1].astype(F32) for chip in range(CHIPS))
+
+
+def last_pair_product(arrived, own, other, near, far):
     mine, theirs, total = pl.pallas_call(
         last_pair_kernel,
         out_shape=[jax.ShapeDtypeStruct((W, W), F32)] * 3,
-        in_specs=[vmem()] * 4,
+        in_specs=[vmem()] * 5,
         out_specs=[vmem()] * 3,
         compiler_params=PARAMS,
         cost_estimate=pl.CostEstimate(flops=2 * 2 * W * W * W * CHIPS, bytes_accessed=2 << 20, transcendentals=0),
-    )(arrived, own, other, start)
+    )(arrived, own, other, near, far)
     return mine, core_pair(theirs), total
 
 
-def pair_product(gathered, own, other, after=(), held=()):
-    fixed = 3 + len(after)
-    mine, theirs, *freed = pl.pallas_call(
-        functools.partial(pair_kernel, len(after + held)),
-        out_shape=[jax.ShapeDtypeStruct((W, W), F32)] * 2
+def pair_product(gathered, own, other, after=()):
+    mine, theirs = pl.pallas_call(
+        functools.partial(pair_kernel, len(after)),
+        out_shape=[jax.ShapeDtypeStruct((W, W), F32)] * 2,
+        in_specs=[vmem()] * 3 + [anywhere()] * len(after),
+        out_specs=[vmem()] * 2,
+        compiler_params=PARAMS,
+        cost_estimate=pl.CostEstimate(flops=2 * 2 * W * W * W * CHIPS, bytes_accessed=2 << 20, transcendentals=0),
+    )(gathered, own, other, *after)
+    return mine, core_pair(theirs)
+
+
+def passed_kernel(count, grad, mine, both, *rest):
+    total = grad[...].reshape(W, W).astype(F32) + mine[...] + both[1 - core_index()]
+    rest[count][...] = total.astype(BF16)
+
+
+def passed_grad(grad, mine, both, held=()):
+    return pl.pallas_call(
+        functools.partial(passed_kernel, len(held)),
+        out_shape=[jax.ShapeDtypeStruct((W, W), BF16)]
         + [jax.ShapeDtypeStruct(x.shape, x.dtype) for x in held],
-        in_specs=[vmem()] * 3 + [anywhere()] * len(after + held),
-        out_specs=[vmem()] * 2 + [anywhere()] * len(held),
-        input_output_aliases={fixed + i: 2 + i for i in range(len(held))},
-        compiler_params=PARAMS,
-        cost_estimate=pl.CostEstimate(flops=2 * 2 * W * W * W * CHIPS, bytes_accessed=2 << 20, transcendentals=0),
-    )(gathered, own, other, *after, *held)
-    return mine, core_pair(theirs), *freed
-
-
-def passed_kernel(grad, mine, both, passed):
-    total = grad[...].reshape(W, W).astype(F32) + mine[...] + both[1 - core_index()]
-    passed[...] = total.astype(BF16)
-
-
-def passed_grad(grad, mine, both):
-    return pl.pallas_call(
-        passed_kernel,
-        out_shape=jax.ShapeDtypeStruct((W, W), BF16),
-        in_specs=[vmem()] * 3,
-        out_specs=vmem(),
-        compiler_params=PARAMS,
-    )(grad, mine, both)
+        in_specs=[vmem()] * 3 + [anywhere()] * len(held),
+        out_specs=[vmem()] + [anywhere()] * len(held),
+        input_output_aliases={3 + i: 1 + i for i in range(len(held))},
+        compiler_params=PARAMS,
+    )(grad, mine, both, *held)
 
 
 def send_to_all(value, out, sems):
@@ -295,51 +304,67 @@
     )(kv, core_pair(kv), query_grad, w_key[0], w_value[0], w_key[1], w_value[1], *after)
 
 
-def x_sum_kernel(parts, out):
-    for z in range(Z):
-        out[z] = sum(parts[x, z].astype(F32) for x in range(X)).astype(BF16)
+def x_sum_kernel(parts, *outs):
+    z, _ = place()
+    for step, out in enumerate(outs):
+        to_z = lax.rem(z + step, Z)
+        out[...] = sum(parts[x, to_z].astype(F32) for x in range(X)).astype(BF16)
 
 
 def x_sum(parts):
     return pl.pallas_call(
         x_sum_kernel,
-        out_shape=jax.ShapeDtypeStruct((Z, W, W), BF16),
+        out_shape=[jax.ShapeDtypeStruct((W, W), BF16)] * Z,
         in_specs=[vmem()],
-        out_specs=vmem(),
+        out_specs=[vmem()] * Z,
         compiler_params=PARAMS,
     )(parts)
 
 
-def z_sum_kernel(start, parts, out):
-    total = start[0] + sum(parts[z].astype(F32) for z in range(Z))
-    out[...] = total.astype(BF16)
+def z_sum_kernel(start, *rest):
+    rest[-1][...] = (start[0] + sum(part[...].astype(F32) for part in rest[:-1])).astype(BF16)
 
 
 def z_sum(start, parts):
     return pl.pallas_call(
         z_sum_kernel,
         out_shape=jax.ShapeDtypeStruct((W, W), BF16),
-        in_specs=[vmem()] * 2,
+        in_specs=[vmem()] * (1 + Z),
         out_specs=vmem(),
         compiler_params=PARAMS,
-    )(start, parts)
-
-
-def spread_kernel(x, *rest):
-    out, sems = rest[-2:]
+    )(start, *parts)
+
+
+def landed_kernel(received, *rest):
+    rest[-1][...] = received[...].astype(F32)
+
+
+def landed(received, after):
+    return pl.pallas_call(
+        landed_kernel,
+        out_shape=jax.ShapeDtypeStruct((W, W), F32),
+        in_specs=[vmem()] + [anywhere()] * len(after),
+        out_specs=vmem(),
+        compiler_params=PARAMS,
+    )(received, *after)
+
+
+def spread_kernel(count, x, *rest):
+    out, sems = rest[count], rest[-1]
     for copy in send_to_all(x, out, sems):
         copy.wait()
 
 
-def spread(x, after=()):
-    return pl.pallas_call(
-        spread_kernel,
-        out_shape=pltpu.HBM((CHIPS, W, W), BF16),
-        in_specs=[anywhere()] * (1 + len(after)),
-        out_specs=hbm(),
+def spread(x, held=()):
+    return pl.pallas_call(
+        functools.partial(spread_kernel, len(held)),
+        out_shape=[pltpu.HBM((CHIPS, W, W), BF16)] + [jax.ShapeDtypeStruct(h.shape, h.dtype) for h in held],
+        in_specs=[anywhere()] * (1 + len(held)),
+        out_specs=[hbm()] + [anywhere()] * len(held),
+        input_output_aliases={1 + i: 1 + i for i in range(len(held))},
         scratch_shapes=[pltpu.SemaphoreType.DMA((CHIPS,))],
         compiler_params=PARAMS,
-    )(x, *after)
+    )(x, *held)
 
 
 def next_kernel(slot, received, fresh, chosen):
@@ -354,7 +379,6 @@
         in_specs=[vmem()] * 2,
         out_specs=vmem(),
         compiler_params=PARAMS,
-        cost_estimate=pl.CostEstimate(flops=40_000_000_000, bytes_accessed=1 << 17, transcendentals=0),
     )(received, fresh)
 
 
@@ -371,33 +395,39 @@
     out_weight,
 ):
     slot_count = queries.shape[1]
+    sections = lax.axis_size("section")
 
     grad_slice = grad_in[0]
-    gathered = chip_exchange(spread(grad_slice))
+    gathered = chip_exchange(spread(grad_slice)[0])
     w_out, w_query = pack(pack_columns_kernel, out_weight, query_weight)
     ready = (w_query[1],)
     passed = grad_slice
     for slot in range(slot_count):
         last = slot + 1 == slot_count
-        mine, both = pair_product(gathered, *w_out, after=() if slot else ready)
+        mine, both = pair_product(gathered, *w_out, after=ready)
         query_grad, kv = attention_grads(mine, both, queries, keys, values, slot, copied=not last)
         if slot == 0:
             w_key, w_value = pack(pack_rows_kernel, key_weight, value_weight, after=(mine,))
         if last:
-            arrived = chip_exchange(last_parts(kv, query_grad, w_key, w_value, ready))
-            mine, both, carried = last_pair_product(arrived, *w_query, carried)
+            near = landed(near, after=(kv,))
+            arrived = chip_exchange(last_parts(kv, query_grad, w_key, w_value, (near,)))
+            mine, both, carried = last_pair_product(arrived, *w_query, near, far)
         else:
             all_queries = chip_exchange(query_grad)
             terms = term_parts(kv, w_key, w_value)
-            mine, both, terms = pair_product(all_queries, *w_query, held=(terms,))
-        passed = passed_grad(grad_slice, mine, both)
+            mine, both = pair_product(all_queries, *w_query, after=(terms,))
+        passed, *terms = passed_grad(grad_slice, mine, both, held=() if last else (terms,))
         if not last:
-            received = passed_along(passed, "section", -1)
-            along_z = z_exchange(x_sum(x_exchange(terms)))
+            received = below(passed, range(1, sections))
+            parts = x_sum(x_exchange(*terms))
             grad_slice = next_grad(received, fresh_grads, slot)
-            gathered = chip_exchange(spread(grad_slice, after=(along_z,)))
-            carried = passed_along(z_sum(acc_in, along_z), "section", -1)
-            ready = (carried,)
+            copies, *parts = spread(grad_slice, held=parts)
+            gathered = chip_exchange(copies)
+            moved = [parts[0]] + [along(parts[step], 0, step) for step in range(1, Z)]
+            summed = z_sum(acc_in, moved)
+            near = below(summed, [i for i in range(1, sections) if i % Z_HI])
+            far = below(summed, range(Z_HI, sections, Z_HI))
+            ready = (summed,)
     return (passed[None], carried[None])
 
 

time: 147 us -> 142 us (0.966)
  blocking collectives: 50.7 us -> 25.6 us
  starting transfers between devices: 51 us -> 69.8 us
  waiting for transfers between devices: 19 us -> 20.5 us
    all_to_all x1 -> x0, blocking collectives: 28.9 us -> none  [chip_exchange(): lax.all_to_all(parts, 'tp', split_axis=0, concat_axis=0, tiled=True, axis...]
    ppermute x2 -> x6, starting transfers between devices: 15.1 us -> 33.8 us  [the longest x3 23.4 us: below(): lax.ppermute(value, 'section', [(source, source - 1) for source in sources])]
    ppermute x2 -> x6, waiting for transfers between devices: 0.01 us -> 8.28 us  [the longest x3 5.56 us: along(): lax.ppermute(value, 'tp', [(member(z, x, core), member((z + z_steps) % Z,...]
    all_to_all x2 -> x1, waiting for transfers between devices: 4.78 us -> 0.01 us  [exchange(): lax.all_to_all(parts, 'tp', split_axis=0, concat_axis=0, tiled=True, axis...]
    all_to_all x3 -> x4, starting transfers between devices: 18.9 us -> 23.3 us  [chip_exchange(): lax.all_to_all(parts, 'tp', split_axis=0, concat_axis=0, tiled=True, axis...]
    all_to_all x2 -> x1, starting transfers between devices: 7.77 us -> 3.48 us  [exchange(): lax.all_to_all(parts, 'tp', split_axis=0, concat_axis=0, tiled=True, axis...]
    all_gather x6, blocking collectives: 21.8 us -> 25.6 us  [core_pair(): lax.all_gather(value, 'tp', axis=0, tiled=False, axis_index_groups=groups)]
    all_to_all x3 -> x4, waiting for transfers between devices: 12.3 us -> 10.4 us  [chip_exchange(): lax.all_to_all(parts, 'tp', split_axis=0, concat_axis=0, tiled=True, axis...]
  transfers between devices with their start and end apart: 11 -> 15, of which waited for: 5 -> 9; matrix products, arithmetic and copies ran while one was open for 0% -> 0% of each run, Pallas kernels for 4% -> 3%
where the time goes in v4:
time: 142 us; the launch traced here: 140 us
  starting transfers between devices  69.8 us (49%)
  blocking collectives  25.6 us (18%)
  waiting for transfers between devices  20.5 us (14%)
  Pallas kernels  14.3 us (10%)
  local copies, waits for them, and re-layouts  8.74 us (6%)
    all_gather x6, blocking collectives, core_pair(): lax.all_gather(value, 'tp', axis=0, tiled=False, axis_index_groups=groups)  25.6 us
    ppermute x3, starting transfers between devices, below(): lax.ppermute(value, 'section', [(source, source - 1) for source in sources])  23.4 us
    all_to_all x4, starting transfers between devices, chip_exchange(): lax.all_to_all(parts, 'tp', split_axis=0, concat_axis=0, tiled=True, axis...  23.3 us
    all_to_all x4, waiting for transfers between devices, chip_exchange(): lax.all_to_all(parts, 'tp', split_axis=0, concat_axis=0, tiled=True, axis...  10.4 us
    ppermute x3, starting transfers between devices, along(): lax.ppermute(value, 'tp', [(member(z, x, core), member((z + z_steps) % Z,...  10.3 us
    ppermute x4, starting transfers between devices, sibling_swap(): return lax.ppermute(value, 'tp', [(i, i ^ 1) for i in range(CHIPS * CORES)])  9.25 us
    unnamed x36, local copies, waits for them, and re-layouts  8.74 us
    ppermute x3, waiting for transfers between devices, along(): lax.ppermute(value, 'tp', [(member(z, x, core), member((z + z_steps) % Z,...  5.56 us
  transfers between devices with their start and end apart: 15, of which 9 were waited for; matrix products, arithmetic and copies ran while one was open for 0% of the time, Pallas kernels for 3%

profile of v4, /device:TPU:25, one launch (start us, length us, event | category | flops | bytes accessed | tf_op | source)
XLA Modules:
  0.0 140.0 jit_solution(7081647301205819052)
XLA Ops:
  0.6 0.0 copy-start.13
  0.6 0.7 copy-done.13
  1.4 0.9 shard_map.113
  2.3 8.2 %all-to-all-start = ((bf16[16,128,128]{2,1,0:T(8,128)(2,1)}), bf16[16,128,128]{2,1,0:T(8,128)(2,1)S(1)}, u32[]{:S(2)}, u32[]{:S(2)}) async-start(bf16[16,128,128]{2,1,0:T(8,128)(2,1)} %shard_map.113), calls=%async_computation | async-start | bytes 1048576 | tf_op jit(solution)/shard_map/all_to_all | solution.py:40
  10.5 0.0 copy-start.6
  10.6 1.2 copy-done.6
  11.8 1.2 copy-done.7
  13.0 0.5 shard_map.114
  13.5 2.9 %collective-permute-start = (bf16[16,128,128]{2,1,0:T(8,128)(2,1)S(1)}, bf16[16,128,128]{2,1,0:T(8,128)(2,1)S(1)}, u32[]{:S(2)}, u32[]{:S(2)}) collective-permute-start(bf16[16,128,128]{2,1,0:T(8,128)(2,1)S(1)} %get-tuple-element.35), channel_id=1, source_target_pairs={{0,1},{1,0},{2,3},{3,2},{4,5},{5,4},{6,7},{7,6},{8,9},{9,8},{10,11... | collective-permute-start | bytes 1572872 | tf_op jit(solution)/shard_map/ppermute | solution.py:81
  16.4 1.9 %collective-permute-start.1 = (bf16[16,128,128]{2,1,0:T(8,128)(2,1)S(1)}, bf16[16,128,128]{2,1,0:T(8,128)(2,1)S(1)}, u32[]{:S(2)}, u32[]{:S(2)}) collective-permute-start(bf16[16,128,128]{2,1,0:T(8,128)(2,1)S(1)} %get-tuple-element.36), channel_id=1, source_target_pairs={{0,1},{1,0},{2,3},{3,2},{4,5},{5,4},{6,7},{7,6},{8,9},{9,8},{10,11... | collective-permute-start | bytes 1572872 | tf_op jit(solution)/shard_map/ppermute | solution.py:81
  18.3 0.0 collective-permute-done.other
  18.4 1.9 %collective-permute-done.1.rest_0_.other = bf16[16,128,128]{2,1,0:T(8,128)(2,1)S(1)} collective-permute-done((bf16[16,128,128]{2,1,0:T(8,128)(2,1)S(1)}, bf16[16,128,128]{2,1,0:T(8,128)(2,1)S(1)}, u32[]{:S(2)}, u32[]{:S(2)}) %collective-permute-start.1) | collective-permute-done | bytes 524320 | tf_op jit(solution)/shard_map/ppermute | solution.py:81
  20.2 4.1 %all-to-all-done.g = bf16[16,128,128]{2,1,0:T(8,128)(2,1)S(1)} async-done(((bf16[16,128,128]{2,1,0:T(8,128)(2,1)}), bf16[16,128,128]{2,1,0:T(8,128)(2,1)S(1)}, u32[]{:S(2)}, u32[]{:S(2)}) %all-to-all-start) | async-done | bytes 524320 | tf_op jit(solution)/shard_map/all_to_all | solution.py:40
  24.3 0.8 shard_map.115
  25.1 0.0 copy-start.10
  25.2 0.0 copy-start.11
  25.2 0.0 copy-start.12
  25.2 4.3 %all-gather = f32[256,128]{1,0:T(8,128)S(1)} all-gather(f32[128,128]{1,0:T(8,128)S(1)} %get-tuple-element.38), channel_id=2, replica_groups={{0,1},{2,3},{4,5},{6,7},{8,9},{10,11},{12,13},{14,15},{16,17},{18,19},{..., dimensions={0}, use_global_device_ids=true | all-gather | bytes 196608 | tf_op jit(solution)/shard_map/all_gather | solution.py:86
  29.5 1.6 %shard_map.116 = (bf16[16,128,128]{2,1,0:T(8,128)(2,1)}, bf16[128,256]{1,0:T(8,128)(2,1)S(1)}) custom-call(f32[128,128]{1,0:T(8,128)S(1)} %get-tuple-element.37.mine.rest_0_, f32[2,128,128]{2,1,0:T(8,128)S(1)} %bitcast.11, bf16[1,2,128,128]{3,2,1,0:T(8,128)(2,1)S(1)} %copy-done.10, bf16[1,2,128,128]{3,2,1,0:T(8,128)(2,1)S(1)} %copy-done.11, ...), custom_call_target="tpu_custom_call" | custom-call | flops 41943040 | bytes 1048576 | tf_op jit(solution)/shard_map/pallas_call | solution.py:232
  31.1 4.2 %all-to-all-start.1 = ((bf16[16,128,128]{2,1,0:T(8,128)(2,1)}), bf16[16,128,128]{2,1,0:T(8,128)(2,1)S(1)}, u32[]{:S(2)}, u32[]{:S(2)}) async-start(bf16[16,128,128]{2,1,0:T(8,128)(2,1)} %get-tuple-element.39), calls=%async_computation.1 | async-start | bytes 1048576 | tf_op jit(solution)/shard_map/all_to_all | solution.py:40
  35.2 0.0 copy-start.8
  35.3 1.2 copy-done.8
  36.5 1.2 copy-done.9
  37.7 0.1 shard_map.117
  37.8 2.5 %collective-permute-start.2 = (bf16[16,128,128]{2,1,0:T(8,128)(2,1)S(1)}, bf16[16,128,128]{2,1,0:T(8,128)(2,1)S(1)}, u32[]{:S(2)}, u32[]{:S(2)}) collective-permute-start(bf16[16,128,128]{2,1,0:T(8,128)(2,1)S(1)} %get-tuple-element.44), channel_id=1, source_target_pairs={{0,1},{1,0},{2,3},{3,2},{4,5},{5,4},{6,7},{7,6},{8,9},{9,8},{10,11... | collective-permute-start | bytes 1572872 | tf_op jit(solution)/shard_map/ppermute | solution.py:81
  40.4 1.9 %collective-permute-start.3 = (bf16[16,128,128]{2,1,0:T(8,128)(2,1)S(1)}, bf16[16,128,128]{2,1,0:T(8,128)(2,1)S(1)}, u32[]{:S(2)}, u32[]{:S(2)}) collective-permute-start(bf16[16,128,128]{2,1,0:T(8,128)(2,1)S(1)} %get-tuple-element.45), channel_id=1, source_target_pairs={{0,1},{1,0},{2,3},{3,2},{4,5},{5,4},{6,7},{7,6},{8,9},{9,8},{10,11... | collective-permute-start | bytes 1572872 | tf_op jit(solution)/shard_map/ppermute | solution.py:81
  42.3 2.0 %all-gather.1 = bf16[256,256]{1,0:T(8,128)(2,1)S(1)} all-gather(bf16[128,256]{1,0:T(8,128)(2,1)S(1)} %get-tuple-element.41.kv), channel_id=3, replica_groups={{0,1},{2,3},{4,5},{6,7},{8,9},{10,11},{12,13},{14,15},{16,17},{18,19},{..., dimensions={0}, use_global_device_ids=true | all-gather | bytes 196608 | tf_op jit(solution)/shard_map/all_gather | solution.py:86
  44.4 0.0 collective-permute-done.2.rk
  44.4 2.4 %shard_map.118.rest_0_ = bf16[4,4,128,128]{3,2,1,0:T(8,128)(2,1)} custom-call(bf16[128,256]{1,0:T(8,128)(2,1)S(1)} %get-tuple-element.41.kv, bf16[2,128,256]{2,1,0:T(8,128)(2,1)S(1)} %bitcast.9, bf16[16,128,128]{2,1,0:T(8,128)(2,1)S(1)} %get-tuple-element.42.ok, bf16[16,128,128]{2,1,0:T(8,128)(2,1)S(1)} %get-tuple-element.43.ov, ...), custom_call_target="tpu_custom_call" | custom-call | flops 268435456 | bytes 3145728 | tf_op jit(solution)/shard_map/pallas_call | solution.py:281
  46.7 0.8 copy-done
  47.5 0.8 copy-done.2
  48.4 0.8 copy-done.4
  49.2 0.2 all-to-all-done.1.g
  49.4 0.8 shard_map.119
  50.2 0.0 copy-start.14
  50.2 3.8 %all-gather.2 = f32[256,128]{1,0:T(8,128)S(1)} all-gather(f32[128,128]{1,0:T(8,128)S(1)} %get-tuple-element.47), channel_id=4, replica_groups={{0,1},{2,3},{4,5},{6,7},{8,9},{10,11},{12,13},{14,15},{16,17},{18,19},{..., dimensions={0}, use_global_device_ids=true | all-gather | bytes 196608 | tf_op jit(solution)/shard_map/all_gather | solution.py:86
  54.0 0.0 copy-start.16
  54.0 3.5 %all-to-all-start.2 = ((bf16[4,4,128,128]{3,2,1,0:T(8,128)(2,1)}), bf16[4,4,128,128]{3,2,1,0:T(8,128)(2,1)S(1)}, u32[]{:S(2)}, u32[]{:S(2)}) async-start(bf16[4,4,128,128]{3,2,1,0:T(8,128)(2,1)} %get-tuple-element.49), calls=%async_computation.2 | async-start | bytes 1048576 | tf_op jit(solution)/shard_map/all_to_all | solution.py:50
  57.5 9.9 %collective-permute-start.4 = (bf16[128,128]{1,0:T(8,128)(2,1)S(1)}, bf16[128,128]{1,0:T(8,128)(2,1)S(1)}, u32[]{:S(2)}, u32[]{:S(2)}) collective-permute-start(bf16[128,128]{1,0:T(8,128)(2,1)S(1)} %get-tuple-element.48), channel_id=1, source_target_pairs={{32,0},{64,32},{96,64},{128,96},{160,128},{192,160},{224,192},{256... | collective-permute-start | bytes 98312 | tf_op jit(solution)/shard_map/ppermute | solution.py:35
  67.4 1.0 collective-permute-done.4.received
  68.5 0.1 shard_map.122
  68.6 1.0 shard_map.123
  69.6 0.0 copy-start.17
  69.6 0.6 copy-done.17
  70.2 6.1 %all-to-all-start.3 = ((bf16[16,128,128]{2,1,0:T(8,128)(2,1)}), bf16[16,128,128]{2,1,0:T(8,128)(2,1)S(1)}, u32[]{:S(2)}, u32[]{:S(2)}) async-start(bf16[16,128,128]{2,1,0:T(8,128)(2,1)} %get-tuple-element.54), calls=%async_computation.3 | async-start | bytes 1048576 | tf_op jit(solution)/shard_map/all_to_all | solution.py:40
  76.2 3.3 %collective-permute-start.5 = (bf16[128,128]{1,0:T(8,128)(2,1)S(1)}, bf16[128,128]{1,0:T(8,128)(2,1)S(1)}, u32[]{:S(2)}, u32[]{:S(2)}) collective-permute-start(bf16[128,128]{1,0:T(8,128)(2,1)S(1)} %get-tuple-element.56), channel_id=1, source_target_pairs={{0,8},{1,9},{2,10},{3,11},{4,12},{5,13},{6,14},{7,15},{8,16},{9,17... | collective-permute-start | bytes 98312 | tf_op jit(solution)/shard_map/ppermute | solution.py:63
  79.5 4.0 %collective-permute-start.6 = (bf16[128,128]{1,0:T(8,128)(2,1)S(1)}, bf16[128,128]{1,0:T(8,128)(2,1)S(1)}, u32[]{:S(2)}, u32[]{:S(2)}) collective-permute-start(bf16[128,128]{1,0:T(8,128)(2,1)S(1)} %get-tuple-element.57), channel_id=1, source_target_pairs={{0,16},{1,17},{2,18},{3,19},{4,20},{5,21},{6,22},{7,23},{8,24},{9,... | collective-permute-start | bytes 98312 | tf_op jit(solution)/shard_map/ppermute | solution.py:63
  83.5 3.1 %collective-permute-start.7 = (bf16[128,128]{1,0:T(8,128)(2,1)}, bf16[128,128]{1,0:T(8,128)(2,1)S(1)}, u32[]{:S(2)}, u32[]{:S(2)}) collective-permute-start(bf16[128,128]{1,0:T(8,128)(2,1)} %copy-done.17), channel_id=1, source_target_pairs={{0,24},{1,25},{2,26},{3,27},{4,28},{5,29},{6,30},{7,31},{8,0},{9,1... | collective-permute-start | bytes 98312 | tf_op jit(solution)/shard_map/ppermute | solution.py:63
  86.6 1.0 collective-permute-done.5.rest_1_
  87.6 4.6 %collective-permute-done.6.rest_2_ = bf16[128,128]{1,0:T(8,128)(2,1)S(1)} collective-permute-done((bf16[128,128]{1,0:T(8,128)(2,1)S(1)}, bf16[128,128]{1,0:T(8,128)(2,1)S(1)}, u32[]{:S(2)}, u32[]{:S(2)}) %collective-permute-start.6) | collective-permute-done | bytes 32800 | tf_op jit(solution)/shard_map/ppermute | solution.py:63
  92.2 1.3 collective-permute-start.8
  93.5 0.8 shard_map.125
  94.4 3.6 %all-gather.3 = f32[256,128]{1,0:T(8,128)S(1)} all-gather(f32[128,128]{1,0:T(8,128)S(1)} %get-tuple-element.60), channel_id=5, replica_groups={{0,1},{2,3},{4,5},{6,7},{8,9},{10,11},{12,13},{14,15},{16,17},{18,19},{..., dimensions={0}, use_global_device_ids=true | all-gather | bytes 196608 | tf_op jit(solution)/shard_map/all_gather | solution.py:86
  98.0 0.7 shard_map.126
  98.6 1.9 %all-gather.4 = bf16[256,256]{1,0:T(8,128)(2,1)S(1)} all-gather(bf16[128,256]{1,0:T(8,128)(2,1)S(1)} %get-tuple-element.61.rest_0_.kv), channel_id=6, replica_groups={{0,1},{2,3},{4,5},{6,7},{8,9},{10,11},{12,13},{14,15},{16,17},{18,19},{..., dimensions={0}, use_global_device_ids=true | all-gather | bytes 196608 | tf_op jit(solution)/shard_map/all_gather | solution.py:86
  100.5 0.7 collective-permute-done.8.received
  101.3 2.5 %shard_map.128 = bf16[16,2,128,128]{3,2,1,0:T(8,128)(2,1)} custom-call(bf16[128,256]{1,0:T(8,128)(2,1)S(1)} %get-tuple-element.61.rest_0_.kv, bf16[2,128,256]{2,1,0:T(8,128)(2,1)S(1)} %bitcast.14, bf16[128,128]{1,0:T(8,128)(2,1)S(1)} %get-tuple-element.62.query_grad, bf16[16,128,128]{2,1,0:T(8,128)(2,1)S(1)} %get-tuple-element.42.ok, ...), custom_call_target="tpu_custom_call" | custom-call | flops 268435456 | bytes 3145728 | tf_op jit(solution)/shard_map/pallas_call | solution.py:292
  103.8 4.9 %all-to-all-start.4 = ((bf16[16,2,128,128]{3,2,1,0:T(8,128)(2,1)}), bf16[16,2,128,128]{3,2,1,0:T(8,128)(2,1)S(1)}, u32[]{:S(2)}, u32[]{:S(2)}) async-start(bf16[16,2,128,128]{3,2,1,0:T(8,128)(2,1)} %shard_map.128), calls=%async_computation.4 | async-start | bytes 2097152 | tf_op jit(solution)/shard_map/all_to_all | solution.py:40
  108.7 12.2 %collective-permute-start.9 = (bf16[128,128]{1,0:T(8,128)(2,1)S(1)}, bf16[128,128]{1,0:T(8,128)(2,1)S(1)}, u32[]{:S(2)}, u32[]{:S(2)}) collective-permute-start(bf16[128,128]{1,0:T(8,128)(2,1)S(1)} %shard_map.124.rest_0_), channel_id=1, source_target_pairs={{128,96},{256,224},{384,352},{129,97},{257,225},{385,353},{130,98}... | collective-permute-start | bytes 98312 | tf_op jit(solution)/shard_map/ppermute | solution.py:35
  120.9 1.0 collective-permute-done.9.far
  121.9 6.1 %all-to-all-done.4.arrived = bf16[16,2,128,128]{3,2,1,0:T(8,128)(2,1)S(1)} async-done(((bf16[16,2,128,128]{3,2,1,0:T(8,128)(2,1)}), bf16[16,2,128,128]{3,2,1,0:T(8,128)(2,1)S(1)}, u32[]{:S(2)}, u32[]{:S(2)}) %all-to-all-start.4) | async-done | bytes 1048608 | tf_op jit(solution)/shard_map/all_to_all | solution.py:40
  128.0 1.4 %shard_map.129 = (f32[128,128]{1,0:T(8,128)S(1)}, f32[128,128]{1,0:T(8,128)S(1)}, f32[128,128]{1,0:T(8,128)}) custom-call(bf16[16,2,128,128]{3,2,1,0:T(8,128)(2,1)S(1)} %all-to-all-done.4.arrived, bf16[16,128,128]{2,1,0:T(8,128)(2,1)S(1)} %get-tuple-element.40.own, bf16[16,128,128]{2,1,0:T(8,128)(2,1)S(1)} %collective-permute-done.1.rest_0_.other, ...), custom_call_target="tpu_custom_call" | custom-call | flops 134217728 | bytes 2097152 | tf_op jit(solution)/shard_map/pallas_call | solution.py:147
  129.4 10.0 %all-gather.5 = f32[256,128]{1,0:T(8,128)S(1)} all-gather(f32[128,128]{1,0:T(8,128)S(1)} %get-tuple-element.64), channel_id=7, replica_groups={{0,1},{2,3},{4,5},{6,7},{8,9},{10,11},{12,13},{14,15},{16,17},{18,19},{..., dimensions={0}, use_global_device_ids=true | all-gather | bytes 196608 | tf_op jit(solution)/shard_map/all_gather | solution.py:86
  139.3 0.6 shard_map.130
  (26 shorter events, 0.1 us)
Async XLA Ops:
  0.6 0.8 copy-start.13
  2.3 22.0 %all-to-all-start = ((bf16[16,128,128]{2,1,0:T(8,128)(2,1)}), bf16[16,128,128]{2,1,0:T(8,128)(2,1)S(1)}, u32[]{:S(2)}, u32[]{:S(2)}) async-start(bf16[16,128,128]{2,1,0:T(8,128)(2,1)} %shard_map.113), calls=%async_computation | async-start | bytes 1048576 | tf_op jit(solution)/shard_map/all_to_all | solution.py:40
  10.5 1.2 copy-start.6
  11.8 1.2 copy-start.7
  13.5 4.8 %collective-permute-start = (bf16[16,128,128]{2,1,0:T(8,128)(2,1)S(1)}, bf16[16,128,128]{2,1,0:T(8,128)(2,1)S(1)}, u32[]{:S(2)}, u32[]{:S(2)}) collective-permute-start(bf16[16,128,128]{2,1,0:T(8,128)(2,1)S(1)} %get-tuple-element.35), channel_id=1, source_target_pairs={{0,1},{1,0},{2,3},{3,2},{4,5},{5,4},{6,7},{7,6},{8,9},{9,8},{10,11... | collective-permute-start | bytes 1572872 | tf_op jit(solution)/shard_map/ppermute | solution.py:81
  16.4 3.8 %collective-permute-start.1 = (bf16[16,128,128]{2,1,0:T(8,128)(2,1)S(1)}, bf16[16,128,128]{2,1,0:T(8,128)(2,1)S(1)}, u32[]{:S(2)}, u32[]{:S(2)}) collective-permute-start(bf16[16,128,128]{2,1,0:T(8,128)(2,1)S(1)} %get-tuple-element.36), channel_id=1, source_target_pairs={{0,1},{1,0},{2,3},{3,2},{4,5},{5,4},{6,7},{7,6},{8,9},{9,8},{10,11... | collective-permute-start | bytes 1572872 | tf_op jit(solution)/shard_map/ppermute | solution.py:81
  25.1 4.3 %copy-start.10 = (bf16[1,2,128,128]{3,2,1,0:T(8,128)(2,1)S(1)}, bf16[1,2,128,128]{3,2,1,0:T(8,128)(2,1)}, u32[]{:S(2)}) copy-start(bf16[1,2,128,128]{3,2,1,0:T(8,128)(2,1)} %queries.3) | copy-start | bytes 196612
  25.2 4.3 %copy-start.11 = (bf16[1,2,128,128]{3,2,1,0:T(8,128)(2,1)S(1)}, bf16[1,2,128,128]{3,2,1,0:T(8,128)(2,1)}, u32[]{:S(2)}) copy-start(bf16[1,2,128,128]{3,2,1,0:T(8,128)(2,1)} %keys.3) | copy-start | bytes 196612
  25.2 4.3 %copy-start.12 = (bf16[1,2,128,128]{3,2,1,0:T(8,128)(2,1)S(1)}, bf16[1,2,128,128]{3,2,1,0:T(8,128)(2,1)}, u32[]{:S(2)}) copy-start(bf16[1,2,128,128]{3,2,1,0:T(8,128)(2,1)} %values.3) | copy-start | bytes 196612
  31.1 18.3 %all-to-all-start.1 = ((bf16[16,128,128]{2,1,0:T(8,128)(2,1)}), bf16[16,128,128]{2,1,0:T(8,128)(2,1)S(1)}, u32[]{:S(2)}, u32[]{:S(2)}) async-start(bf16[16,128,128]{2,1,0:T(8,128)(2,1)} %get-tuple-element.39), calls=%async_computation.1 | async-start | bytes 1048576 | tf_op jit(solution)/shard_map/all_to_all | solution.py:40
  35.2 1.2 copy-start.8
  36.5 1.2 copy-start.9
  37.8 6.5 %collective-permute-start.2 = (bf16[16,128,128]{2,1,0:T(8,128)(2,1)S(1)}, bf16[16,128,128]{2,1,0:T(8,128)(2,1)S(1)}, u32[]{:S(2)}, u32[]{:S(2)}) collective-permute-start(bf16[16,128,128]{2,1,0:T(8,128)(2,1)S(1)} %get-tuple-element.44), channel_id=1, source_target_pairs={{0,1},{1,0},{2,3},{3,2},{4,5},{5,4},{6,7},{7,6},{8,9},{9,8},{10,11... | collective-permute-start | bytes 1572872 | tf_op jit(solution)/shard_map/ppermute | solution.py:81
  40.4 4.0 %collective-permute-start.3 = (bf16[16,128,128]{2,1,0:T(8,128)(2,1)S(1)}, bf16[16,128,128]{2,1,0:T(8,128)(2,1)S(1)}, u32[]{:S(2)}, u32[]{:S(2)}) collective-permute-start(bf16[16,128,128]{2,1,0:T(8,128)(2,1)S(1)} %get-tuple-element.45), channel_id=1, source_target_pairs={{0,1},{1,0},{2,3},{3,2},{4,5},{5,4},{6,7},{7,6},{8,9},{9,8},{10,11... | collective-permute-start | bytes 1572872 | tf_op jit(solution)/shard_map/ppermute | solution.py:81
  46.7 0.8 copy-start
  47.5 0.8 copy-start.2
  48.4 0.8 copy-start.4
  50.2 3.8 %copy-start.14 = (bf16[1,128,128]{2,1,0:T(8,128)(2,1)S(1)}, bf16[1,128,128]{2,1,0:T(8,128)(2,1)}, u32[]{:S(2)}) copy-start(bf16[1,128,128]{2,1,0:T(8,128)(2,1)} %param.10) | copy-start | bytes 98308
  54.0 14.5 %copy-start.16 = (bf16[1,128,128]{2,1,0:T(8,128)(2,1)S(1)}, bf16[1,128,128]{2,1,0:T(8,128)(2,1)}, u32[]{:S(2)}) copy-start(bf16[1,128,128]{2,1,0:T(8,128)(2,1)} %fresh.1) | copy-start | bytes 98308
  54.0 14.5 %all-to-all-start.2 = ((bf16[4,4,128,128]{3,2,1,0:T(8,128)(2,1)}), bf16[4,4,128,128]{3,2,1,0:T(8,128)(2,1)S(1)}, u32[]{:S(2)}, u32[]{:S(2)}) async-start(bf16[4,4,128,128]{3,2,1,0:T(8,128)(2,1)} %get-tuple-element.49), calls=%async_computation.2 | async-start | bytes 1048576 | tf_op jit(solution)/shard_map/all_to_all | solution.py:50
  57.5 11.0 %collective-permute-start.4 = (bf16[128,128]{1,0:T(8,128)(2,1)S(1)}, bf16[128,128]{1,0:T(8,128)(2,1)S(1)}, u32[]{:S(2)}, u32[]{:S(2)}) collective-permute-start(bf16[128,128]{1,0:T(8,128)(2,1)S(1)} %get-tuple-element.48), channel_id=1, source_target_pairs={{32,0},{64,32},{96,64},{128,96},{160,128},{192,160},{224,192},{256... | collective-permute-start | bytes 98312 | tf_op jit(solution)/shard_map/ppermute | solution.py:35
  69.6 0.6 copy-start.17
  70.2 22.0 %copy-start.15 = (f32[1,128,128]{2,1,0:T(8,128)S(1)}, f32[1,128,128]{2,1,0:T(8,128)}, u32[]{:S(2)}) copy-start(f32[1,128,128]{2,1,0:T(8,128)} %start.1) | copy-start | bytes 196612
  70.2 23.3 %all-to-all-start.3 = ((bf16[16,128,128]{2,1,0:T(8,128)(2,1)}), bf16[16,128,128]{2,1,0:T(8,128)(2,1)S(1)}, u32[]{:S(2)}, u32[]{:S(2)}) async-start(bf16[16,128,128]{2,1,0:T(8,128)(2,1)} %get-tuple-element.54), calls=%async_computation.3 | async-start | bytes 1048576 | tf_op jit(solution)/shard_map/all_to_all | solution.py:40
  76.2 11.3 %collective-permute-start.5 = (bf16[128,128]{1,0:T(8,128)(2,1)S(1)}, bf16[128,128]{1,0:T(8,128)(2,1)S(1)}, u32[]{:S(2)}, u32[]{:S(2)}) collective-permute-start(bf16[128,128]{1,0:T(8,128)(2,1)S(1)} %get-tuple-element.56), channel_id=1, source_target_pairs={{0,8},{1,9},{2,10},{3,11},{4,12},{5,13},{6,14},{7,15},{8,16},{9,17... | collective-permute-start | bytes 98312 | tf_op jit(solution)/shard_map/ppermute | solution.py:63
  79.5 12.7 %collective-permute-start.6 = (bf16[128,128]{1,0:T(8,128)(2,1)S(1)}, bf16[128,128]{1,0:T(8,128)(2,1)S(1)}, u32[]{:S(2)}, u32[]{:S(2)}) collective-permute-start(bf16[128,128]{1,0:T(8,128)(2,1)S(1)} %get-tuple-element.57), channel_id=1, source_target_pairs={{0,16},{1,17},{2,18},{3,19},{4,20},{5,21},{6,22},{7,23},{8,24},{9,... | collective-permute-start | bytes 98312 | tf_op jit(solution)/shard_map/ppermute | solution.py:63
  83.5 8.7 %collective-permute-start.7 = (bf16[128,128]{1,0:T(8,128)(2,1)}, bf16[128,128]{1,0:T(8,128)(2,1)S(1)}, u32[]{:S(2)}, u32[]{:S(2)}) collective-permute-start(bf16[128,128]{1,0:T(8,128)(2,1)} %copy-done.17), channel_id=1, source_target_pairs={{0,24},{1,25},{2,26},{3,27},{4,28},{5,29},{6,30},{7,31},{8,0},{9,1... | collective-permute-start | bytes 98312 | tf_op jit(solution)/shard_map/ppermute | solution.py:63
  92.2 9.1 %collective-permute-start.8 = (bf16[128,128]{1,0:T(8,128)(2,1)S(1)}, bf16[128,128]{1,0:T(8,128)(2,1)S(1)}, u32[]{:S(2)}, u32[]{:S(2)}) collective-permute-start(bf16[128,128]{1,0:T(8,128)(2,1)S(1)} %shard_map.124.rest_0_), channel_id=1, source_target_pairs={{32,0},{64,32},{96,64},{160,128},{192,160},{224,192},{288,256},{32... | collective-permute-start | bytes 98312 | tf_op jit(solution)/shard_map/ppermute | solution.py:35
  93.5 7.8 %copy-start.3 = (bf16[16,128,128]{2,1,0:T(8,128)(2,1)S(1)}, bf16[16,128,128]{2,1,0:T(8,128)(2,1)}, u32[]{:S(2)}) copy-start(bf16[16,128,128]{2,1,0:T(8,128)(2,1)} %copy-done.2) | copy-start | bytes 1572868
  93.5 7.7 %copy-start.5 = (bf16[16,128,128]{2,1,0:T(8,128)(2,1)S(1)}, bf16[16,128,128]{2,1,0:T(8,128)(2,1)}, u32[]{:S(2)}) copy-start(bf16[16,128,128]{2,1,0:T(8,128)(2,1)} %copy-done.4) | copy-start | bytes 1572868
  94.4 6.9 %copy-start.1 = (bf16[16,128,128]{2,1,0:T(8,128)(2,1)S(1)}, bf16[16,128,128]{2,1,0:T(8,128)(2,1)}, u32[]{:S(2)}) copy-start(bf16[16,128,128]{2,1,0:T(8,128)(2,1)} %copy-done) | copy-start | bytes 1572868
  103.8 24.2 %all-to-all-start.4 = ((bf16[16,2,128,128]{3,2,1,0:T(8,128)(2,1)}), bf16[16,2,128,128]{3,2,1,0:T(8,128)(2,1)S(1)}, u32[]{:S(2)}, u32[]{:S(2)}) async-start(bf16[16,2,128,128]{3,2,1,0:T(8,128)(2,1)} %shard_map.128), calls=%async_computation.4 | async-start | bytes 2097152 | tf_op jit(solution)/shard_map/all_to_all | solution.py:40
  108.7 13.2 %collective-permute-start.9 = (bf16[128,128]{1,0:T(8,128)(2,1)S(1)}, bf16[128,128]{1,0:T(8,128)(2,1)S(1)}, u32[]{:S(2)}, u32[]{:S(2)}) collective-permute-start(bf16[128,128]{1,0:T(8,128)(2,1)S(1)} %shard_map.124.rest_0_), channel_id=1, source_target_pairs={{128,96},{256,224},{384,352},{129,97},{257,225},{385,353},{130,98}... | collective-permute-start | bytes 98312 | tf_op jit(solution)/shard_map/ppermute | solution.py:35

commit v5 on v4

--- a/solution.py
+++ b/solution.py
@@ -16,7 +16,7 @@
 W = 128
 F32 = jnp.float32
 BF16 = jnp.bfloat16
-PARAMS = pltpu.CompilerParams(vmem_limit_bytes=24 * 1024 * 1024)
+PARAMS = pltpu.CompilerParams(vmem_limit_bytes=12 * 1024 * 1024)
 
 
 def vmem():
@@ -25,6 +25,10 @@
 
 def hbm():
     return pl.BlockSpec(memory_space=pltpu.HBM)
+
+
+def in_hbm(x):
+    return pltpu.with_memory_space_constraint(x, pltpu.HBM)
 
 
 def anywhere():
@@ -102,44 +106,62 @@
         yield chip, own, other
 
 
-def pack_columns_kernel(a, b, own_a, own_b, other_a, other_b):
+def pack_columns_kernel(a, b, grad, own_a, own_b, other_a, other_b, grad_out):
     for chip, own, other in halves():
-        other_a[chip] = a[0, :, other]
-        other_b[chip] = b[0, :, other]
-        own_a[chip] = a[0, :, own]
-        own_b[chip] = b[0, :, own]
+        there = slice(chip * W, (chip + 1) * W)
+        other_a[:, there] = a[0, :, other]
+        other_b[:, there] = b[0, :, other]
+        own_a[:, there] = a[0, :, own]
+        own_b[:, there] = b[0, :, own]
+    grad_out[...] = grad[0]
+
+
+def pack_columns(a, b, grad):
+    own_a, own_b, other_a, other_b, grad = pl.pallas_call(
+        pack_columns_kernel,
+        out_shape=[jax.ShapeDtypeStruct((W, CHIPS * W), BF16)] * 4 + [jax.ShapeDtypeStruct((W, W), BF16)],
+        in_specs=[vmem()] * 3,
+        out_specs=[vmem()] * 5,
+        compiler_params=PARAMS,
+        cost_estimate=pl.CostEstimate(flops=0, bytes_accessed=4 << 20, transcendentals=0),
+    )(a, b, grad)
+    return (own_a, sibling_swap(other_a)), (own_b, sibling_swap(other_b)), grad
 
 
 def pack_rows_kernel(a, b, *rest):
-    own_a, own_b, other_a, other_b = rest[-4:]
+    own_ab, other_ab = rest[-2:]
     for chip, own, other in halves():
-        other_a[chip] = a[0, other, :]
-        other_b[chip] = b[0, other, :]
-        own_a[chip] = a[0, own, :]
-        own_b[chip] = b[0, own, :]
-
-
-def pack(kernel, a, b, after=()):
-    own_a, own_b, other_a, other_b = pl.pallas_call(
-        kernel,
-        out_shape=[jax.ShapeDtypeStruct((CHIPS, W, W), BF16)] * 4,
+        other_ab[chip, :, :W] = a[0, other, :]
+        other_ab[chip, :, W:] = b[0, other, :]
+        own_ab[chip, :, :W] = a[0, own, :]
+        own_ab[chip, :, W:] = b[0, own, :]
+
+
+def pack_rows(a, b, after):
+    own, other = pl.pallas_call(
+        pack_rows_kernel,
+        out_shape=[jax.ShapeDtypeStruct((CHIPS, W, 2 * W), BF16)] * 2,
         in_specs=[vmem()] * 2 + [anywhere()] * len(after),
-        out_specs=[vmem()] * 4,
+        out_specs=[vmem()] * 2,
         compiler_params=PARAMS,
         cost_estimate=pl.CostEstimate(flops=0, bytes_accessed=4 << 20, transcendentals=0),
     )(a, b, *after)
-    return (own_a, sibling_swap(other_a)), (own_b, sibling_swap(other_b))
+    return own, sibling_swap(other)
 
 
 def pair_kernel(after, g, own, other, *rest):
-    mine, theirs = rest[after:][:2]
-    for out, weight in ((theirs, other), (mine, own)):
-        out[...] = sum(dot(g[chip], weight[chip], 1, 1) for chip in range(CHIPS))
-
-
-def last_pair_kernel(arrived, own, other, near, far, mine, theirs, total):
-    for out, weight in ((theirs, other), (mine, own)):
-        out[...] = sum(dot(arrived[chip, 0], weight[chip], 1, 1) for chip in range(CHIPS))
+    mine, theirs, joined = rest[after:]
+    for chip in range(CHIPS):
+        joined[:, chip * W : (chip + 1) * W] = g[chip]
+    theirs[...] = dot(joined[...], other[...], 1, 1)
+    mine[...] = dot(joined[...], own[...], 1, 1)
+
+
+def last_pair_kernel(arrived, own, other, near, far, mine, theirs, total, joined):
+    for chip in range(CHIPS):
+        joined[:, chip * W : (chip + 1) * W] = arrived[chip, 0]
+    theirs[...] = dot(joined[...], other[...], 1, 1)
+    mine[...] = dot(joined[...], own[...], 1, 1)
     total[...] = near[...] + far[...].astype(F32) + sum(arrived[chip, 1].astype(F32) for chip in range(CHIPS))
 
 
@@ -149,6 +171,7 @@
         out_shape=[jax.ShapeDtypeStruct((W, W), F32)] * 3,
         in_specs=[vmem()] * 5,
         out_specs=[vmem()] * 3,
+        scratch_shapes=[pltpu.VMEM((W, CHIPS * W), BF16)],
         compiler_params=PARAMS,
         cost_estimate=pl.CostEstimate(flops=2 * 2 * W * W * W * CHIPS, bytes_accessed=2 << 20, transcendentals=0),
     )(arrived, own, other, near, far)
@@ -161,6 +184,7 @@
         out_shape=[jax.ShapeDtypeStruct((W, W), F32)] * 2,
         in_specs=[vmem()] * 3 + [anywhere()] * len(after),
         out_specs=[vmem()] * 2,
+        scratch_shapes=[pltpu.VMEM((W, CHIPS * W), BF16)],
         compiler_params=PARAMS,
         cost_estimate=pl.CostEstimate(flops=2 * 2 * W * W * W * CHIPS, bytes_accessed=2 << 20, transcendentals=0),
     )(gathered, own, other, *after)
@@ -243,21 +267,17 @@
     )(mine, both, queries, keys, values)
 
 
-def term_of(chip, own, other, ok, ov, rk, rv):
-    total = dot(own[:, :W], ok[chip], 1, 1)
-    total += dot(own[:, W:], ov[chip], 1, 1)
-    total += dot(other[:, :W], rk[chip], 1, 1)
-    total += dot(other[:, W:], rv[chip], 1, 1)
-    return total.astype(BF16)
-
-
-def term_kernel(kv, both, ok, ov, rk, rv, out):
+def term_of(chip, own, other, own_weight, other_weight):
+    return (dot(own, own_weight[chip], 1, 1) + dot(other, other_weight[chip], 1, 1)).astype(BF16)
+
+
+def term_kernel(kv, both, own_weight, other_weight, out):
     own, other = kv[...], both[1 - core_index()]
     for chip in range(CHIPS):
-        out[chip % X, chip // X] = term_of(chip, own, other, ok, ov, rk, rv)
-
-
-def last_kernel(kv, both, query_grad, ok, ov, rk, rv, *rest):
+        out[chip % X, chip // X] = term_of(chip, own, other, own_weight, other_weight)
+
+
+def last_kernel(kv, both, query_grad, own_weight, other_weight, *rest):
     out, held, term_sems, query_sems = rest[-4:]
     copies = [
         pltpu.make_async_copy(query_grad, out.at[chip, 0], query_sems.at[chip])
@@ -267,7 +287,7 @@
         copy.start()
     own, other = kv[...], both[1 - core_index()]
     for chip in range(CHIPS):
-        held[chip] = term_of(chip, own, other, ok, ov, rk, rv)
+        held[chip] = term_of(chip, own, other, own_weight, other_weight)
         copies.append(pltpu.make_async_copy(held.at[chip], out.at[chip, 1], term_sems.at[chip]))
         copies[-1].start()
     for copy in copies:
@@ -277,22 +297,22 @@
 TERM_COST = pl.CostEstimate(flops=2 * W * W * 4 * W * CHIPS, bytes_accessed=3 << 20, transcendentals=0)
 
 
-def term_parts(kv, w_key, w_value):
+def term_parts(kv, w_term):
     return pl.pallas_call(
         term_kernel,
         out_shape=jax.ShapeDtypeStruct((X, Z, W, W), BF16),
-        in_specs=[vmem()] * 6,
+        in_specs=[vmem()] * 4,
         out_specs=vmem(),
         compiler_params=PARAMS,
         cost_estimate=TERM_COST,
-    )(kv, core_pair(kv), w_key[0], w_value[0], w_key[1], w_value[1])
-
-
-def last_parts(kv, query_grad, w_key, w_value, after):
+    )(kv, core_pair(kv), *w_term)
+
+
+def last_parts(kv, query_grad, w_term, after):
     return pl.pallas_call(
         last_kernel,
         out_shape=pltpu.HBM((CHIPS, 2, W, W), BF16),
-        in_specs=[vmem()] * 7 + [anywhere()] * len(after),
+        in_specs=[vmem()] * 5 + [anywhere()] * len(after),
         out_specs=hbm(),
         scratch_shapes=[
             pltpu.VMEM((CHIPS, W, W), BF16),
@@ -301,24 +321,24 @@
         ],
         compiler_params=PARAMS,
         cost_estimate=TERM_COST,
-    )(kv, core_pair(kv), query_grad, w_key[0], w_value[0], w_key[1], w_value[1], *after)
-
-
-def x_sum_kernel(parts, *outs):
+    )(kv, core_pair(kv), query_grad, *w_term, *after)
+
+
+def x_sum_kernel(parts, *rest):
     z, _ = place()
-    for step, out in enumerate(outs):
+    for step, out in enumerate(rest[-Z:]):
         to_z = lax.rem(z + step, Z)
         out[...] = sum(parts[x, to_z].astype(F32) for x in range(X)).astype(BF16)
 
 
-def x_sum(parts):
+def x_sum(parts, after):
     return pl.pallas_call(
         x_sum_kernel,
         out_shape=[jax.ShapeDtypeStruct((W, W), BF16)] * Z,
-        in_specs=[vmem()],
+        in_specs=[vmem()] + [hbm()] * len(after),
         out_specs=[vmem()] * Z,
         compiler_params=PARAMS,
-    )(parts)
+    )(parts, *after)
 
 
 def z_sum_kernel(start, *rest):
@@ -349,22 +369,21 @@
     )(received, *after)
 
 
-def spread_kernel(count, x, *rest):
-    out, sems = rest[count], rest[-1]
-    for copy in send_to_all(x, out, sems):
+def spread_kernel(x, *rest):
+    out, sems = rest[-2:]
+    for copy in send_to_all(x.at[0] if len(x.shape) == 3 else x, out, sems):
         copy.wait()
 
 
-def spread(x, held=()):
-    return pl.pallas_call(
-        functools.partial(spread_kernel, len(held)),
-        out_shape=[pltpu.HBM((CHIPS, W, W), BF16)] + [jax.ShapeDtypeStruct(h.shape, h.dtype) for h in held],
-        in_specs=[anywhere()] * (1 + len(held)),
-        out_specs=[hbm()] + [anywhere()] * len(held),
-        input_output_aliases={1 + i: 1 + i for i in range(len(held))},
+def spread(x, source, after=()):
+    return pl.pallas_call(
+        spread_kernel,
+        out_shape=pltpu.HBM((CHIPS, W, W), BF16),
+        in_specs=[source] + [anywhere()] * len(after),
+        out_specs=hbm(),
         scratch_shapes=[pltpu.SemaphoreType.DMA((CHIPS,))],
         compiler_params=PARAMS,
-    )(x, *held)
+    )(x, *after)
 
 
 def next_kernel(slot, received, fresh, chosen):
@@ -397,32 +416,31 @@
     slot_count = queries.shape[1]
     sections = lax.axis_size("section")
 
-    grad_slice = grad_in[0]
-    gathered = chip_exchange(spread(grad_slice)[0])
-    w_out, w_query = pack(pack_columns_kernel, out_weight, query_weight)
+    gathered = chip_exchange(spread(grad_in, hbm()))
+    w_out, w_query, grad_slice = pack_columns(out_weight, query_weight, grad_in)
     ready = (w_query[1],)
-    passed = grad_slice
     for slot in range(slot_count):
         last = slot + 1 == slot_count
         mine, both = pair_product(gathered, *w_out, after=ready)
         query_grad, kv = attention_grads(mine, both, queries, keys, values, slot, copied=not last)
         if slot == 0:
-            w_key, w_value = pack(pack_rows_kernel, key_weight, value_weight, after=(mine,))
+            w_term = pack_rows(key_weight, value_weight, after=(mine,))
         if last:
             near = landed(near, after=(kv,))
-            arrived = chip_exchange(last_parts(kv, query_grad, w_key, w_value, (near,)))
+            arrived = chip_exchange(last_parts(kv, query_grad, w_term, (near,)))
             mine, both, carried = last_pair_product(arrived, *w_query, near, far)
         else:
             all_queries = chip_exchange(query_grad)
-            terms = term_parts(kv, w_key, w_value)
+            terms = term_parts(kv, w_term)
             mine, both = pair_product(all_queries, *w_query, after=(terms,))
         passed, *terms = passed_grad(grad_slice, mine, both, held=() if last else (terms,))
         if not last:
             received = below(passed, range(1, sections))
-            parts = x_sum(x_exchange(*terms))
+            arrived = x_exchange(*terms)
             grad_slice = next_grad(received, fresh_grads, slot)
-            copies, *parts = spread(grad_slice, held=parts)
+            copies = spread(grad_slice, vmem(), after=(arrived,))
             gathered = chip_exchange(copies)
+            parts = x_sum(arrived, after=(in_hbm(copies),))
             moved = [parts[0]] + [along(parts[step], 0, step) for step in range(1, Z)]
             summed = z_sum(acc_in, moved)
             near = below(summed, [i for i in range(1, sections) if i % Z_HI])

time: 142 us -> 143 us (level)
  waiting for transfers between devices: 20.5 us -> 30.2 us
  blocking collectives: 25.6 us -> 21.1 us
  Pallas kernels: 14.3 us -> 12.4 us
  starting transfers between devices: 69.8 us -> 68.1 us
  local copies, waits for them, and re-layouts: 8.74 us -> 7.24 us
    all_to_all x4, waiting for transfers between devices: 10.4 us -> 20.7 us  [chip_exchange(): lax.all_to_all(parts, 'tp', split_axis=0, concat_axis=0, tiled=True, axis...]
    all_gather x6, blocking collectives: 25.6 us -> 21.1 us  [core_pair(): lax.all_gather(value, 'tp', axis=0, tiled=False, axis_index_groups=groups)]
    ppermute x4 -> x3, starting transfers between devices: 9.25 us -> 7.32 us  [sibling_swap(): return lax.ppermute(value, 'tp', [(i, i ^ 1) for i in range(CHIPS * CORES)])]
    unnamed x36, local copies, waits for them, and re-layouts: 8.74 us -> 7.24 us
  transfers between devices with their start and end apart: 15 -> 14, of which waited for: 9 -> 8; matrix products, arithmetic and copies ran while one was open for 0% -> 0% of each run, Pallas kernels for 3% -> 3%
where the time goes in v5:
time: 143 us; the launch traced here: 140 us
  starting transfers between devices  68.1 us (48%)
  waiting for transfers between devices  30.2 us (21%)
  blocking collectives  21.1 us (15%)
  Pallas kernels  12.4 us (9%)
  local copies, waits for them, and re-layouts  7.24 us (5%)
    all_to_all x4, starting transfers between devices, chip_exchange(): lax.all_to_all(parts, 'tp', split_axis=0, concat_axis=0, tiled=True, axis...  24.7 us
    ppermute x3, starting transfers between devices, below(): lax.ppermute(value, 'section', [(source, source - 1) for source in sources])  22.4 us
    all_gather x6, blocking collectives, core_pair(): lax.all_gather(value, 'tp', axis=0, tiled=False, axis_index_groups=groups)  21.1 us
    all_to_all x4, waiting for transfers between devices, chip_exchange(): lax.all_to_all(parts, 'tp', split_axis=0, concat_axis=0, tiled=True, axis...  20.7 us
    ppermute x3, starting transfers between devices, along(): lax.ppermute(value, 'tp', [(member(z, x, core), member((z + z_steps) % Z,...  10.3 us
    ppermute x3, starting transfers between devices, sibling_swap(): return lax.ppermute(value, 'tp', [(i, i ^ 1) for i in range(CHIPS * CORES)])  7.32 us
    unnamed x36, local copies, waits for them, and re-layouts  7.24 us
    ppermute x3, waiting for transfers between devices, along(): lax.ppermute(value, 'tp', [(member(z, x, core), member((z + z_steps) % Z,...  5.61 us
  transfers between devices with their start and end apart: 14, of which 8 were waited for; matrix products, arithmetic and copies ran while one was open for 0% of the time, Pallas kernels for 3%

profile of v5, /device:TPU:25, one launch (start us, length us, event | category | flops | bytes accessed | tf_op | source)
XLA Modules:
  0.0 140.1 jit_solution(3725438561697442658)
XLA Ops:
  0.6 0.0 copy-start.14
  0.7 0.8 copy-done.14
  1.5 0.9 shard_map.114
  2.4 0.0 copy-start.15
  2.4 8.2 %all-to-all-start = ((bf16[16,128,128]{2,1,0:T(8,128)(2,1)}), bf16[16,128,128]{2,1,0:T(8,128)(2,1)S(1)}, u32[]{:S(2)}, u32[]{:S(2)}) async-start(bf16[16,128,128]{2,1,0:T(8,128)(2,1)} %shard_map.114), calls=%async_computation | async-start | bytes 1048576 | tf_op jit(solution)/shard_map/all_to_all | solution.py:44
  10.7 0.0 copy-start.8
  10.7 1.2 copy-done.8
  11.9 0.6 shard_map.113
  12.5 0.8 copy-done.4
  13.3 2.9 %collective-permute-start = (bf16[128,2048]{1,0:T(8,128)(2,1)S(1)}, bf16[128,2048]{1,0:T(8,128)(2,1)S(1)}, u32[]{:S(2)}, u32[]{:S(2)}) collective-permute-start(bf16[128,2048]{1,0:T(8,128)(2,1)S(1)} %get-tuple-element.30), channel_id=1, source_target_pairs={{0,1},{1,0},{2,3},{3,2},{4,5},{5,4},{6,7},{7,6},{8,9},{9,8},{10,11... | collective-permute-start | bytes 1572872 | tf_op jit(solution)/shard_map/ppermute | solution.py:85
  16.1 1.9 %collective-permute-start.1 = (bf16[128,2048]{1,0:T(8,128)(2,1)S(1)}, bf16[128,2048]{1,0:T(8,128)(2,1)S(1)}, u32[]{:S(2)}, u32[]{:S(2)}) collective-permute-start(bf16[128,2048]{1,0:T(8,128)(2,1)S(1)} %get-tuple-element.31), channel_id=1, source_target_pairs={{0,1},{1,0},{2,3},{3,2},{4,5},{5,4},{6,7},{7,6},{8,9},{9,8},{10,11... | collective-permute-start | bytes 1572872 | tf_op jit(solution)/shard_map/ppermute | solution.py:85
  18.1 0.0 collective-permute-done.other
  18.1 0.0 copy-start.2
  18.1 1.9 %collective-permute-done.1.rest_0_.other = bf16[128,2048]{1,0:T(8,128)(2,1)S(1)} collective-permute-done((bf16[128,2048]{1,0:T(8,128)(2,1)S(1)}, bf16[128,2048]{1,0:T(8,128)(2,1)S(1)}, u32[]{:S(2)}, u32[]{:S(2)}) %collective-permute-start.1) | collective-permute-done | bytes 524320 | tf_op jit(solution)/shard_map/ppermute | solution.py:85
  19.9 4.5 %all-to-all-done.g = bf16[16,128,128]{2,1,0:T(8,128)(2,1)S(1)} async-done(((bf16[16,128,128]{2,1,0:T(8,128)(2,1)}), bf16[16,128,128]{2,1,0:T(8,128)(2,1)S(1)}, u32[]{:S(2)}, u32[]{:S(2)}) %all-to-all-start) | async-done | bytes 524320 | tf_op jit(solution)/shard_map/all_to_all | solution.py:44
  24.4 0.4 shard_map.115
  24.9 0.0 copy-start.9
  24.9 4.3 %all-gather = f32[256,128]{1,0:T(8,128)S(1)} all-gather(f32[128,128]{1,0:T(8,128)S(1)} %get-tuple-element.33), channel_id=2, replica_groups={{0,1},{2,3},{4,5},{6,7},{8,9},{10,11},{12,13},{14,15},{16,17},{18,19},{..., dimensions={0}, use_global_device_ids=true | all-gather | bytes 196608 | tf_op jit(solution)/shard_map/all_gather | solution.py:90
  29.2 1.5 %shard_map.116 = (bf16[16,128,128]{2,1,0:T(8,128)(2,1)}, bf16[128,256]{1,0:T(8,128)(2,1)S(1)}) custom-call(f32[128,128]{1,0:T(8,128)S(1)} %get-tuple-element.32.mine.rest_0_, f32[2,128,128]{2,1,0:T(8,128)S(1)} %bitcast.10, bf16[1,2,128,128]{3,2,1,0:T(8,128)(2,1)S(1)} %copy-done.11, bf16[1,2,128,128]{3,2,1,0:T(8,128)(2,1)S(1)} %copy-done.12, ...), custom_call_target="tpu_custom_call" | custom-call | flops 41943040 | bytes 1048576 | tf_op jit(solution)/shard_map/pallas_call | solution.py:256
  30.8 4.2 %all-to-all-start.1 = ((bf16[16,128,128]{2,1,0:T(8,128)(2,1)}), bf16[16,128,128]{2,1,0:T(8,128)(2,1)S(1)}, u32[]{:S(2)}, u32[]{:S(2)}) async-start(bf16[16,128,128]{2,1,0:T(8,128)(2,1)} %get-tuple-element.34), calls=%async_computation.1 | async-start | bytes 1048576 | tf_op jit(solution)/shard_map/all_to_all | solution.py:44
  35.0 0.0 copy-start.10
  35.0 1.2 copy-done.10
  36.2 0.4 shard_map.117
  36.6 2.5 %collective-permute-start.2 = (bf16[16,128,256]{2,1,0:T(8,128)(2,1)S(1)}, bf16[16,128,256]{2,1,0:T(8,128)(2,1)S(1)}, u32[]{:S(2)}, u32[]{:S(2)}) collective-permute-start(bf16[16,128,256]{2,1,0:T(8,128)(2,1)S(1)} %get-tuple-element.38), channel_id=1, source_target_pairs={{0,1},{1,0},{2,3},{3,2},{4,5},{5,4},{6,7},{7,6},{8,9},{9,8},{10,11... | collective-permute-start | bytes 3145736 | tf_op jit(solution)/shard_map/ppermute | solution.py:85
  39.1 2.4 %all-gather.1 = bf16[256,256]{1,0:T(8,128)(2,1)S(1)} all-gather(bf16[128,256]{1,0:T(8,128)(2,1)S(1)} %get-tuple-element.36.kv), channel_id=3, replica_groups={{0,1},{2,3},{4,5},{6,7},{8,9},{10,11},{12,13},{14,15},{16,17},{18,19},{..., dimensions={0}, use_global_device_ids=true | all-gather | bytes 196608 | tf_op jit(solution)/shard_map/all_gather | solution.py:90
  41.5 0.0 collective-permute-done.2.other_weight
  41.5 1.5 %shard_map.118.rest_0_ = bf16[4,4,128,128]{3,2,1,0:T(8,128)(2,1)} custom-call(bf16[128,256]{1,0:T(8,128)(2,1)S(1)} %get-tuple-element.36.kv, bf16[2,128,256]{2,1,0:T(8,128)(2,1)S(1)} %bitcast.8, bf16[16,128,256]{2,1,0:T(8,128)(2,1)S(1)} %get-tuple-element.37.own_weight, bf16[16,128,256]{2,1,0:T(8,128)(2,1)S(1)} %collective-permute-done.2.other_weight), custom_call_target="tpu_custom_call" | custom-call | flops 268435456 | bytes 3145728 | tf_op jit(solution)/shard_map/pallas_call | solution.py:301
  43.0 6.1 %all-to-all-done.1.g = bf16[16,128,128]{2,1,0:T(8,128)(2,1)S(1)} async-done(((bf16[16,128,128]{2,1,0:T(8,128)(2,1)}), bf16[16,128,128]{2,1,0:T(8,128)(2,1)S(1)}, u32[]{:S(2)}, u32[]{:S(2)}) %all-to-all-start.1) | async-done | bytes 524320 | tf_op jit(solution)/shard_map/all_to_all | solution.py:44
  49.1 1.0 copy-done.5
  50.1 0.4 shard_map.119
  50.6 3.8 %all-gather.2 = f32[256,128]{1,0:T(8,128)S(1)} all-gather(f32[128,128]{1,0:T(8,128)S(1)} %get-tuple-element.40), channel_id=4, replica_groups={{0,1},{2,3},{4,5},{6,7},{8,9},{10,11},{12,13},{14,15},{16,17},{18,19},{..., dimensions={0}, use_global_device_ids=true | all-gather | bytes 196608 | tf_op jit(solution)/shard_map/all_gather | solution.py:90
  54.4 0.0 copy-start.17
  54.4 3.5 %all-to-all-start.2 = ((bf16[4,4,128,128]{3,2,1,0:T(8,128)(2,1)}), bf16[4,4,128,128]{3,2,1,0:T(8,128)(2,1)S(1)}, u32[]{:S(2)}, u32[]{:S(2)}) async-start(bf16[4,4,128,128]{3,2,1,0:T(8,128)(2,1)} %get-tuple-element.42), calls=%async_computation.2 | async-start | bytes 1048576 | tf_op jit(solution)/shard_map/all_to_all | solution.py:54
  57.9 9.9 %collective-permute-start.3 = (bf16[128,128]{1,0:T(8,128)(2,1)S(1)}, bf16[128,128]{1,0:T(8,128)(2,1)S(1)}, u32[]{:S(2)}, u32[]{:S(2)}) collective-permute-start(bf16[128,128]{1,0:T(8,128)(2,1)S(1)} %get-tuple-element.41), channel_id=1, source_target_pairs={{32,0},{64,32},{96,64},{128,96},{160,128},{192,160},{224,192},{256... | collective-permute-start | bytes 98312 | tf_op jit(solution)/shard_map/ppermute | solution.py:39
  67.8 1.0 collective-permute-done.3.received
  68.8 0.0 copy-done.17
  68.8 0.0 all-to-all-done.2.rest_0_.parts
  68.9 0.9 shard_map.122.rest_0_
  69.8 6.8 %all-to-all-start.3 = ((bf16[16,128,128]{2,1,0:T(8,128)(2,1)}), bf16[16,128,128]{2,1,0:T(8,128)(2,1)}, u32[]{:S(2)}, u32[]{:S(2)}) async-start(bf16[16,128,128]{2,1,0:T(8,128)(2,1)} %shard_map.122.rest_0_), calls=%async_computation.3 | async-start | bytes 1048576 | tf_op jit(solution)/shard_map/all_to_all | solution.py:44
  76.6 0.0 copy-start.16
  76.6 0.1 shard_map.123
  76.7 3.2 %collective-permute-start.4 = (bf16[128,128]{1,0:T(8,128)(2,1)S(1)}, bf16[128,128]{1,0:T(8,128)(2,1)S(1)}, u32[]{:S(2)}, u32[]{:S(2)}) collective-permute-start(bf16[128,128]{1,0:T(8,128)(2,1)S(1)} %get-tuple-element.44), channel_id=1, source_target_pairs={{0,8},{1,9},{2,10},{3,11},{4,12},{5,13},{6,14},{7,15},{8,16},{9,17... | collective-permute-start | bytes 98312 | tf_op jit(solution)/shard_map/ppermute | solution.py:67
  80.0 4.0 %collective-permute-start.5 = (bf16[128,128]{1,0:T(8,128)(2,1)S(1)}, bf16[128,128]{1,0:T(8,128)(2,1)S(1)}, u32[]{:S(2)}, u32[]{:S(2)}) collective-permute-start(bf16[128,128]{1,0:T(8,128)(2,1)S(1)} %get-tuple-element.45), channel_id=1, source_target_pairs={{0,16},{1,17},{2,18},{3,19},{4,20},{5,21},{6,22},{7,23},{8,24},{9,... | collective-permute-start | bytes 98312 | tf_op jit(solution)/shard_map/ppermute | solution.py:67
  84.0 3.1 %collective-permute-start.6 = (bf16[128,128]{1,0:T(8,128)(2,1)S(1)}, bf16[128,128]{1,0:T(8,128)(2,1)S(1)}, u32[]{:S(2)}, u32[]{:S(2)}) collective-permute-start(bf16[128,128]{1,0:T(8,128)(2,1)S(1)} %get-tuple-element.46), channel_id=1, source_target_pairs={{0,24},{1,25},{2,26},{3,27},{4,28},{5,29},{6,30},{7,31},{8,0},{9,1... | collective-permute-start | bytes 98312 | tf_op jit(solution)/shard_map/ppermute | solution.py:67
  87.1 1.6 %collective-permute-done.4.rest_1_ = bf16[128,128]{1,0:T(8,128)(2,1)S(1)} collective-permute-done((bf16[128,128]{1,0:T(8,128)(2,1)S(1)}, bf16[128,128]{1,0:T(8,128)(2,1)S(1)}, u32[]{:S(2)}, u32[]{:S(2)}) %collective-permute-start.4) | collective-permute-done | bytes 32800 | tf_op jit(solution)/shard_map/ppermute | solution.py:67
  88.7 4.0 %collective-permute-done.5.rest_2_ = bf16[128,128]{1,0:T(8,128)(2,1)S(1)} collective-permute-done((bf16[128,128]{1,0:T(8,128)(2,1)S(1)}, bf16[128,128]{1,0:T(8,128)(2,1)S(1)}, u32[]{:S(2)}, u32[]{:S(2)}) %collective-permute-start.5) | collective-permute-done | bytes 32800 | tf_op jit(solution)/shard_map/ppermute | solution.py:67
  92.7 0.0 collective-permute-done.6.rest_3_
  92.7 1.3 collective-permute-start.7
  94.0 0.0 all-to-all-done.3.g
  94.0 1.0 copy-done.1
  95.1 1.0 copy-done.3
  96.1 1.5 %shard_map.125 = (f32[128,128]{1,0:T(8,128)S(1)}, f32[128,128]{1,0:T(8,128)S(1)}) custom-call(bf16[16,128,128]{2,1,0:T(8,128)(2,1)} %all-to-all-done.3.g, bf16[128,2048]{1,0:T(8,128)(2,1)S(1)} %copy-done.1, bf16[128,2048]{1,0:T(8,128)(2,1)S(1)} %copy-done.3, bf16[128,128]{1,0:T(8,128)(2,1)S(1)} %shard_map.124.rest_0_), custom_call_target="tpu_custom_call" | custom-call | flops 134217728 | bytes 2097152 | tf_op jit(solution)/shard_map/pallas_call | solution.py:182
  97.6 3.3 %all-gather.3 = f32[256,128]{1,0:T(8,128)S(1)} all-gather(f32[128,128]{1,0:T(8,128)S(1)} %get-tuple-element.48), channel_id=5, replica_groups={{0,1},{2,3},{4,5},{6,7},{8,9},{10,11},{12,13},{14,15},{16,17},{18,19},{..., dimensions={0}, use_global_device_ids=true | all-gather | bytes 196608 | tf_op jit(solution)/shard_map/all_gather | solution.py:90
  100.9 0.7 shard_map.126
  101.5 1.9 %all-gather.4 = bf16[256,256]{1,0:T(8,128)(2,1)S(1)} all-gather(bf16[128,256]{1,0:T(8,128)(2,1)S(1)} %get-tuple-element.49.rest_0_.kv), channel_id=6, replica_groups={{0,1},{2,3},{4,5},{6,7},{8,9},{10,11},{12,13},{14,15},{16,17},{18,19},{..., dimensions={0}, use_global_device_ids=true | all-gather | bytes 196608 | tf_op jit(solution)/shard_map/all_gather | solution.py:90
  103.4 0.0 collective-permute-done.7.received
  103.4 1.6 %shard_map.128 = bf16[16,2,128,128]{3,2,1,0:T(8,128)(2,1)} custom-call(bf16[128,256]{1,0:T(8,128)(2,1)S(1)} %get-tuple-element.49.rest_0_.kv, bf16[2,128,256]{2,1,0:T(8,128)(2,1)S(1)} %bitcast.13, bf16[128,128]{1,0:T(8,128)(2,1)S(1)} %get-tuple-element.50.query_grad, bf16[16,128,256]{2,1,0:T(8,128)(2,1)S(1)} %get-tuple-element.37.own_weight, ...), custom_call_target="tpu_custom_call" | custom-call | flops 268435456 | bytes 3145728 | tf_op jit(solution)/shard_map/pallas_call | solution.py:312
  105.1 5.5 %all-to-all-start.4 = ((bf16[16,2,128,128]{3,2,1,0:T(8,128)(2,1)}), bf16[16,2,128,128]{3,2,1,0:T(8,128)(2,1)S(1)}, u32[]{:S(2)}, u32[]{:S(2)}) async-start(bf16[16,2,128,128]{3,2,1,0:T(8,128)(2,1)} %shard_map.128), calls=%async_computation.4 | async-start | bytes 2097152 | tf_op jit(solution)/shard_map/all_to_all | solution.py:44
  110.6 11.1 %collective-permute-start.8 = (bf16[128,128]{1,0:T(8,128)(2,1)S(1)}, bf16[128,128]{1,0:T(8,128)(2,1)S(1)}, u32[]{:S(2)}, u32[]{:S(2)}) collective-permute-start(bf16[128,128]{1,0:T(8,128)(2,1)S(1)} %shard_map.124.rest_0_), channel_id=1, source_target_pairs={{128,96},{256,224},{384,352},{129,97},{257,225},{385,353},{130,98}... | collective-permute-start | bytes 98312 | tf_op jit(solution)/shard_map/ppermute | solution.py:39
  121.7 1.0 collective-permute-done.8.far
  122.7 10.1 %all-to-all-done.4.arrived = bf16[16,2,128,128]{3,2,1,0:T(8,128)(2,1)S(1)} async-done(((bf16[16,2,128,128]{3,2,1,0:T(8,128)(2,1)}), bf16[16,2,128,128]{3,2,1,0:T(8,128)(2,1)S(1)}, u32[]{:S(2)}, u32[]{:S(2)}) %all-to-all-start.4) | async-done | bytes 1048608 | tf_op jit(solution)/shard_map/all_to_all | solution.py:44
  132.9 1.1 shard_map.129
  133.9 5.5 %all-gather.5 = f32[256,128]{1,0:T(8,128)S(1)} all-gather(f32[128,128]{1,0:T(8,128)S(1)} %get-tuple-element.52), channel_id=7, replica_groups={{0,1},{2,3},{4,5},{6,7},{8,9},{10,11},{12,13},{14,15},{16,17},{18,19},{..., dimensions={0}, use_global_device_ids=true | all-gather | bytes 196608 | tf_op jit(solution)/shard_map/all_gather | solution.py:90
  139.5 0.6 shard_map.130
  (24 shorter events, 0.1 us)
Async XLA Ops:
  0.6 10.0 %copy-start.7 = (bf16[1,128,4096]{2,1,0:T(8,128)(2,1)S(1)}, bf16[1,128,4096]{2,1,0:T(8,128)(2,1)}, u32[]{:S(2)}) copy-start(bf16[1,128,4096]{2,1,0:T(8,128)(2,1)} %a.2) | copy-start | bytes 3145732
  0.6 0.8 copy-start.14
  2.4 8.2 %copy-start.15 = (bf16[1,128,128]{2,1,0:T(8,128)(2,1)S(1)}, bf16[1,128,128]{2,1,0:T(8,128)(2,1)}, u32[]{:S(2)}) copy-start(bf16[1,128,128]{2,1,0:T(8,128)(2,1)} %x.1) | copy-start | bytes 98308
  2.4 22.0 %all-to-all-start = ((bf16[16,128,128]{2,1,0:T(8,128)(2,1)}), bf16[16,128,128]{2,1,0:T(8,128)(2,1)S(1)}, u32[]{:S(2)}, u32[]{:S(2)}) async-start(bf16[16,128,128]{2,1,0:T(8,128)(2,1)} %shard_map.114), calls=%async_computation | async-start | bytes 1048576 | tf_op jit(solution)/shard_map/all_to_all | solution.py:44
  10.7 1.2 copy-start.8
  12.5 0.8 copy-start.4
  13.3 11.6 %copy-start = (bf16[128,2048]{1,0:T(8,128)(2,1)}, bf16[128,2048]{1,0:T(8,128)(2,1)S(1)}, u32[]{:S(2)}) copy-start(bf16[128,2048]{1,0:T(8,128)(2,1)S(1)} %get-tuple-element.29.own) | copy-start | bytes 1572868
  13.3 4.8 %collective-permute-start = (bf16[128,2048]{1,0:T(8,128)(2,1)S(1)}, bf16[128,2048]{1,0:T(8,128)(2,1)S(1)}, u32[]{:S(2)}, u32[]{:S(2)}) collective-permute-start(bf16[128,2048]{1,0:T(8,128)(2,1)S(1)} %get-tuple-element.30), channel_id=1, source_target_pairs={{0,1},{1,0},{2,3},{3,2},{4,5},{5,4},{6,7},{7,6},{8,9},{9,8},{10,11... | collective-permute-start | bytes 1572872 | tf_op jit(solution)/shard_map/ppermute | solution.py:85
  16.1 3.8 %collective-permute-start.1 = (bf16[128,2048]{1,0:T(8,128)(2,1)S(1)}, bf16[128,2048]{1,0:T(8,128)(2,1)S(1)}, u32[]{:S(2)}, u32[]{:S(2)}) collective-permute-start(bf16[128,2048]{1,0:T(8,128)(2,1)S(1)} %get-tuple-element.31), channel_id=1, source_target_pairs={{0,1},{1,0},{2,3},{3,2},{4,5},{5,4},{6,7},{7,6},{8,9},{9,8},{10,11... | collective-permute-start | bytes 1572872 | tf_op jit(solution)/shard_map/ppermute | solution.py:85
  18.1 6.8 %copy-start.2 = (bf16[128,2048]{1,0:T(8,128)(2,1)}, bf16[128,2048]{1,0:T(8,128)(2,1)S(1)}, u32[]{:S(2)}) copy-start(bf16[128,2048]{1,0:T(8,128)(2,1)S(1)} %collective-permute-done.other) | copy-start | bytes 1572868
  24.4 4.8 %copy-start.11 = (bf16[1,2,128,128]{3,2,1,0:T(8,128)(2,1)S(1)}, bf16[1,2,128,128]{3,2,1,0:T(8,128)(2,1)}, u32[]{:S(2)}) copy-start(bf16[1,2,128,128]{3,2,1,0:T(8,128)(2,1)} %queries.3) | copy-start | bytes 196612
  24.4 4.8 %copy-start.12 = (bf16[1,2,128,128]{3,2,1,0:T(8,128)(2,1)S(1)}, bf16[1,2,128,128]{3,2,1,0:T(8,128)(2,1)}, u32[]{:S(2)}) copy-start(bf16[1,2,128,128]{3,2,1,0:T(8,128)(2,1)} %keys.3) | copy-start | bytes 196612
  24.4 4.8 %copy-start.13 = (bf16[1,2,128,128]{3,2,1,0:T(8,128)(2,1)S(1)}, bf16[1,2,128,128]{3,2,1,0:T(8,128)(2,1)}, u32[]{:S(2)}) copy-start(bf16[1,2,128,128]{3,2,1,0:T(8,128)(2,1)} %values.3) | copy-start | bytes 196612
  24.9 10.1 %copy-start.9 = (bf16[1,4096,128]{2,1,0:T(8,128)(2,1)S(1)}, bf16[1,4096,128]{2,1,0:T(8,128)(2,1)}, u32[]{:S(2)}) copy-start(bf16[1,4096,128]{2,1,0:T(8,128)(2,1)} %a.3) | copy-start | bytes 3145732
  30.8 18.3 %all-to-all-start.1 = ((bf16[16,128,128]{2,1,0:T(8,128)(2,1)}), bf16[16,128,128]{2,1,0:T(8,128)(2,1)S(1)}, u32[]{:S(2)}, u32[]{:S(2)}) async-start(bf16[16,128,128]{2,1,0:T(8,128)(2,1)} %get-tuple-element.34), calls=%async_computation.1 | async-start | bytes 1048576 | tf_op jit(solution)/shard_map/all_to_all | solution.py:44
  35.0 1.2 copy-start.10
  36.6 4.9 %collective-permute-start.2 = (bf16[16,128,256]{2,1,0:T(8,128)(2,1)S(1)}, bf16[16,128,256]{2,1,0:T(8,128)(2,1)S(1)}, u32[]{:S(2)}, u32[]{:S(2)}) collective-permute-start(bf16[16,128,256]{2,1,0:T(8,128)(2,1)S(1)} %get-tuple-element.38), channel_id=1, source_target_pairs={{0,1},{1,0},{2,3},{3,2},{4,5},{5,4},{6,7},{7,6},{8,9},{9,8},{10,11... | collective-permute-start | bytes 3145736 | tf_op jit(solution)/shard_map/ppermute | solution.py:85
  49.1 1.0 copy-start.5
  54.4 14.5 %copy-start.17 = (bf16[1,128,128]{2,1,0:T(8,128)(2,1)S(1)}, bf16[1,128,128]{2,1,0:T(8,128)(2,1)}, u32[]{:S(2)}) copy-start(bf16[1,128,128]{2,1,0:T(8,128)(2,1)} %fresh.1) | copy-start | bytes 98308
  54.4 14.5 %all-to-all-start.2 = ((bf16[4,4,128,128]{3,2,1,0:T(8,128)(2,1)}), bf16[4,4,128,128]{3,2,1,0:T(8,128)(2,1)S(1)}, u32[]{:S(2)}, u32[]{:S(2)}) async-start(bf16[4,4,128,128]{3,2,1,0:T(8,128)(2,1)} %get-tuple-element.42), calls=%async_computation.2 | async-start | bytes 1048576 | tf_op jit(solution)/shard_map/all_to_all | solution.py:54
  57.9 10.9 %collective-permute-start.3 = (bf16[128,128]{1,0:T(8,128)(2,1)S(1)}, bf16[128,128]{1,0:T(8,128)(2,1)S(1)}, u32[]{:S(2)}, u32[]{:S(2)}) collective-permute-start(bf16[128,128]{1,0:T(8,128)(2,1)S(1)} %get-tuple-element.41), channel_id=1, source_target_pairs={{32,0},{64,32},{96,64},{128,96},{160,128},{192,160},{224,192},{256... | collective-permute-start | bytes 98312 | tf_op jit(solution)/shard_map/ppermute | solution.py:39
  69.8 24.2 %all-to-all-start.3 = ((bf16[16,128,128]{2,1,0:T(8,128)(2,1)}), bf16[16,128,128]{2,1,0:T(8,128)(2,1)}, u32[]{:S(2)}, u32[]{:S(2)}) async-start(bf16[16,128,128]{2,1,0:T(8,128)(2,1)} %shard_map.122.rest_0_), calls=%async_computation.3 | async-start | bytes 1048576 | tf_op jit(solution)/shard_map/all_to_all | solution.py:44
  76.6 16.0 %copy-start.16 = (f32[1,128,128]{2,1,0:T(8,128)S(1)}, f32[1,128,128]{2,1,0:T(8,128)}, u32[]{:S(2)}) copy-start(f32[1,128,128]{2,1,0:T(8,128)} %start.1) | copy-start | bytes 196612
  76.7 12.0 %collective-permute-start.4 = (bf16[128,128]{1,0:T(8,128)(2,1)S(1)}, bf16[128,128]{1,0:T(8,128)(2,1)S(1)}, u32[]{:S(2)}, u32[]{:S(2)}) collective-permute-start(bf16[128,128]{1,0:T(8,128)(2,1)S(1)} %get-tuple-element.44), channel_id=1, source_target_pairs={{0,8},{1,9},{2,10},{3,11},{4,12},{5,13},{6,14},{7,15},{8,16},{9,17... | collective-permute-start | bytes 98312 | tf_op jit(solution)/shard_map/ppermute | solution.py:67
  80.0 12.7 %collective-permute-start.5 = (bf16[128,128]{1,0:T(8,128)(2,1)S(1)}, bf16[128,128]{1,0:T(8,128)(2,1)S(1)}, u32[]{:S(2)}, u32[]{:S(2)}) collective-permute-start(bf16[128,128]{1,0:T(8,128)(2,1)S(1)} %get-tuple-element.45), channel_id=1, source_target_pairs={{0,16},{1,17},{2,18},{3,19},{4,20},{5,21},{6,22},{7,23},{8,24},{9,... | collective-permute-start | bytes 98312 | tf_op jit(solution)/shard_map/ppermute | solution.py:67
  84.0 8.7 %collective-permute-start.6 = (bf16[128,128]{1,0:T(8,128)(2,1)S(1)}, bf16[128,128]{1,0:T(8,128)(2,1)S(1)}, u32[]{:S(2)}, u32[]{:S(2)}) collective-permute-start(bf16[128,128]{1,0:T(8,128)(2,1)S(1)} %get-tuple-element.46), channel_id=1, source_target_pairs={{0,24},{1,25},{2,26},{3,27},{4,28},{5,29},{6,30},{7,31},{8,0},{9,1... | collective-permute-start | bytes 98312 | tf_op jit(solution)/shard_map/ppermute | solution.py:67
  92.7 10.7 %collective-permute-start.7 = (bf16[128,128]{1,0:T(8,128)(2,1)S(1)}, bf16[128,128]{1,0:T(8,128)(2,1)S(1)}, u32[]{:S(2)}, u32[]{:S(2)}) collective-permute-start(bf16[128,128]{1,0:T(8,128)(2,1)S(1)} %shard_map.124.rest_0_), channel_id=1, source_target_pairs={{32,0},{64,32},{96,64},{160,128},{192,160},{224,192},{288,256},{32... | collective-permute-start | bytes 98312 | tf_op jit(solution)/shard_map/ppermute | solution.py:39
  94.0 1.0 copy-start.1
  95.1 1.0 copy-start.3
  105.1 27.8 %copy-start.6 = (bf16[128,2048]{1,0:T(8,128)(2,1)S(1)}, bf16[128,2048]{1,0:T(8,128)(2,1)}, u32[]{:S(2)}) copy-start(bf16[128,2048]{1,0:T(8,128)(2,1)} %copy-done.4) | copy-start | bytes 1572868
  105.1 27.8 %all-to-all-start.4 = ((bf16[16,2,128,128]{3,2,1,0:T(8,128)(2,1)}), bf16[16,2,128,128]{3,2,1,0:T(8,128)(2,1)S(1)}, u32[]{:S(2)}, u32[]{:S(2)}) async-start(bf16[16,2,128,128]{3,2,1,0:T(8,128)(2,1)} %shard_map.128), calls=%async_computation.4 | async-start | bytes 2097152 | tf_op jit(solution)/shard_map/all_to_all | solution.py:44
  110.6 12.1 %collective-permute-start.8 = (bf16[128,128]{1,0:T(8,128)(2,1)S(1)}, bf16[128,128]{1,0:T(8,128)(2,1)S(1)}, u32[]{:S(2)}, u32[]{:S(2)}) collective-permute-start(bf16[128,128]{1,0:T(8,128)(2,1)S(1)} %shard_map.124.rest_0_), channel_id=1, source_target_pairs={{128,96},{256,224},{384,352},{129,97},{257,225},{385,353},{130,98}... | collective-permute-start | bytes 98312 | tf_op jit(solution)/shard_map/ppermute | solution.py:39

commit v6 on v5

--- a/solution.py
+++ b/solution.py
@@ -129,24 +129,24 @@
 
 
 def pack_rows_kernel(a, b, *rest):
-    own_ab, other_ab = rest[-2:]
+    own_a, own_b, other_a, other_b = rest[-4:]
     for chip, own, other in halves():
-        other_ab[chip, :, :W] = a[0, other, :]
-        other_ab[chip, :, W:] = b[0, other, :]
-        own_ab[chip, :, :W] = a[0, own, :]
-        own_ab[chip, :, W:] = b[0, own, :]
+        other_a[chip] = a[0, other, :]
+        other_b[chip] = b[0, other, :]
+        own_a[chip] = a[0, own, :]
+        own_b[chip] = b[0, own, :]
 
 
 def pack_rows(a, b, after):
-    own, other = pl.pallas_call(
+    own_a, own_b, other_a, other_b = pl.pallas_call(
         pack_rows_kernel,
-        out_shape=[jax.ShapeDtypeStruct((CHIPS, W, 2 * W), BF16)] * 2,
+        out_shape=[jax.ShapeDtypeStruct((CHIPS, W, W), BF16)] * 4,
         in_specs=[vmem()] * 2 + [anywhere()] * len(after),
-        out_specs=[vmem()] * 2,
+        out_specs=[vmem()] * 4,
         compiler_params=PARAMS,
         cost_estimate=pl.CostEstimate(flops=0, bytes_accessed=4 << 20, transcendentals=0),
     )(a, b, *after)
-    return own, sibling_swap(other)
+    return own_a, own_b, sibling_swap(other_a), sibling_swap(other_b)
 
 
 def pair_kernel(after, g, own, other, *rest):
@@ -267,17 +267,21 @@
     )(mine, both, queries, keys, values)
 
 
-def term_of(chip, own, other, own_weight, other_weight):
-    return (dot(own, own_weight[chip], 1, 1) + dot(other, other_weight[chip], 1, 1)).astype(BF16)
-
-
-def term_kernel(kv, both, own_weight, other_weight, out):
+def term_of(chip, own, other, ok, ov, rk, rv):
+    total = dot(own[:, :W], ok[chip], 1, 1)
+    total += dot(own[:, W:], ov[chip], 1, 1)
+    total += dot(other[:, :W], rk[chip], 1, 1)
+    total += dot(other[:, W:], rv[chip], 1, 1)
+    return total.astype(BF16)
+
+
+def term_kernel(kv, both, ok, ov, rk, rv, out):
     own, other = kv[...], both[1 - core_index()]
     for chip in range(CHIPS):
-        out[chip % X, chip // X] = term_of(chip, own, other, own_weight, other_weight)
-
-
-def last_kernel(kv, both, query_grad, own_weight, other_weight, *rest):
+        out[chip % X, chip // X] = term_of(chip, own, other, ok, ov, rk, rv)
+
+
+def last_kernel(kv, both, query_grad, ok, ov, rk, rv, *rest):
     out, held, term_sems, query_sems = rest[-4:]
     copies = [
         pltpu.make_async_copy(query_grad, out.at[chip, 0], query_sems.at[chip])
@@ -287,7 +291,7 @@
         copy.start()
     own, other = kv[...], both[1 - core_index()]
     for chip in range(CHIPS):
-        held[chip] = term_of(chip, own, other, own_weight, other_weight)
+        held[chip] = term_of(chip, own, other, ok, ov, rk, rv)
         copies.append(pltpu.make_async_copy(held.at[chip], out.at[chip, 1], term_sems.at[chip]))
         copies[-1].start()
     for copy in copies:
@@ -301,7 +305,7 @@
     return pl.pallas_call(
         term_kernel,
         out_shape=jax.ShapeDtypeStruct((X, Z, W, W), BF16),
-        in_specs=[vmem()] * 4,
+        in_specs=[vmem()] * 6,
         out_specs=vmem(),
         compiler_params=PARAMS,
         cost_estimate=TERM_COST,
@@ -312,7 +316,7 @@
     return pl.pallas_call(
         last_kernel,
         out_shape=pltpu.HBM((CHIPS, 2, W, W), BF16),
-        in_specs=[vmem()] * 5 + [anywhere()] * len(after),
+        in_specs=[vmem()] * 7 + [anywhere()] * len(after),
         out_specs=hbm(),
         scratch_shapes=[
             pltpu.VMEM((CHIPS, W, W), BF16),

time: 143 us -> 140 us (0.979)
  waiting for transfers between devices: 30.2 us -> 21.8 us
  blocking collectives: 21.1 us -> 25.8 us
  starting transfers between devices: 68.1 us -> 69.6 us
    all_to_all x4, waiting for transfers between devices: 20.7 us -> 11.8 us  [chip_exchange(): lax.all_to_all(parts, 'tp', split_axis=0, concat_axis=0, tiled=True, axis...]
    all_gather x6, blocking collectives: 21.1 us -> 25.8 us  [core_pair(): lax.all_gather(value, 'tp', axis=0, tiled=False, axis_index_groups=groups)]
    ppermute x3 -> x4, starting transfers between devices: 7.32 us -> 9.25 us  [sibling_swap(): return lax.ppermute(value, 'tp', [(i, i ^ 1) for i in range(CHIPS * CORES)])]
    unnamed x36 -> x38, local copies, waits for them, and re-layouts: 7.24 us -> 7.03 us
  transfers between devices with their start and end apart: 14 -> 15, of which waited for: 8 -> 9; matrix products, arithmetic and copies ran while one was open for 0% -> 0% of each run, Pallas kernels for 3% -> 3%
where the time goes in v6:
time: 140 us; the launch traced here: 138 us
  starting transfers between devices  69.6 us (50%)
  blocking collectives  25.8 us (18%)
  waiting for transfers between devices  21.8 us (16%)
  Pallas kernels  12.8 us (9%)
  local copies, waits for them, and re-layouts  7.03 us (5%)
    all_gather x6, blocking collectives, core_pair(): lax.all_gather(value, 'tp', axis=0, tiled=False, axis_index_groups=groups)  25.8 us
    all_to_all x4, starting transfers between devices, chip_exchange(): lax.all_to_all(parts, 'tp', split_axis=0, concat_axis=0, tiled=True, axis...  23.7 us
    ppermute x3, starting transfers between devices, below(): lax.ppermute(value, 'section', [(source, source - 1) for source in sources])  22.9 us
    all_to_all x4, waiting for transfers between devices, chip_exchange(): lax.all_to_all(parts, 'tp', split_axis=0, concat_axis=0, tiled=True, axis...  11.8 us
    ppermute x3, starting transfers between devices, along(): lax.ppermute(value, 'tp', [(member(z, x, core), member((z + z_steps) % Z,...  10.4 us
    ppermute x4, starting transfers between devices, sibling_swap(): return lax.ppermute(value, 'tp', [(i, i ^ 1) for i in range(CHIPS * CORES)])  9.25 us
    unnamed x38, local copies, waits for them, and re-layouts  7.03 us
    ppermute x3, waiting for transfers between devices, along(): lax.ppermute(value, 'tp', [(member(z, x, core), member((z + z_steps) % Z,...  5.45 us
  transfers between devices with their start and end apart: 15, of which 9 were waited for; matrix products, arithmetic and copies ran while one was open for 0% of the time, Pallas kernels for 3%

profile of v6, /device:TPU:25, one launch (start us, length us, event | category | flops | bytes accessed | tf_op | source)
XLA Modules:
  0.0 138.1 jit_solution(8027295202963313595)
XLA Ops:
  0.6 0.0 copy-start.15
  0.7 0.8 copy-done.15
  1.5 0.9 shard_map.114
  2.4 0.0 copy-start.16
  2.4 8.2 %all-to-all-start = ((bf16[16,128,128]{2,1,0:T(8,128)(2,1)}), bf16[16,128,128]{2,1,0:T(8,128)(2,1)S(1)}, u32[]{:S(2)}, u32[]{:S(2)}) async-start(bf16[16,128,128]{2,1,0:T(8,128)(2,1)} %shard_map.114), calls=%async_computation | async-start | bytes 1048576 | tf_op jit(solution)/shard_map/all_to_all | solution.py:44
  10.7 0.0 copy-start.9
  10.7 1.2 copy-done.9
  11.9 0.6 shard_map.113
  12.5 2.9 %collective-permute-start = (bf16[128,2048]{1,0:T(8,128)(2,1)S(1)}, bf16[128,2048]{1,0:T(8,128)(2,1)S(1)}, u32[]{:S(2)}, u32[]{:S(2)}) collective-permute-start(bf16[128,2048]{1,0:T(8,128)(2,1)S(1)} %get-tuple-element.32), channel_id=1, source_target_pairs={{0,1},{1,0},{2,3},{3,2},{4,5},{5,4},{6,7},{7,6},{8,9},{9,8},{10,11... | collective-permute-start | bytes 1572872 | tf_op jit(solution)/shard_map/ppermute | solution.py:85
  15.3 1.9 %collective-permute-start.1 = (bf16[128,2048]{1,0:T(8,128)(2,1)S(1)}, bf16[128,2048]{1,0:T(8,128)(2,1)S(1)}, u32[]{:S(2)}, u32[]{:S(2)}) collective-permute-start(bf16[128,2048]{1,0:T(8,128)(2,1)S(1)} %get-tuple-element.33), channel_id=1, source_target_pairs={{0,1},{1,0},{2,3},{3,2},{4,5},{5,4},{6,7},{7,6},{8,9},{9,8},{10,11... | collective-permute-start | bytes 1572872 | tf_op jit(solution)/shard_map/ppermute | solution.py:85
  17.3 0.0 collective-permute-done.other
  17.3 1.9 %collective-permute-done.1.rest_0_.other = bf16[128,2048]{1,0:T(8,128)(2,1)S(1)} collective-permute-done((bf16[128,2048]{1,0:T(8,128)(2,1)S(1)}, bf16[128,2048]{1,0:T(8,128)(2,1)S(1)}, u32[]{:S(2)}, u32[]{:S(2)}) %collective-permute-start.1) | collective-permute-done | bytes 524320 | tf_op jit(solution)/shard_map/ppermute | solution.py:85
  19.2 5.3 %all-to-all-done.g = bf16[16,128,128]{2,1,0:T(8,128)(2,1)S(1)} async-done(((bf16[16,128,128]{2,1,0:T(8,128)(2,1)}), bf16[16,128,128]{2,1,0:T(8,128)(2,1)S(1)}, u32[]{:S(2)}, u32[]{:S(2)}) %all-to-all-start) | async-done | bytes 524320 | tf_op jit(solution)/shard_map/all_to_all | solution.py:44
  24.4 0.4 shard_map.115
  24.9 0.0 copy-start.12
  24.9 0.0 copy-start.13
  24.9 0.0 copy-start.14
  24.9 4.3 %all-gather = f32[256,128]{1,0:T(8,128)S(1)} all-gather(f32[128,128]{1,0:T(8,128)S(1)} %get-tuple-element.35), channel_id=2, replica_groups={{0,1},{2,3},{4,5},{6,7},{8,9},{10,11},{12,13},{14,15},{16,17},{18,19},{..., dimensions={0}, use_global_device_ids=true | all-gather | bytes 196608 | tf_op jit(solution)/shard_map/all_gather | solution.py:90
  29.2 1.6 %shard_map.116 = (bf16[16,128,128]{2,1,0:T(8,128)(2,1)}, bf16[128,256]{1,0:T(8,128)(2,1)S(1)}) custom-call(f32[128,128]{1,0:T(8,128)S(1)} %get-tuple-element.34.mine.rest_0_, f32[2,128,128]{2,1,0:T(8,128)S(1)} %bitcast.10, bf16[1,2,128,128]{3,2,1,0:T(8,128)(2,1)S(1)} %copy-done.12, bf16[1,2,128,128]{3,2,1,0:T(8,128)(2,1)S(1)} %copy-done.13, ...), custom_call_target="tpu_custom_call" | custom-call | flops 41943040 | bytes 1048576 | tf_op jit(solution)/shard_map/pallas_call | solution.py:256
  30.8 4.2 %all-to-all-start.1 = ((bf16[16,128,128]{2,1,0:T(8,128)(2,1)}), bf16[16,128,128]{2,1,0:T(8,128)(2,1)S(1)}, u32[]{:S(2)}, u32[]{:S(2)}) async-start(bf16[16,128,128]{2,1,0:T(8,128)(2,1)} %get-tuple-element.36), calls=%async_computation.1 | async-start | bytes 1048576 | tf_op jit(solution)/shard_map/all_to_all | solution.py:44
  35.0 0.0 copy-start.10
  35.0 1.2 copy-done.10
  36.2 1.2 copy-done.11
  37.4 0.1 shard_map.117
  37.6 2.5 %collective-permute-start.2 = (bf16[16,128,128]{2,1,0:T(8,128)(2,1)S(1)}, bf16[16,128,128]{2,1,0:T(8,128)(2,1)S(1)}, u32[]{:S(2)}, u32[]{:S(2)}) collective-permute-start(bf16[16,128,128]{2,1,0:T(8,128)(2,1)S(1)} %get-tuple-element.41), channel_id=1, source_target_pairs={{0,1},{1,0},{2,3},{3,2},{4,5},{5,4},{6,7},{7,6},{8,9},{9,8},{10,11... | collective-permute-start | bytes 1572872 | tf_op jit(solution)/shard_map/ppermute | solution.py:85
  40.1 1.9 %collective-permute-start.3 = (bf16[16,128,128]{2,1,0:T(8,128)(2,1)S(1)}, bf16[16,128,128]{2,1,0:T(8,128)(2,1)S(1)}, u32[]{:S(2)}, u32[]{:S(2)}) collective-permute-start(bf16[16,128,128]{2,1,0:T(8,128)(2,1)S(1)} %get-tuple-element.42), channel_id=1, source_target_pairs={{0,1},{1,0},{2,3},{3,2},{4,5},{5,4},{6,7},{7,6},{8,9},{9,8},{10,11... | collective-permute-start | bytes 1572872 | tf_op jit(solution)/shard_map/ppermute | solution.py:85
  42.1 2.0 %all-gather.1 = bf16[256,256]{1,0:T(8,128)(2,1)S(1)} all-gather(bf16[128,256]{1,0:T(8,128)(2,1)S(1)} %get-tuple-element.38.kv), channel_id=3, replica_groups={{0,1},{2,3},{4,5},{6,7},{8,9},{10,11},{12,13},{14,15},{16,17},{18,19},{..., dimensions={0}, use_global_device_ids=true | all-gather | bytes 196608 | tf_op jit(solution)/shard_map/all_gather | solution.py:90
  44.1 0.0 collective-permute-done.2.rk
  44.1 0.0 collective-permute-done.3.rv
  44.1 2.3 %shard_map.118.rest_0_ = bf16[4,4,128,128]{3,2,1,0:T(8,128)(2,1)} custom-call(bf16[128,256]{1,0:T(8,128)(2,1)S(1)} %get-tuple-element.38.kv, bf16[2,128,256]{2,1,0:T(8,128)(2,1)S(1)} %bitcast.8, bf16[16,128,128]{2,1,0:T(8,128)(2,1)S(1)} %get-tuple-element.39.ok, bf16[16,128,128]{2,1,0:T(8,128)(2,1)S(1)} %get-tuple-element.40.ov, ...), custom_call_target="tpu_custom_call" | custom-call | flops 268435456 | bytes 3145728 | tf_op jit(solution)/shard_map/pallas_call | solution.py:305
  46.5 0.8 copy-done.2
  47.3 0.8 copy-done.4
  48.1 0.8 copy-done.6
  48.9 0.2 all-to-all-done.1.g
  49.1 0.4 shard_map.119
  49.6 3.8 %all-gather.2 = f32[256,128]{1,0:T(8,128)S(1)} all-gather(f32[128,128]{1,0:T(8,128)S(1)} %get-tuple-element.44), channel_id=4, replica_groups={{0,1},{2,3},{4,5},{6,7},{8,9},{10,11},{12,13},{14,15},{16,17},{18,19},{..., dimensions={0}, use_global_device_ids=true | all-gather | bytes 196608 | tf_op jit(solution)/shard_map/all_gather | solution.py:90
  53.3 0.0 copy-start.18
  53.4 3.5 %all-to-all-start.2 = ((bf16[4,4,128,128]{3,2,1,0:T(8,128)(2,1)}), bf16[4,4,128,128]{3,2,1,0:T(8,128)(2,1)S(1)}, u32[]{:S(2)}, u32[]{:S(2)}) async-start(bf16[4,4,128,128]{3,2,1,0:T(8,128)(2,1)} %get-tuple-element.46), calls=%async_computation.2 | async-start | bytes 1048576 | tf_op jit(solution)/shard_map/all_to_all | solution.py:54
  56.8 9.9 %collective-permute-start.4 = (bf16[128,128]{1,0:T(8,128)(2,1)S(1)}, bf16[128,128]{1,0:T(8,128)(2,1)S(1)}, u32[]{:S(2)}, u32[]{:S(2)}) collective-permute-start(bf16[128,128]{1,0:T(8,128)(2,1)S(1)} %get-tuple-element.45), channel_id=1, source_target_pairs={{32,0},{64,32},{96,64},{128,96},{160,128},{192,160},{224,192},{256... | collective-permute-start | bytes 98312 | tf_op jit(solution)/shard_map/ppermute | solution.py:39
  66.8 1.0 collective-permute-done.4.received
  67.8 0.0 all-to-all-done.2.rest_0_.parts
  67.8 1.0 shard_map.122.rest_0_
  68.8 5.9 %all-to-all-start.3 = ((bf16[16,128,128]{2,1,0:T(8,128)(2,1)}), bf16[16,128,128]{2,1,0:T(8,128)(2,1)S(1)}, u32[]{:S(2)}, u32[]{:S(2)}) async-start(bf16[16,128,128]{2,1,0:T(8,128)(2,1)} %shard_map.122.rest_0_), calls=%async_computation.3 | async-start | bytes 1048576 | tf_op jit(solution)/shard_map/all_to_all | solution.py:44
  74.7 0.0 copy-start.17
  74.7 0.1 shard_map.123
  74.8 3.3 %collective-permute-start.5 = (bf16[128,128]{1,0:T(8,128)(2,1)S(1)}, bf16[128,128]{1,0:T(8,128)(2,1)S(1)}, u32[]{:S(2)}, u32[]{:S(2)}) collective-permute-start(bf16[128,128]{1,0:T(8,128)(2,1)S(1)} %get-tuple-element.48), channel_id=1, source_target_pairs={{0,8},{1,9},{2,10},{3,11},{4,12},{5,13},{6,14},{7,15},{8,16},{9,17... | collective-permute-start | bytes 98312 | tf_op jit(solution)/shard_map/ppermute | solution.py:67
  78.1 4.0 %collective-permute-start.6 = (bf16[128,128]{1,0:T(8,128)(2,1)S(1)}, bf16[128,128]{1,0:T(8,128)(2,1)S(1)}, u32[]{:S(2)}, u32[]{:S(2)}) collective-permute-start(bf16[128,128]{1,0:T(8,128)(2,1)S(1)} %get-tuple-element.49), channel_id=1, source_target_pairs={{0,16},{1,17},{2,18},{3,19},{4,20},{5,21},{6,22},{7,23},{8,24},{9,... | collective-permute-start | bytes 98312 | tf_op jit(solution)/shard_map/ppermute | solution.py:67
  82.1 3.1 %collective-permute-start.7 = (bf16[128,128]{1,0:T(8,128)(2,1)S(1)}, bf16[128,128]{1,0:T(8,128)(2,1)S(1)}, u32[]{:S(2)}, u32[]{:S(2)}) collective-permute-start(bf16[128,128]{1,0:T(8,128)(2,1)S(1)} %get-tuple-element.50), channel_id=1, source_target_pairs={{0,24},{1,25},{2,26},{3,27},{4,28},{5,29},{6,30},{7,31},{8,0},{9,1... | collective-permute-start | bytes 98312 | tf_op jit(solution)/shard_map/ppermute | solution.py:67
  85.2 0.9 collective-permute-done.5.rest_1_
  86.1 4.6 %collective-permute-done.6.rest_2_ = bf16[128,128]{1,0:T(8,128)(2,1)S(1)} collective-permute-done((bf16[128,128]{1,0:T(8,128)(2,1)S(1)}, bf16[128,128]{1,0:T(8,128)(2,1)S(1)}, u32[]{:S(2)}, u32[]{:S(2)}) %collective-permute-start.6) | collective-permute-done | bytes 32800 | tf_op jit(solution)/shard_map/ppermute | solution.py:67
  90.7 1.3 collective-permute-start.8
  92.0 0.4 shard_map.125
  92.5 3.6 %all-gather.3 = f32[256,128]{1,0:T(8,128)S(1)} all-gather(f32[128,128]{1,0:T(8,128)S(1)} %get-tuple-element.52), channel_id=5, replica_groups={{0,1},{2,3},{4,5},{6,7},{8,9},{10,11},{12,13},{14,15},{16,17},{18,19},{..., dimensions={0}, use_global_device_ids=true | all-gather | bytes 196608 | tf_op jit(solution)/shard_map/all_gather | solution.py:90
  96.1 0.7 shard_map.126
  96.8 1.9 %all-gather.4 = bf16[256,256]{1,0:T(8,128)(2,1)S(1)} all-gather(bf16[128,256]{1,0:T(8,128)(2,1)S(1)} %get-tuple-element.53.rest_0_.kv), channel_id=6, replica_groups={{0,1},{2,3},{4,5},{6,7},{8,9},{10,11},{12,13},{14,15},{16,17},{18,19},{..., dimensions={0}, use_global_device_ids=true | all-gather | bytes 196608 | tf_op jit(solution)/shard_map/all_gather | solution.py:90
  98.7 0.6 collective-permute-done.8.received
  99.3 2.5 %shard_map.128 = bf16[16,2,128,128]{3,2,1,0:T(8,128)(2,1)} custom-call(bf16[128,256]{1,0:T(8,128)(2,1)S(1)} %get-tuple-element.53.rest_0_.kv, bf16[2,128,256]{2,1,0:T(8,128)(2,1)S(1)} %bitcast.13, bf16[128,128]{1,0:T(8,128)(2,1)S(1)} %get-tuple-element.54.query_grad, bf16[16,128,128]{2,1,0:T(8,128)(2,1)S(1)} %copy-done.1, ...), custom_call_target="tpu_custom_call" | custom-call | flops 268435456 | bytes 3145728 | tf_op jit(solution)/shard_map/pallas_call | solution.py:316
  101.8 5.4 %all-to-all-start.4 = ((bf16[16,2,128,128]{3,2,1,0:T(8,128)(2,1)}), bf16[16,2,128,128]{3,2,1,0:T(8,128)(2,1)S(1)}, u32[]{:S(2)}, u32[]{:S(2)}) async-start(bf16[16,2,128,128]{3,2,1,0:T(8,128)(2,1)} %shard_map.128), calls=%async_computation.4 | async-start | bytes 2097152 | tf_op jit(solution)/shard_map/all_to_all | solution.py:44
  107.2 11.6 %collective-permute-start.9 = (bf16[128,128]{1,0:T(8,128)(2,1)S(1)}, bf16[128,128]{1,0:T(8,128)(2,1)S(1)}, u32[]{:S(2)}, u32[]{:S(2)}) collective-permute-start(bf16[128,128]{1,0:T(8,128)(2,1)S(1)} %shard_map.124.rest_0_), channel_id=1, source_target_pairs={{128,96},{256,224},{384,352},{129,97},{257,225},{385,353},{130,98}... | collective-permute-start | bytes 98312 | tf_op jit(solution)/shard_map/ppermute | solution.py:39
  118.8 1.0 collective-permute-done.9.far
  119.8 6.4 %all-to-all-done.4.arrived = bf16[16,2,128,128]{3,2,1,0:T(8,128)(2,1)S(1)} async-done(((bf16[16,2,128,128]{3,2,1,0:T(8,128)(2,1)}), bf16[16,2,128,128]{3,2,1,0:T(8,128)(2,1)S(1)}, u32[]{:S(2)}, u32[]{:S(2)}) %all-to-all-start.4) | async-done | bytes 1048608 | tf_op jit(solution)/shard_map/all_to_all | solution.py:44
  126.2 1.1 shard_map.129
  127.3 10.2 %all-gather.5 = f32[256,128]{1,0:T(8,128)S(1)} all-gather(f32[128,128]{1,0:T(8,128)S(1)} %get-tuple-element.56), channel_id=7, replica_groups={{0,1},{2,3},{4,5},{6,7},{8,9},{10,11},{12,13},{14,15},{16,17},{18,19},{..., dimensions={0}, use_global_device_ids=true | all-gather | bytes 196608 | tf_op jit(solution)/shard_map/all_gather | solution.py:90
  137.5 0.6 shard_map.130
  (28 shorter events, 0.1 us)
Async XLA Ops:
  0.6 10.0 %copy-start.8 = (bf16[1,128,4096]{2,1,0:T(8,128)(2,1)S(1)}, bf16[1,128,4096]{2,1,0:T(8,128)(2,1)}, u32[]{:S(2)}) copy-start(bf16[1,128,4096]{2,1,0:T(8,128)(2,1)} %a.2) | copy-start | bytes 3145732
  0.6 0.8 copy-start.15
  2.4 8.2 %copy-start.16 = (bf16[1,128,128]{2,1,0:T(8,128)(2,1)S(1)}, bf16[1,128,128]{2,1,0:T(8,128)(2,1)}, u32[]{:S(2)}) copy-start(bf16[1,128,128]{2,1,0:T(8,128)(2,1)} %x.1) | copy-start | bytes 98308
  2.4 22.0 %all-to-all-start = ((bf16[16,128,128]{2,1,0:T(8,128)(2,1)}), bf16[16,128,128]{2,1,0:T(8,128)(2,1)S(1)}, u32[]{:S(2)}, u32[]{:S(2)}) async-start(bf16[16,128,128]{2,1,0:T(8,128)(2,1)} %shard_map.114), calls=%async_computation | async-start | bytes 1048576 | tf_op jit(solution)/shard_map/all_to_all | solution.py:44
  10.7 1.2 copy-start.9
  12.5 4.8 %collective-permute-start = (bf16[128,2048]{1,0:T(8,128)(2,1)S(1)}, bf16[128,2048]{1,0:T(8,128)(2,1)S(1)}, u32[]{:S(2)}, u32[]{:S(2)}) collective-permute-start(bf16[128,2048]{1,0:T(8,128)(2,1)S(1)} %get-tuple-element.32), channel_id=1, source_target_pairs={{0,1},{1,0},{2,3},{3,2},{4,5},{5,4},{6,7},{7,6},{8,9},{9,8},{10,11... | collective-permute-start | bytes 1572872 | tf_op jit(solution)/shard_map/ppermute | solution.py:85
  15.3 3.8 %collective-permute-start.1 = (bf16[128,2048]{1,0:T(8,128)(2,1)S(1)}, bf16[128,2048]{1,0:T(8,128)(2,1)S(1)}, u32[]{:S(2)}, u32[]{:S(2)}) collective-permute-start(bf16[128,2048]{1,0:T(8,128)(2,1)S(1)} %get-tuple-element.33), channel_id=1, source_target_pairs={{0,1},{1,0},{2,3},{3,2},{4,5},{5,4},{6,7},{7,6},{8,9},{9,8},{10,11... | collective-permute-start | bytes 1572872 | tf_op jit(solution)/shard_map/ppermute | solution.py:85
  24.9 4.4 %copy-start.12 = (bf16[1,2,128,128]{3,2,1,0:T(8,128)(2,1)S(1)}, bf16[1,2,128,128]{3,2,1,0:T(8,128)(2,1)}, u32[]{:S(2)}) copy-start(bf16[1,2,128,128]{3,2,1,0:T(8,128)(2,1)} %queries.3) | copy-start | bytes 196612
  24.9 4.3 %copy-start.13 = (bf16[1,2,128,128]{3,2,1,0:T(8,128)(2,1)S(1)}, bf16[1,2,128,128]{3,2,1,0:T(8,128)(2,1)}, u32[]{:S(2)}) copy-start(bf16[1,2,128,128]{3,2,1,0:T(8,128)(2,1)} %keys.3) | copy-start | bytes 196612
  24.9 4.3 %copy-start.14 = (bf16[1,2,128,128]{3,2,1,0:T(8,128)(2,1)S(1)}, bf16[1,2,128,128]{3,2,1,0:T(8,128)(2,1)}, u32[]{:S(2)}) copy-start(bf16[1,2,128,128]{3,2,1,0:T(8,128)(2,1)} %values.3) | copy-start | bytes 196612
  30.8 18.3 %all-to-all-start.1 = ((bf16[16,128,128]{2,1,0:T(8,128)(2,1)}), bf16[16,128,128]{2,1,0:T(8,128)(2,1)S(1)}, u32[]{:S(2)}, u32[]{:S(2)}) async-start(bf16[16,128,128]{2,1,0:T(8,128)(2,1)} %get-tuple-element.36), calls=%async_computation.1 | async-start | bytes 1048576 | tf_op jit(solution)/shard_map/all_to_all | solution.py:44
  35.0 1.2 copy-start.10
  36.2 1.2 copy-start.11
  37.6 8.9 %copy-start = (bf16[16,128,128]{2,1,0:T(8,128)(2,1)}, bf16[16,128,128]{2,1,0:T(8,128)(2,1)S(1)}, u32[]{:S(2)}) copy-start(bf16[16,128,128]{2,1,0:T(8,128)(2,1)S(1)} %get-tuple-element.39.ok) | copy-start | bytes 1572868
  37.6 6.5 %collective-permute-start.2 = (bf16[16,128,128]{2,1,0:T(8,128)(2,1)S(1)}, bf16[16,128,128]{2,1,0:T(8,128)(2,1)S(1)}, u32[]{:S(2)}, u32[]{:S(2)}) collective-permute-start(bf16[16,128,128]{2,1,0:T(8,128)(2,1)S(1)} %get-tuple-element.41), channel_id=1, source_target_pairs={{0,1},{1,0},{2,3},{3,2},{4,5},{5,4},{6,7},{7,6},{8,9},{9,8},{10,11... | collective-permute-start | bytes 1572872 | tf_op jit(solution)/shard_map/ppermute | solution.py:85
  40.1 4.0 %collective-permute-start.3 = (bf16[16,128,128]{2,1,0:T(8,128)(2,1)S(1)}, bf16[16,128,128]{2,1,0:T(8,128)(2,1)S(1)}, u32[]{:S(2)}, u32[]{:S(2)}) collective-permute-start(bf16[16,128,128]{2,1,0:T(8,128)(2,1)S(1)} %get-tuple-element.42), channel_id=1, source_target_pairs={{0,1},{1,0},{2,3},{3,2},{4,5},{5,4},{6,7},{7,6},{8,9},{9,8},{10,11... | collective-permute-start | bytes 1572872 | tf_op jit(solution)/shard_map/ppermute | solution.py:85
  46.5 0.8 copy-start.2
  47.3 0.8 copy-start.4
  48.1 0.8 copy-start.6
  53.3 14.4 %copy-start.18 = (bf16[1,128,128]{2,1,0:T(8,128)(2,1)S(1)}, bf16[1,128,128]{2,1,0:T(8,128)(2,1)}, u32[]{:S(2)}) copy-start(bf16[1,128,128]{2,1,0:T(8,128)(2,1)} %fresh.1) | copy-start | bytes 98308
  53.4 14.5 %all-to-all-start.2 = ((bf16[4,4,128,128]{3,2,1,0:T(8,128)(2,1)}), bf16[4,4,128,128]{3,2,1,0:T(8,128)(2,1)S(1)}, u32[]{:S(2)}, u32[]{:S(2)}) async-start(bf16[4,4,128,128]{3,2,1,0:T(8,128)(2,1)} %get-tuple-element.46), calls=%async_computation.2 | async-start | bytes 1048576 | tf_op jit(solution)/shard_map/all_to_all | solution.py:54
  56.8 10.9 %collective-permute-start.4 = (bf16[128,128]{1,0:T(8,128)(2,1)S(1)}, bf16[128,128]{1,0:T(8,128)(2,1)S(1)}, u32[]{:S(2)}, u32[]{:S(2)}) collective-permute-start(bf16[128,128]{1,0:T(8,128)(2,1)S(1)} %get-tuple-element.45), channel_id=1, source_target_pairs={{32,0},{64,32},{96,64},{128,96},{160,128},{192,160},{224,192},{256... | collective-permute-start | bytes 98312 | tf_op jit(solution)/shard_map/ppermute | solution.py:39
  68.8 23.2 %all-to-all-start.3 = ((bf16[16,128,128]{2,1,0:T(8,128)(2,1)}), bf16[16,128,128]{2,1,0:T(8,128)(2,1)S(1)}, u32[]{:S(2)}, u32[]{:S(2)}) async-start(bf16[16,128,128]{2,1,0:T(8,128)(2,1)} %shard_map.122.rest_0_), calls=%async_computation.3 | async-start | bytes 1048576 | tf_op jit(solution)/shard_map/all_to_all | solution.py:44
  74.7 15.9 %copy-start.17 = (f32[1,128,128]{2,1,0:T(8,128)S(1)}, f32[1,128,128]{2,1,0:T(8,128)}, u32[]{:S(2)}) copy-start(f32[1,128,128]{2,1,0:T(8,128)} %start.1) | copy-start | bytes 196612
  74.8 11.2 %collective-permute-start.5 = (bf16[128,128]{1,0:T(8,128)(2,1)S(1)}, bf16[128,128]{1,0:T(8,128)(2,1)S(1)}, u32[]{:S(2)}, u32[]{:S(2)}) collective-permute-start(bf16[128,128]{1,0:T(8,128)(2,1)S(1)} %get-tuple-element.48), channel_id=1, source_target_pairs={{0,8},{1,9},{2,10},{3,11},{4,12},{5,13},{6,14},{7,15},{8,16},{9,17... | collective-permute-start | bytes 98312 | tf_op jit(solution)/shard_map/ppermute | solution.py:67
  78.1 12.5 %collective-permute-start.6 = (bf16[128,128]{1,0:T(8,128)(2,1)S(1)}, bf16[128,128]{1,0:T(8,128)(2,1)S(1)}, u32[]{:S(2)}, u32[]{:S(2)}) collective-permute-start(bf16[128,128]{1,0:T(8,128)(2,1)S(1)} %get-tuple-element.49), channel_id=1, source_target_pairs={{0,16},{1,17},{2,18},{3,19},{4,20},{5,21},{6,22},{7,23},{8,24},{9,... | collective-permute-start | bytes 98312 | tf_op jit(solution)/shard_map/ppermute | solution.py:67
  82.1 8.5 %collective-permute-start.7 = (bf16[128,128]{1,0:T(8,128)(2,1)S(1)}, bf16[128,128]{1,0:T(8,128)(2,1)S(1)}, u32[]{:S(2)}, u32[]{:S(2)}) collective-permute-start(bf16[128,128]{1,0:T(8,128)(2,1)S(1)} %get-tuple-element.50), channel_id=1, source_target_pairs={{0,24},{1,25},{2,26},{3,27},{4,28},{5,29},{6,30},{7,31},{8,0},{9,1... | collective-permute-start | bytes 98312 | tf_op jit(solution)/shard_map/ppermute | solution.py:67
  90.7 8.6 %collective-permute-start.8 = (bf16[128,128]{1,0:T(8,128)(2,1)S(1)}, bf16[128,128]{1,0:T(8,128)(2,1)S(1)}, u32[]{:S(2)}, u32[]{:S(2)}) collective-permute-start(bf16[128,128]{1,0:T(8,128)(2,1)S(1)} %shard_map.124.rest_0_), channel_id=1, source_target_pairs={{32,0},{64,32},{96,64},{160,128},{192,160},{224,192},{288,256},{32... | collective-permute-start | bytes 98312 | tf_op jit(solution)/shard_map/ppermute | solution.py:39
  92.0 7.3 %copy-start.3 = (bf16[16,128,128]{2,1,0:T(8,128)(2,1)S(1)}, bf16[16,128,128]{2,1,0:T(8,128)(2,1)}, u32[]{:S(2)}) copy-start(bf16[16,128,128]{2,1,0:T(8,128)(2,1)} %copy-done.2) | copy-start | bytes 1572868
  92.0 7.3 %copy-start.5 = (bf16[16,128,128]{2,1,0:T(8,128)(2,1)S(1)}, bf16[16,128,128]{2,1,0:T(8,128)(2,1)}, u32[]{:S(2)}) copy-start(bf16[16,128,128]{2,1,0:T(8,128)(2,1)} %copy-done.4) | copy-start | bytes 1572868
  92.0 7.3 %copy-start.7 = (bf16[16,128,128]{2,1,0:T(8,128)(2,1)S(1)}, bf16[16,128,128]{2,1,0:T(8,128)(2,1)}, u32[]{:S(2)}) copy-start(bf16[16,128,128]{2,1,0:T(8,128)(2,1)} %copy-done.6) | copy-start | bytes 1572868
  92.5 6.8 %copy-start.1 = (bf16[16,128,128]{2,1,0:T(8,128)(2,1)S(1)}, bf16[16,128,128]{2,1,0:T(8,128)(2,1)}, u32[]{:S(2)}) copy-start(bf16[16,128,128]{2,1,0:T(8,128)(2,1)} %copy-done) | copy-start | bytes 1572868
  101.8 24.4 %all-to-all-start.4 = ((bf16[16,2,128,128]{3,2,1,0:T(8,128)(2,1)}), bf16[16,2,128,128]{3,2,1,0:T(8,128)(2,1)S(1)}, u32[]{:S(2)}, u32[]{:S(2)}) async-start(bf16[16,2,128,128]{3,2,1,0:T(8,128)(2,1)} %shard_map.128), calls=%async_computation.4 | async-start | bytes 2097152 | tf_op jit(solution)/shard_map/all_to_all | solution.py:44
  107.2 12.7 %collective-permute-start.9 = (bf16[128,128]{1,0:T(8,128)(2,1)S(1)}, bf16[128,128]{1,0:T(8,128)(2,1)S(1)}, u32[]{:S(2)}, u32[]{:S(2)}) collective-permute-start(bf16[128,128]{1,0:T(8,128)(2,1)S(1)} %shard_map.124.rest_0_), channel_id=1, source_target_pairs={{128,96},{256,224},{384,352},{129,97},{257,225},{385,353},{130,98}... | collective-permute-start | bytes 98312 | tf_op jit(solution)/shard_map/ppermute | solution.py:39
